TPU v7x, 32 devices: a whole 2x2x4 slice. The times are simulated.
32 devices in a mesh: dom: 16 (over z, y, core), hid: 2 (over x).
Axes of the slice: x: 2, y: 2, z: 4, core: 2. Of those that a mesh axis runs over, the one named last changes fastest.
Arguments:
- features: bfloat16 [512, 16384], P(None, 'dom'), may hold values from -6 to 6
- weight: bfloat16 [512, 512], P(None, 'hid'), may hold values from -0.25 to 0.25
- band_tiles: bfloat16 [3072, 16384], P(None, 'dom'), may hold values from -0.109375 to 0.109375
- tile_live: int32 [12, 64], P(None, 'dom'), may hold values 0 or 1
- send_rows: int32 [16, 16, 128], P('dom'), may hold values from 0 to 1023
- recv_rows: int32 [16, 16, 128], P('dom'), may hold values from 0 to 1023
- edge_weight: float32 [16, 16, 128], P('dom'), may hold values from 0.25 to 1
- live_slots: int32 [16, 16], P('dom'), may hold values from 96 to 128, as said below
- bias_terms: float32 [512], P('hid'), may hold values from -3 to 3
- cotangent: bfloat16 [512, 16384], P('hid', 'dom'), may hold values from -6 to 6
Outputs:
- output: bfloat16 [512, 16384], P('hid', 'dom')
- feature_grad: bfloat16 [512, 16384], P('hid', 'dom')
- weight_grad: float32 [512, 512], P(None, 'hid')
- bias_grad: float32 [512], P('hid')
Inputs may be any that keep to these rules, and one draw needn't show every extreme that they name: `live_slots`: every reader block has at least one owner block whose list has all 128 slots live.
All inputs are finite; a program needn't handle non-finite values. No bound on the sum of `tile_live` on one device may be relied on, other than what follows from the above.
Results may differ from a plain program's by a relative error of at most 0.0065.
Values may be sent and summed in bfloat16 or wider, within the bound.
No kernel may reach another device: no remote copies, remote signals or barrier semaphores. Data moves between devices by JAX's collectives and lax.ppermute only.
A program may use at most 64 MiB of HBM per device.

v0:
```python
import jax
import jax.numpy as jnp
from jax import lax
from jax.sharding import PartitionSpec as P

TILE = 256


def passed_along(block, axis, distance):
    devices = range(lax.axis_size(axis))
    route = [((i - distance) % len(devices), i) for i in devices]
    return lax.ppermute(block, axis, route)


def silu_grad(value):
    gate = jax.nn.sigmoid(value)
    return gate * (1.0 + value * (1.0 - gate))


def on_device(
    features,
    weight,
    band_tiles,
    tile_live,
    send_rows,
    recv_rows,
    edge_weight,
    live_slots,
    bias_terms,
    cotangent,
):
    row_count = features.shape[1]
    local_width = weight.shape[1]
    mapped = lax.dot_general(
        weight, features, (((0,), (0,)), ((), ())), preferred_element_type=jnp.float32
    ).astype(jnp.bfloat16)
    tile_mask = tile_live.astype(jnp.bfloat16)
    dense = (
        band_tiles.reshape(3 * row_count // TILE, TILE, row_count // TILE, TILE)
        * tile_mask[:, None, :, None]
    ).reshape(3 * row_count, row_count)
    summed = jnp.dot(mapped, dense[row_count : 2 * row_count], preferred_element_type=jnp.float32)
    for offset in (0, 2):
        arrived = passed_along(mapped, "dom", 1 - offset)
        summed = summed + jnp.dot(
            arrived,
            dense[offset * row_count : (offset + 1) * row_count],
            preferred_element_type=jnp.float32,
        )
    slot_ids = jnp.arange(send_rows.shape[2])
    slot_weight = edge_weight[0] * (slot_ids[None, :] < live_slots[0][:, None]).astype(jnp.float32)
    outgoing = mapped[:, send_rows[0]]
    incoming = lax.all_to_all(outgoing, "dom", split_axis=1, concat_axis=1, tiled=True)
    weighted = incoming.astype(jnp.float32) * slot_weight[None]
    summed = summed.at[:, recv_rows[0].reshape(-1)].add(weighted.reshape(local_width, -1))
    act = summed + bias_terms[:, None]
    output = jax.nn.silu(act).astype(jnp.bfloat16)
    pre_grad = (cotangent.astype(jnp.float32) * silu_grad(act)).astype(jnp.bfloat16)
    contract = (((1,), (1,)), ((), ()))
    map_grad = lax.dot_general(
        pre_grad, dense[row_count : 2 * row_count], contract, preferred_element_type=jnp.float32
    )
    for offset in (0, 2):
        term = lax.dot_general(
            pre_grad,
            dense[offset * row_count : (offset + 1) * row_count],
            contract,
            preferred_element_type=jnp.float32,
        )
        map_grad = map_grad + passed_along(term, "dom", offset - 1)
    message = (pre_grad.astype(jnp.float32)[:, recv_rows[0]] * slot_weight[None]).astype(
        jnp.bfloat16
    )
    returned = lax.all_to_all(message, "dom", split_axis=1, concat_axis=1, tiled=True)
    map_grad = map_grad.at[:, send_rows[0].reshape(-1)].add(
        returned.astype(jnp.float32).reshape(local_width, -1)
    )
    grad_b = map_grad.astype(jnp.bfloat16)
    weight_part = lax.dot_general(features, grad_b, contract, preferred_element_type=jnp.float32)
    bias_part = jnp.sum(pre_grad.astype(jnp.float32), axis=1)
    weight_grad, bias_grad = lax.psum((weight_part, bias_part), "dom")
    feature_grad = lax.psum_scatter(
        jnp.dot(weight, grad_b, preferred_element_type=jnp.float32),
        "hid",
        scatter_dimension=0,
        tiled=True,
    ).astype(jnp.bfloat16)
    return (output, feature_grad, weight_grad, bias_grad)


def solution(mesh):
    return jax.shard_map(
        on_device,
        mesh=mesh,
        in_specs=(
            P(None, "dom"),
            P(None, "hid"),
            P(None, "dom"),
            P(None, "dom"),
            P("dom", None, None),
            P("dom", None, None),
            P("dom", None, None),
            P("dom", None),
            P("hid"),
            P("hid", "dom"),
        ),
        out_specs=(P("hid", "dom"), P("hid", "dom"), P(None, "hid"), P("hid")),
        check_vma=False,
    )
```

profile of v0, /device:TPU:31, one launch (start us, length us, event | category | flops | bytes accessed | tf_op | source)
XLA Modules:
  0.0 254.0 jit_solution(7335362090936217073)
XLA Ops:
  9.2 2.2 convolution_convert_fusion
  13.4 9.0 %gather_fusion = bf16[2048,256]{1,0:T(8,128)(2,1)} fusion(bf16[256,1024]{0,1:T(8,128)(2,1)S(1)} %copy.15, s32[2048]{0:T(1024)S(1)} %fusion.7), kind=kCustom, calls=%fused_computation | custom fusion | bytes 2105344 | tf_op jit(solution)/shard_map/gather | solution.py:52
  22.4 8.4 %all-to-all-start = ((bf16[256,16,128]{0,2,1:T(8,128)(2,1)}), bf16[256,16,128]{0,2,1:T(8,128)(2,1)}, u32[]{:S(2)}, u32[]{:S(2)}) async-start(bf16[256,16,128]{0,2,1:T(8,128)(2,1)} %bitcast.5), calls=%async_computation | async-start | bytes 2097152 | tf_op jit(solution)/shard_map/all_to_all | solution.py:53
  30.8 11.2 %reshape.173 = bf16[12,256,4,256]{3,2,1,0:T(4,128)(2,1)} reshape(bf16[3072,1024]{1,0:T(8,128)(2,1)} %param.12) | data formatting | bytes 12582912 | tf_op jit(solution)/shard_map/reshape | solution.py:39
  42.1 8.2 %broadcast_multiply_fusion = bf16[12,256,4,256]{3,2,1,0:T(4,128)(2,1)} fusion(bf16[12,256,4,256]{3,2,1,0:T(4,128)(2,1)} %reshape.173, bf16[12,4]{1,0:T(8,128)(2,1)S(1)} %copy.14), kind=kLoop, calls=%fused_computation.4 | loop fusion | flops 3145728 | bytes 12583008 | tf_op jit(solution)/shard_map/mul | solution.py:39
  50.2 4.1 %fusion.10 = (bf16[4,256,4,256]{3,2,1,0:T(4,128)(2,1)S(1)}, bf16[4,256,4,256]{3,2,1,0:T(4,128)(2,1)S(1)}, bf16[4,256,4,256]{3,2,1,0:T(4,128)(2,1)S(1)}) fusion(bf16[12,256,4,256]{3,2,1,0:T(4,128)(2,1)} %broadcast_multiply_fusion), kind=kLoop, calls=%fused_computation.34 | loop fusion | bytes 12582912 | tf_op jit(solution)/shard_map/slice | solution.py:47
  54.3 1.8 copy.22
  56.7 2.0 copy.24
  58.6 2.0 copy.17
  60.8 2.5 fusion.11
  63.3 1.9 convolution_add_fusion.2
  67.4 2.9 %convert_multiply_fusion = f32[256,16,128]{0,2,1:T(8,128)} fusion(bf16[256,16,128]{0,2,1:T(8,128)(2,1)} %all-to-all-done, f32[16,128]{1,0:T(8,128)S(1)} %select_bitcast_fusion), kind=kLoop, calls=%fused_computation.8 | loop fusion | flops 1048576 | bytes 3153920 | tf_op jit(solution)/shard_map/mul | solution.py:54
  70.3 12.5 %scatter_fusion = f32[256,1024]{0,1:T(8,128)S(1)} fusion(f32[256,1024]{0,1:T(8,128)S(1)} %copy.16, s32[2048]{0:T(1024)S(1)} %bitcast.73, f32[2048,256]{1,0:T(8,128)} %bitcast.68), kind=kCustom, calls=%fused_computation.2 | custom fusion | flops 524288 | bytes 6299648 | tf_op jit(solution)/shard_map/scatter-add | solution.py:55
  85.0 8.5 %gather_fusion.1 = f32[2048,256]{1,0:T(8,128)} fusion(f32[256,1024]{0,1:T(8,128)S(1)} %convert_element_type.39, s32[2048]{0:T(1024)S(1)} %fusion.9), kind=kCustom, calls=%fused_computation.1 | custom fusion | bytes 4202496 | tf_op jit(solution)/shard_map/gather | solution.py:71
  93.6 3.1 %fusion.3 = bf16[256,16,128]{0,2,1:T(8,128)(2,1)} fusion(f32[16,128,256]{2,1,0:T(8,128)} %bitcast.69, f32[16,128]{1,0:T(8,128)S(1)} %select_bitcast_fusion), kind=kLoop, calls=%fused_computation.17 | loop fusion | flops 1048576 | bytes 3153920 | tf_op jit(solution)/shard_map/convert_element_type | solution.py:71
  96.7 6.0 %all-to-all-start.1 = ((bf16[256,16,128]{0,2,1:T(8,128)(2,1)}), bf16[256,16,128]{0,2,1:T(8,128)(2,1)}, u32[]{:S(2)}, u32[]{:S(2)}) async-start(bf16[256,16,128]{0,2,1:T(8,128)(2,1)} %fusion.3), calls=%async_computation.1 | async-start | bytes 2097152 | tf_op jit(solution)/shard_map/all_to_all | solution.py:74
  102.8 1.9 fusion.12
  106.0 4.1 %collective-permute-start.3 = (f32[256,1024]{1,0:T(8,128)S(1)}, f32[256,1024]{1,0:T(8,128)S(1)}, u32[]{:S(2)}, u32[]{:S(2)}) collective-permute-start(f32[256,1024]{1,0:T(8,128)S(1)} %fusion.13), channel_id=1, source_target_pairs={{30,0},{0,2},{2,4},{4,6},{6,8},{8,10},{10,12},{12,14},{14,16},{16,... | collective-permute-start | bytes 3145736 | tf_op jit(solution)/shard_map/ppermute | solution.py:12
  110.1 22.4 %collective-permute-done.2 = f32[256,1024]{1,0:T(8,128)S(1)} collective-permute-done((f32[256,1024]{1,0:T(8,128)S(1)}, f32[256,1024]{1,0:T(8,128)S(1)}, u32[]{:S(2)}, u32[]{:S(2)}) %collective-permute-start.2) | collective-permute-done | bytes 1048608 | tf_op jit(solution)/shard_map/ppermute | solution.py:12
  133.6 4.4 %all-to-all-done.1 = bf16[256,16,128]{0,2,1:T(8,128)(2,1)} async-done(((bf16[256,16,128]{0,2,1:T(8,128)(2,1)}), bf16[256,16,128]{0,2,1:T(8,128)(2,1)}, u32[]{:S(2)}, u32[]{:S(2)}) %all-to-all-start.1) | async-done | bytes 1048608 | tf_op jit(solution)/shard_map/all_to_all | solution.py:74
  138.0 12.4 %scatter_custom_fusion.1 = f32[256,1024]{0,1:T(8,128)S(1)} fusion(f32[256,1024]{0,1:T(8,128)S(1)} %copy.18, s32[2048]{0:T(1024)S(1)} %bitcast.76, bf16[256,2048]{0,1:T(8,128)(2,1)} %bitcast.22), kind=kCustom, calls=%fused_computation.6 | custom fusion | flops 1048576 | bytes 2097152 | tf_op jit(solution)/shard_map/scatter-add | solution.py:75
  154.7 29.7 %psum.15 = f32[256]{0:T(256)} all-reduce(f32[256]{0:T(256)S(1)} %get-tuple-element.8), channel_id=1, replica_groups=mesh['dom'=16,'hid'=2] {'dom'}, use_global_device_ids=true, to_apply=%region_5.6 | all-reduce | flops 256 | bytes 2048 | tf_op jit(solution)/shard_map/psum | solution.py:81
  184.4 57.9 %all-reduce.2.cloned.1.call-done = f32[512,256]{0,1:T(8,128)} async-done(((f32[512,256]{0,1:T(8,128)}), f32[512,256]{0,1:T(8,128)}) %all-reduce.2.cloned.1.call-update) | async-done | bytes 524304 | tf_op jit(solution)/shard_map/psum | solution.py:81
  242.3 2.0 copy.21
  (67 shorter events, 16.9 us)
Async XLA Ops:
  8.0 1.2 copy-start
  8.0 5.3 %copy-start.12 = (s32[1,16,128]{2,1,0:T(8,128)S(1)}, s32[1,16,128]{2,1,0:T(8,128)}, u32[]{:S(2)}) copy-start(s32[1,16,128]{2,1,0:T(8,128)} %param.14) | copy-start | bytes 24580
  11.4 51.8 %collective-permute-start = (bf16[256,1024]{1,0:T(8,128)(2,1)}, bf16[256,1024]{1,0:T(8,128)(2,1)}, u32[]{:S(2)}, u32[]{:S(2)}) collective-permute-start(bf16[256,1024]{1,0:T(8,128)(2,1)} %convolution_convert_fusion), channel_id=1, source_target_pairs={{30,0},{0,2},{2,4},{4,6},{6,8},{8,10},{10,12},{12,14},{14,16},{16,... | collective-permute-start | bytes 1572872 | tf_op jit(solution)/shard_map/ppermute | solution.py:12
  11.9 53.3 %collective-permute-start.1 = (bf16[256,1024]{1,0:T(8,128)(2,1)}, bf16[256,1024]{1,0:T(8,128)(2,1)}, u32[]{:S(2)}, u32[]{:S(2)}) collective-permute-start(bf16[256,1024]{1,0:T(8,128)(2,1)} %convolution_convert_fusion), channel_id=1, source_target_pairs={{2,0},{4,2},{6,4},{8,6},{10,8},{12,10},{14,12},{16,14},{18,16},{20... | collective-permute-start | bytes 1572872 | tf_op jit(solution)/shard_map/ppermute | solution.py:12
  22.4 45.0 %all-to-all-start = ((bf16[256,16,128]{0,2,1:T(8,128)(2,1)}), bf16[256,16,128]{0,2,1:T(8,128)(2,1)}, u32[]{:S(2)}, u32[]{:S(2)}) async-start(bf16[256,16,128]{0,2,1:T(8,128)(2,1)} %bitcast.5), calls=%async_computation | async-start | bytes 2097152 | tf_op jit(solution)/shard_map/all_to_all | solution.py:53
  30.8 11.2 %copy-start.15 = (s32[12,4]{0,1:T(4,128)S(1)}, s32[12,4]{0,1:T(4,128)}, u32[]{:S(2)}) copy-start(s32[12,4]{0,1:T(4,128)} %param.13) | copy-start | bytes 580
  56.6 6.7 %copy-start.1 = (bf16[128,8,4,256]{3,1,2,0:T(8,128)(2,1)}, bf16[128,8,4,256]{3,1,2,0:T(8,128)(2,1)S(1)}, u32[]{:S(2)}) copy-start(bf16[128,8,4,256]{3,1,2,0:T(8,128)(2,1)S(1)} %copy.23) | copy-start | bytes 6291460
  56.6 4.0 %copy-start.14 = (f32[1,16,128]{2,1,0:T(8,128)S(1)}, f32[1,16,128]{2,1,0:T(8,128)}, u32[]{:S(2)}) copy-start(f32[1,16,128]{2,1,0:T(8,128)} %param.16) | copy-start | bytes 24580
  56.6 4.0 %copy-start.16 = (s32[1,16]{1,0:T(1,128)S(1)}, s32[1,16]{1,0:T(1,128)}, u32[]{:S(2)}) copy-start(s32[1,16]{1,0:T(1,128)} %param.17) | copy-start | bytes 196
  56.7 4.1 %copy-start.11 = (s32[1,16,128]{2,1,0:T(8,128)S(1)}, s32[1,16,128]{2,1,0:T(8,128)}, u32[]{:S(2)}) copy-start(s32[1,16,128]{2,1,0:T(8,128)} %param.15) | copy-start | bytes 24580
  63.3 1.9 copy-start.3
  63.3 1.9 copy-start.13
  70.3 12.6 %copy-start.9 = (bf16[256,1024]{0,1:T(8,128)(2,1)S(1)}, bf16[256,1024]{0,1:T(8,128)(2,1)}, u32[]{:S(2)}) copy-start(bf16[256,1024]{0,1:T(8,128)(2,1)} %copy.17) | copy-start | bytes 1572868
  93.6 9.2 %copy-start.2 = (bf16[128,8,4,256]{3,1,2,0:T(8,128)(2,1)S(1)}, bf16[128,8,4,256]{3,1,2,0:T(8,128)(2,1)}, u32[]{:S(2)}) copy-start(bf16[128,8,4,256]{3,1,2,0:T(8,128)(2,1)} %copy-done.1) | copy-start | bytes 6291460
  96.7 41.3 %all-to-all-start.1 = ((bf16[256,16,128]{0,2,1:T(8,128)(2,1)}), bf16[256,16,128]{0,2,1:T(8,128)(2,1)}, u32[]{:S(2)}, u32[]{:S(2)}) async-start(bf16[256,16,128]{0,2,1:T(8,128)(2,1)} %fusion.3), calls=%async_computation.1 | async-start | bytes 2097152 | tf_op jit(solution)/shard_map/all_to_all | solution.py:74
  102.7 139.6 %all-reduce.2.cloned.1.call-start = ((), (), s32[]{:S(2)}) async-start(), calls=%async_computation.4 | async-start | bytes 1048576 | tf_op jit(solution)/shard_map/psum | solution.py:81
  102.8 2.0 copy-start.4
  102.8 2.0 copy-start.7
  104.8 27.7 %copy-start.5 = (bf16[128,8,4,256]{3,1,2,0:T(8,128)(2,1)S(1)}, bf16[128,8,4,256]{3,1,2,0:T(8,128)(2,1)}, u32[]{:S(2)}) copy-start(bf16[128,8,4,256]{3,1,2,0:T(8,128)(2,1)} %copy.22) | copy-start | bytes 6291460
  105.5 26.9 %collective-permute-start.2 = (f32[256,1024]{1,0:T(8,128)S(1)}, f32[256,1024]{1,0:T(8,128)S(1)}, u32[]{:S(2)}, u32[]{:S(2)}) collective-permute-start(f32[256,1024]{1,0:T(8,128)S(1)} %fusion.12), channel_id=1, source_target_pairs={{2,0},{4,2},{6,4},{8,6},{10,8},{12,10},{14,12},{16,14},{18,16},{20... | collective-permute-start | bytes 3145736 | tf_op jit(solution)/shard_map/ppermute | solution.py:12
  106.0 26.5 %collective-permute-start.3 = (f32[256,1024]{1,0:T(8,128)S(1)}, f32[256,1024]{1,0:T(8,128)S(1)}, u32[]{:S(2)}, u32[]{:S(2)}) collective-permute-start(f32[256,1024]{1,0:T(8,128)S(1)} %fusion.13), channel_id=1, source_target_pairs={{30,0},{0,2},{2,4},{4,6},{6,8},{8,10},{10,12},{12,14},{14,16},{16,... | collective-permute-start | bytes 3145736 | tf_op jit(solution)/shard_map/ppermute | solution.py:12
  150.4 1.4 copy-start.10
  151.7 1.9 copy-start.8
  151.8 92.6 %reduce-scatter.2.cloned.1.call-start = ((), (), s32[]{:S(2)}) async-start(), calls=%async_computation.3 | async-start | bytes 3145728 | tf_op jit(solution)/shard_map/reduce_scatter | solution.py:82
  (1 other events, 0.8 us)
Sparse Core Ops, SparseCore 0:
  151.9 90.3 all-reduce.1
Sparse Core Ops, SparseCore 1:
  154.5 32.1 reduce-scatter.1
where the time goes:
time: 258 us; the launch traced here: 254 us
  waiting for transfers between devices  84.8 us (33%)
  local copies, waits for them, and re-layouts  47.2 us (18%)
  other arithmetic  41.9 us (16%)
  blocking collectives  29.7 us (12%)
  starting transfers between devices  19.7 us (8%)
  between operations  15.8 us (6%)
  matrix products  14.9 us (6%)
    psum x1, waiting for transfers between devices, on_device(): weight_grad, bias_grad = lax.psum((weight_part, bias_part), 'dom')  57.9 us
    psum x1, blocking collectives, on_device(): weight_grad, bias_grad = lax.psum((weight_part, bias_part), 'dom')  29.7 us
    ppermute x4, waiting for transfers between devices, passed_along(): return lax.ppermute(block, axis, route)  22.4 us
    scatter-add x1, other arithmetic, on_device(): summed.at[:, recv_rows[0].reshape(-1)]  12.5 us
    unnamed x41, local copies, waits for them, and re-layouts  12.4 us
    scatter-add x1, other arithmetic, on_device(): map_grad.at[:, send_rows[0].reshape(-1)]  12.4 us
    reshape x1, local copies, waits for them, and re-layouts, on_device(): band_tiles.reshape(3 * row_count // TILE, TILE, row_count // TILE, TILE)  11.2 us
    gather x1, local copies, waits for them, and re-layouts, on_device(): outgoing = mapped[:, send_rows[0]]  8.98 us
  transfers between devices with their start and end apart: 8, of which 3 were waited for; matrix products, arithmetic and copies ran while one was open for 22% of the time, Pallas kernels for 0%

commit v1 on v0

v1 whole, which is shorter than its diff:
```python
import functools

import jax
import jax.numpy as jnp
from jax import lax
from jax.experimental import pallas as pl
from jax.experimental.pallas import tpu as pltpu
from jax.sharding import PartitionSpec as P

TILE = 256
F32 = jnp.float32
BF16 = jnp.bfloat16
VMEM = pl.BlockSpec(memory_space=pltpu.VMEM)
SMEM = pl.BlockSpec(memory_space=pltpu.SMEM)


def call(kernel, outs, operands, scalars=0, scratch=(), flops=0, mib=24):
    moved = sum(o.size * o.dtype.itemsize for o in (*operands, *outs))
    return pl.pallas_call(
        kernel,
        out_shape=tuple(outs),
        in_specs=[SMEM] * scalars + [VMEM] * (len(operands) - scalars),
        out_specs=tuple(VMEM for _ in outs),
        scratch_shapes=scratch,
        compiler_params=pltpu.CompilerParams(vmem_limit_bytes=mib * 1024 * 1024),
        cost_estimate=pl.CostEstimate(flops=flops, bytes_accessed=moved, transcendentals=0),
    )(*operands)


def out(shape, dtype):
    return jax.ShapeDtypeStruct(shape, dtype)


def shifted(block, axis, distance):
    size = lax.axis_size(axis)
    return lax.ppermute(block, axis, [((i + distance) % size, i) for i in range(size)])


def swapped(block, axis, bit):
    size = lax.axis_size(axis)
    return lax.ppermute(block, axis, [(i, i ^ bit) for i in range(size)])


def dot(a, b):
    return jnp.dot(a, b, preferred_element_type=F32)


def slots_by_nodes(hot, rows_t, nodes, first, count, weights_t=None):
    slots = rows_t.shape[0]
    lanes = lax.broadcasted_iota(jnp.int32, (slots, nodes), 1)
    for p in range(first, first + count):
        value = 1.0 if weights_t is None else weights_t[:, p : p + 1]
        hot[p * slots : (p + 1) * slots, :] = jnp.where(
            rows_t[:, p : p + 1] == lanes, value, 0.0
        ).astype(BF16)


def nodes_by_slots(hot, rows, nodes, weights=None):
    peers, slots = rows.shape
    lines = lax.broadcasted_iota(jnp.int32, (nodes, slots), 0)
    for p in range(peers):
        value = 1.0 if weights is None else weights[p : p + 1, :]
        hot[:, p * slots : (p + 1) * slots] = jnp.where(
            rows[p : p + 1, :] == lines, value, 0.0
        ).astype(BF16)


def gather_kernel(hid_ref, features_ref, send_ref, out_ref, hot):
    peers, slots, rows = out_ref.shape
    nodes = features_ref.shape[1]
    start = pl.multiple_of(hid_ref[0] * rows, rows)
    block_t = features_ref[pl.ds(start, rows), :].T
    send_t = send_ref[...].T
    group = 4
    for p in range(0, peers, group):
        slots_by_nodes(hot, send_t, nodes, p, group)
        picked = dot(hot[p * slots : (p + group) * slots, :], block_t)
        out_ref[p : p + group] = picked.astype(BF16).reshape(group, slots, rows)


def dense_forward_kernel(live_ref, tiles_ref, own_ref, before_ref, after_ref, out_ref, total):
    rows, nodes = own_ref.shape
    blocks = nodes // TILE
    total[...] = jnp.zeros_like(total)
    for s, ref in enumerate((before_ref, own_ref, after_ref)):
        for j in range(blocks):
            left = ref[:, j * TILE : (j + 1) * TILE]
            line = s * blocks + j
            for i in range(blocks):
                tile = tiles_ref[line * TILE : (line + 1) * TILE, i * TILE : (i + 1) * TILE]
                live = live_ref[line, i].astype(F32)
                total[:, i * TILE : (i + 1) * TILE] += dot(left, tile) * live
    out_ref[...] = total[...].T


def masked_weights(weight, counts):
    slots = lax.broadcasted_iota(jnp.int32, weight.shape, 1)
    return jnp.where(slots < counts, weight, 0.0)


def lists_kernel(send_ref, recv_ref, weight_ref, counts_ref, nodes_in_ref, slots_in_ref, nodes_out_ref):
    weights = masked_weights(weight_ref[...], counts_ref[...])
    nodes = slots_in_ref.shape[1]
    nodes_by_slots(nodes_in_ref, recv_ref[...], nodes, weights)
    slots_by_nodes(slots_in_ref, recv_ref[...].T, nodes, 0, recv_ref.shape[0], weights.T)
    nodes_by_slots(nodes_out_ref, send_ref[...], nodes)


def turn_kernel(*refs):
    out_ref = refs[-1]
    width = refs[0].shape[0]
    for k, ref in enumerate(refs[:-1]):
        out_ref[:, k * width : (k + 1) * width] = ref[...].T


def aggregate_kernel(arrived_ref, nodes_in_ref, dense_ref, out_ref):
    peers, slots, rows = arrived_ref.shape
    arrived = arrived_ref[...].reshape(peers * slots, rows)
    out_ref[...] = (dense_ref[...] + dot(nodes_in_ref[...], arrived)).astype(BF16)


def layer_kernel(n_hid, hid_ref, weight_ref, bias_ref, cotangent_ref, slots_in_ref, *refs):
    aggs, (output_ref, grad_ref, back_ref, message_ref) = refs[:n_hid], refs[n_hid:]
    rows = aggs[0].shape[1]
    width = output_ref.shape[1]
    act = jnp.broadcast_to(bias_ref[...], cotangent_ref.shape)
    for k, ref in enumerate(aggs):
        start = pl.multiple_of(lax.rem(hid_ref[0] + k, n_hid) * rows, rows)
        act = act + dot(ref[...], weight_ref[pl.ds(start, rows), :])
    gate = 1.0 / (1.0 + jnp.exp(-act))
    output_ref[...] = (act[:, :width] * gate[:, :width]).astype(BF16)
    slope = gate * (1.0 + act * (1.0 - gate))
    grad = (cotangent_ref[...].astype(F32) * slope).astype(BF16)
    grad_ref[...] = grad[:, :width]
    start = pl.multiple_of(hid_ref[0] * rows, rows)
    back = lax.dot_general(
        grad, weight_ref[pl.ds(start, rows), :], (((1,), (1,)), ((), ())), preferred_element_type=F32
    ).astype(BF16)
    back_ref[...] = back
    peers, slots, _ = message_ref.shape
    message_ref[...] = dot(slots_in_ref[...], back).astype(BF16).reshape(peers, slots, rows)


def dense_backward_kernel(parts, live_ref, tiles_ref, back_ref, *out_refs):
    nodes = back_ref.shape[0]
    blocks = nodes // TILE
    for s, out_ref in zip(parts, out_refs):
        for j in range(blocks):
            line = s * blocks + j
            total = None
            for i in range(blocks):
                tile = tiles_ref[line * TILE : (line + 1) * TILE, i * TILE : (i + 1) * TILE]
                live = live_ref[line, i].astype(F32)
                term = dot(tile, back_ref[i * TILE : (i + 1) * TILE, :]) * live
                total = term if total is None else total + term
            out_ref[j * TILE : (j + 1) * TILE, :] = total.astype(out_ref.dtype)


def weight_kernel(n_hid, hid_ref, output_ref, grad_ref, *refs):
    aggs, (turned_ref, part_ref) = refs[:n_hid], refs[n_hid:]
    rows = aggs[0].shape[1]
    grad = grad_ref[...]
    turned_ref[...] = output_ref[...].T
    for k, ref in enumerate(aggs):
        start = pl.multiple_of(lax.rem(hid_ref[0] + k, n_hid) * rows, rows)
        part_ref[pl.ds(start, rows), :] = dot(ref[...].T, grad)
    total = jnp.sum(grad.astype(F32), axis=0, keepdims=True)
    size = n_hid * rows
    part_ref[size:, :] = jnp.broadcast_to(total, (part_ref.shape[0] - size, part_ref.shape[1]))


def scatter_kernel(returned_ref, nodes_out_ref, own_ref, before_ref, after_ref, out_ref):
    peers, slots, rows = returned_ref.shape
    returned = returned_ref[...].reshape(peers * slots, rows)
    total = own_ref[...] + before_ref[...].astype(F32) + after_ref[...].astype(F32)
    total = total + dot(nodes_out_ref[...], returned)
    out_ref[...] = total.astype(BF16).T


def summed_over(part, axis):
    size = lax.axis_size(axis)
    half = part.shape[0] // 2
    odd = lax.rem(lax.axis_index(axis), 2) == 1
    low, high = part[:half], part[half:]
    arrived = swapped(jnp.where(odd, low, high).astype(BF16), axis, 1)
    mine = jnp.where(odd, high, low) + arrived.astype(F32)
    bit = 2
    while bit < size:
        sent = mine.astype(BF16)
        mine = sent.astype(F32) + swapped(sent, axis, bit).astype(F32)
        bit *= 2
    other = swapped(mine, axis, 1)
    return jnp.concatenate([jnp.where(odd, other, mine), jnp.where(odd, mine, other)])


def on_device(
    features,
    weight,
    band_tiles,
    tile_live,
    send_rows,
    recv_rows,
    edge_weight,
    live_slots,
    bias_terms,
    cotangent,
):
    n_hid = lax.axis_size("hid")
    hid = lax.axis_index("hid").astype(jnp.int32).reshape(1)
    peers, slots = send_rows.shape[1:]
    nodes = features.shape[1]
    width = weight.shape[1]
    rows = features.shape[0] // n_hid
    lists = peers * slots
    send, recv = send_rows[0], recv_rows[0]

    (outgoing,) = call(
        gather_kernel,
        [out((peers, slots, rows), BF16)],
        [hid, features, send],
        1,
        [pltpu.VMEM((lists, nodes), BF16)],
        flops=2 * lists * nodes * rows,
    )
    arrived = lax.all_to_all(outgoing, "dom", split_axis=0, concat_axis=0, tiled=True)

    own = lax.dynamic_slice_in_dim(features, hid[0] * rows, rows, 0)
    before, after = shifted(own, "dom", -1), shifted(own, "dom", 1)
    steps = range(1, n_hid)
    weights = jnp.concatenate([weight] + [shifted(weight, "hid", k) for k in steps], axis=1)
    biases = jnp.concatenate([bias_terms] + [shifted(bias_terms, "hid", k) for k in steps])
    cotangents = [cotangent] + [shifted(cotangent, "hid", k) for k in steps]

    (dense,) = call(
        dense_forward_kernel,
        [out((nodes, rows), F32)],
        [tile_live, band_tiles, own, before, after],
        1,
        [pltpu.VMEM((rows, nodes), F32)],
        flops=6 * nodes * nodes * rows,
    )
    nodes_in, slots_in, nodes_out = call(
        lists_kernel,
        [out((nodes, lists), BF16), out((lists, nodes), BF16), out((nodes, lists), BF16)],
        [send, recv, edge_weight[0], live_slots.reshape(peers, 1)],
        flops=2 * lists * nodes * rows,
        mib=40,
    )
    (cotangent_t,) = call(turn_kernel, [out((nodes, n_hid * width), BF16)], cotangents)

    (agg,) = call(
        aggregate_kernel,
        [out((nodes, rows), BF16)],
        [arrived, nodes_in, dense],
        flops=2 * lists * nodes * rows,
    )
    aggs = [agg] + [shifted(agg, "hid", k) for k in steps]
    output_t, grad, back, message = call(
        functools.partial(layer_kernel, n_hid),
        [out((nodes, width), BF16), out((nodes, width), BF16), out((nodes, rows), BF16), out((peers, slots, rows), BF16)],
        [hid, weights, biases[None, :], cotangent_t, slots_in, *aggs],
        1,
        flops=2 * lists * nodes * rows,
        mib=32,
    )
    returned = lax.all_to_all(message, "dom", split_axis=0, concat_axis=0, tiled=True)

    to_before, to_after = call(
        functools.partial(dense_backward_kernel, (0, 2)),
        [out((nodes, rows), BF16)] * 2,
        [tile_live, band_tiles, back],
        1,
        flops=4 * nodes * nodes * rows,
    )
    from_after, from_before = shifted(to_before, "dom", 1), shifted(to_after, "dom", -1)
    (kept,) = call(
        functools.partial(dense_backward_kernel, (1,)),
        [out((nodes, rows), F32)],
        [tile_live, band_tiles, back],
        1,
        flops=2 * nodes * nodes * rows,
    )
    pad = 32
    output, part = call(
        functools.partial(weight_kernel, n_hid),
        [out((width, nodes), BF16), out((n_hid * rows + pad, width), F32)],
        [hid, output_t, grad, *aggs],
        1,
        flops=2 * nodes * n_hid * rows * width,
    )
    total = summed_over(part, "dom")
    weight_grad, bias_grad = total[: n_hid * rows], total[n_hid * rows]
    (feature_grad,) = call(
        scatter_kernel,
        [out((rows, nodes), BF16)],
        [returned, nodes_out, kept, from_before, from_after],
        flops=2 * lists * nodes * rows,
    )
    return (output, feature_grad, weight_grad, bias_grad)


def solution(mesh):
    return jax.shard_map(
        on_device,
        mesh=mesh,
        in_specs=(
            P(None, "dom"),
            P(None, "hid"),
            P(None, "dom"),
            P(None, "dom"),
            P("dom", None, None),
            P("dom", None, None),
            P("dom", None, None),
            P("dom", None),
            P("hid"),
            P("hid", "dom"),
        ),
        out_specs=(P("hid", "dom"), P("hid", "dom"), P(None, "hid"), P("hid")),
        check_vma=False,
    )
```

time: 258 us -> 142 us (0.55)
  the two profiles are of different devices: /device:TPU:31 before, /device:TPU:1 now
where the time goes in v1:
time: 142 us; the launch traced here: 141 us
  waiting for transfers between devices  52.9 us (37%)
  starting transfers between devices  36.5 us (26%)
  Pallas kernels  25.1 us (18%)
  local copies, waits for them, and re-layouts  24.6 us (17%)
    ppermute x5, waiting for transfers between devices, swapped(): return lax.ppermute(block, axis, [(i, i ^ bit) for i in range(size)])  26.2 us
    pallas_call x10, Pallas kernels, call(): pl.pallas_call(kernel, out_shape=tuple(outs), in_specs=[SMEM] * scalars +...  25.1 us
    ppermute x8, waiting for transfers between devices, shifted(): lax.ppermute(block, axis, [((i + distance) % size, i) for i in range(size)])  24.9 us
    unnamed x45, local copies, waits for them, and re-layouts  23.9 us
    ppermute x5, starting transfers between devices, swapped(): return lax.ppermute(block, axis, [(i, i ^ bit) for i in range(size)])  14.6 us
    all_to_all x1, starting transfers between devices, on_device(): lax.all_to_all(message, 'dom', split_axis=0, concat_axis=0, tiled=True)  7.69 us
    all_to_all x1, starting transfers between devices, on_device(): lax.all_to_all(outgoing, 'dom', split_axis=0, concat_axis=0, tiled=True)  7.35 us
    ppermute x8, starting transfers between devices, shifted(): lax.ppermute(block, axis, [((i + distance) % size, i) for i in range(size)])  6.8 us
  transfers between devices with their start and end apart: 15, of which 8 were waited for; matrix products, arithmetic and copies ran while one was open for 1% of the time, Pallas kernels for 10%

profile of v1, /device:TPU:1, one launch (start us, length us, event | category | flops | bytes accessed | tf_op | source)
XLA Modules:
  0.0 141.1 jit_solution(12686081678285143444)
XLA Ops:
  2.6 2.4 %shard_map.131 = bf16[16,128,256]{2,1,0:T(8,128)(2,1)} custom-call(s32[1]{0:T(128)} %bitcast.hid_ref, bf16[512,1024]{1,0:T(8,128)(2,1)S(1)} %copy-done.12, s32[16,128]{1,0:T(8,128)S(1)} %bitcast.8), custom_call_target="tpu_custom_call" | custom-call | flops 1073741824 | bytes 2105348 | tf_op jit(solution)/shard_map/pallas_call | solution.py:19
  5.0 7.3 %all-to-all-start = ((bf16[16,128,256]{2,1,0:T(8,128)(2,1)}), bf16[16,128,256]{2,1,0:T(8,128)(2,1)S(1)}, u32[]{:S(2)}, u32[]{:S(2)}) async-start(bf16[16,128,256]{2,1,0:T(8,128)(2,1)} %shard_map.131), calls=%async_computation | async-start | bytes 2097152 | tf_op jit(solution)/shard_map/all_to_all | solution.py:225
  15.5 6.0 %shard_map.130 = (bf16[1024,2048]{1,0:T(8,128)(2,1)S(1)}, bf16[2048,1024]{1,0:T(8,128)(2,1)S(1)}, bf16[1024,2048]{1,0:T(8,128)(2,1)S(1)}) custom-call(s32[16,128]{1,0:T(8,128)S(1)} %bitcast.9, s32[16,128]{1,0:T(8,128)S(1)} %bitcast.10, f32[16,128]{1,0:T(8,128)S(1)} %bitcast.11, s32[16,1]{1,0:T(8,128)S(1)} %copy.14.counts_ref), custom_call_target="tpu_custom_call" | custom-call | flops 1073741824 | bytes 12607552 | tf_op jit(solution)/shard_map/pallas_call | solution.py:19
  21.5 2.0 %copy-done.2 = bf16[2048,1024]{1,0:T(8,128)(2,1)} copy-done((bf16[2048,1024]{1,0:T(8,128)(2,1)}, bf16[2048,1024]{1,0:T(8,128)(2,1)S(1)}, u32[]{:S(2)}) %copy-start.2) | copy-done | bytes 4194328
  23.5 2.0 %copy-done.4 = bf16[1024,2048]{1,0:T(8,128)(2,1)} copy-done((bf16[1024,2048]{1,0:T(8,128)(2,1)}, bf16[1024,2048]{1,0:T(8,128)(2,1)S(1)}, u32[]{:S(2)}) %copy-start.4) | copy-done | bytes 4194328
  25.5 2.0 %copy-done.6 = bf16[1024,2048]{1,0:T(8,128)(2,1)} copy-done((bf16[1024,2048]{1,0:T(8,128)(2,1)}, bf16[1024,2048]{1,0:T(8,128)(2,1)S(1)}, u32[]{:S(2)}) %copy-start.6) | copy-done | bytes 4194328
  27.5 4.5 %collective-permute-done.3.before_ref = bf16[256,1024]{1,0:T(8,128)(2,1)S(1)} collective-permute-done((bf16[256,1024]{1,0:T(8,128)(2,1)S(1)}, bf16[256,1024]{1,0:T(8,128)(2,1)S(1)}, u32[]{:S(2)}, u32[]{:S(2)}) %collective-permute-start.3) | collective-permute-done | bytes 524320 | tf_op jit(solution)/shard_map/ppermute | solution.py:36
  32.8 2.8 %copy-done = bf16[3072,1024]{1,0:T(8,128)(2,1)S(1)} copy-done((bf16[3072,1024]{1,0:T(8,128)(2,1)S(1)}, bf16[3072,1024]{1,0:T(8,128)(2,1)}, u32[]{:S(2)}) %copy-start) | copy-done | bytes 6291480
  36.6 2.7 %shard_map.132.dense_ref = f32[1024,256]{1,0:T(8,128)S(1)} custom-call(s32[12,4]{1,0:T(8,128)S(1)} %copy.15.live_ref, bf16[3072,1024]{1,0:T(8,128)(2,1)S(1)} %copy-done, bf16[256,1024]{1,0:T(8,128)(2,1)S(1)} %constant_dynamic-slice_fusion.own_ref, bf16[256,1024]{1,0:T(8,128)(2,1)S(1)} %collective-permute-done.3.before_ref, bf16[256,1024]{1,0:T(8,128)(2,1)S(1)} %copy-done.9), custom_call_target="tpu_custom_call" | custom-call | flops 1610612736 | bytes 8913088 | tf_op jit(solution)/shard_map/pallas_call | solution.py:19
  41.1 2.2 %copy-done.7 = bf16[1024,2048]{1,0:T(8,128)(2,1)S(1)} copy-done((bf16[1024,2048]{1,0:T(8,128)(2,1)S(1)}, bf16[1024,2048]{1,0:T(8,128)(2,1)}, u32[]{:S(2)}) %copy-start.7) | copy-done | bytes 4194328
  47.3 9.1 %collective-permute-done.1 = f32[256]{0:T(256)S(1)} collective-permute-done((f32[256]{0:T(256)S(1)}, f32[256]{0:T(256)S(1)}, u32[]{:S(2)}, u32[]{:S(2)}) %collective-permute-start.1) | collective-permute-done | bytes 1056 | tf_op jit(solution)/shard_map/ppermute | solution.py:36
  58.0 2.2 %copy-done.3 = bf16[2048,1024]{1,0:T(8,128)(2,1)S(1)} copy-done((bf16[2048,1024]{1,0:T(8,128)(2,1)S(1)}, bf16[2048,1024]{1,0:T(8,128)(2,1)}, u32[]{:S(2)}) %copy-start.3) | copy-done | bytes 4194328
  60.2 4.4 %shard_map.134 = (bf16[1024,256]{1,0:T(8,128)(2,1)S(1)}, bf16[1024,256]{1,0:T(8,128)(2,1)S(1)}, bf16[1024,256]{1,0:T(8,128)(2,1)S(1)}, bf16[16,128,256]{2,1,0:T(8,128)(2,1)}) custom-call(s32[1]{0:T(128)} %bitcast.hid_ref, bf16[512,512]{1,0:T(8,128)(2,1)S(1)} %pad_maximum_fusion.1.weight_ref, f32[1,512]{1,0:T(1,128)S(1)} %bitcast.7, ...), custom_call_target="tpu_custom_call" | custom-call | flops 1073741824 | bytes 9439236 | tf_op jit(solution)/shard_map/pallas_call | solution.py:19
  66.1 8.3 %collective-permute-start.8 = (bf16[272,256]{1,0:T(8,128)(2,1)S(1)}, bf16[272,256]{1,0:T(8,128)(2,1)S(1)}, u32[]{:S(2)}, u32[]{:S(2)}) collective-permute-start(bf16[272,256]{1,0:T(8,128)(2,1)S(1)} %select_convert_fusion), channel_id=1, source_target_pairs={{0,2},{2,0},{4,6},{6,4},{8,10},{10,8},{12,14},{14,12},{16,18},{18,... | collective-permute-start | bytes 417800 | tf_op jit(solution)/shard_map/ppermute | solution.py:41
  74.4 7.7 %all-to-all-start.1 = ((bf16[16,128,256]{2,1,0:T(8,128)(2,1)}), bf16[16,128,256]{2,1,0:T(8,128)(2,1)S(1)}, u32[]{:S(2)}, u32[]{:S(2)}) async-start(bf16[16,128,256]{2,1,0:T(8,128)(2,1)} %get-tuple-element.20), calls=%async_computation.1 | async-start | bytes 2097152 | tf_op jit(solution)/shard_map/all_to_all | solution.py:266
  83.6 10.6 %collective-permute-done.9 = bf16[272,256]{1,0:T(8,128)(2,1)S(1)} collective-permute-done((bf16[272,256]{1,0:T(8,128)(2,1)S(1)}, bf16[272,256]{1,0:T(8,128)(2,1)S(1)}, u32[]{:S(2)}, u32[]{:S(2)}) %collective-permute-start.9) | collective-permute-done | bytes 139296 | tf_op jit(solution)/shard_map/ppermute | solution.py:41
  94.3 8.4 %collective-permute-done.10 = bf16[272,256]{1,0:T(8,128)(2,1)S(1)} collective-permute-done((bf16[272,256]{1,0:T(8,128)(2,1)S(1)}, bf16[272,256]{1,0:T(8,128)(2,1)S(1)}, u32[]{:S(2)}, u32[]{:S(2)}) %collective-permute-start.10) | collective-permute-done | bytes 139296 | tf_op jit(solution)/shard_map/ppermute | solution.py:41
  102.8 3.9 %collective-permute-start.11 = (bf16[272,256]{1,0:T(8,128)(2,1)S(1)}, bf16[272,256]{1,0:T(8,128)(2,1)S(1)}, u32[]{:S(2)}, u32[]{:S(2)}) collective-permute-start(bf16[272,256]{1,0:T(8,128)(2,1)S(1)} %add_convert_fusion), channel_id=1, source_target_pairs={{0,16},{2,18},{4,20},{6,22},{8,24},{10,26},{12,28},{14,30},{16,0},... | collective-permute-start | bytes 417800 | tf_op jit(solution)/shard_map/ppermute | solution.py:41
  106.6 7.2 %collective-permute-done.11 = bf16[272,256]{1,0:T(8,128)(2,1)S(1)} collective-permute-done((bf16[272,256]{1,0:T(8,128)(2,1)S(1)}, bf16[272,256]{1,0:T(8,128)(2,1)S(1)}, u32[]{:S(2)}, u32[]{:S(2)}) %collective-permute-start.11) | collective-permute-done | bytes 139296 | tf_op jit(solution)/shard_map/ppermute | solution.py:41
  114.8 2.8 %copy-done.1 = bf16[3072,1024]{1,0:T(8,128)(2,1)S(1)} copy-done((bf16[3072,1024]{1,0:T(8,128)(2,1)S(1)}, bf16[3072,1024]{1,0:T(8,128)(2,1)}, u32[]{:S(2)}) %copy-start.1) | copy-done | bytes 6291480
  123.6 8.9 %collective-permute-done.6.before_ref = bf16[1024,256]{1,0:T(8,128)(2,1)S(1)} collective-permute-done((bf16[1024,256]{1,0:T(8,128)(2,1)S(1)}, bf16[1024,256]{1,0:T(8,128)(2,1)S(1)}, u32[]{:S(2)}, u32[]{:S(2)}) %collective-permute-start.6) | collective-permute-done | bytes 524320 | tf_op jit(solution)/shard_map/ppermute | solution.py:36
  132.4 2.5 %collective-permute-done.7.after_ref = bf16[1024,256]{1,0:T(8,128)(2,1)S(1)} collective-permute-done((bf16[1024,256]{1,0:T(8,128)(2,1)S(1)}, bf16[1024,256]{1,0:T(8,128)(2,1)S(1)}, u32[]{:S(2)}, u32[]{:S(2)}) %collective-permute-start.7) | collective-permute-done | bytes 524320 | tf_op jit(solution)/shard_map/ppermute | solution.py:36
  135.7 2.2 %copy-done.5 = bf16[1024,2048]{1,0:T(8,128)(2,1)S(1)} copy-done((bf16[1024,2048]{1,0:T(8,128)(2,1)S(1)}, bf16[1024,2048]{1,0:T(8,128)(2,1)}, u32[]{:S(2)}) %copy-start.5) | copy-done | bytes 4194328
  139.0 2.1 %shard_map.138 = bf16[256,1024]{1,0:T(8,128)(2,1)} custom-call(bf16[16,128,256]{2,1,0:T(8,128)(2,1)S(1)} %all-to-all-done.1.returned_ref, bf16[1024,2048]{1,0:T(8,128)(2,1)S(1)} %copy-done.5, f32[1024,256]{1,0:T(8,128)S(1)} %shard_map.136.own_ref, bf16[1024,256]{1,0:T(8,128)(2,1)S(1)} %collective-permute-done.6.before_ref, bf16[1024,256]{1,0:T(8,128)(2,1)S(1)} %copy-done.11), custom_call_target="tpu_custom_call" | custom-call | flops 1073741824 | bytes 7864320 | tf_op jit(solution)/shard_map/pallas_call | solution.py:19
  (73 shorter events, 26.2 us)
Async XLA Ops:
  0.6 14.9 %copy-start.15 = (s32[1,16,128]{2,1,0:T(8,128)S(1)}, s32[1,16,128]{2,1,0:T(8,128)}, u32[]{:S(2)}) copy-start(s32[1,16,128]{2,1,0:T(8,128)} %param.14) | copy-start | bytes 24580
  0.6 14.8 %copy-start.21 = (s32[1,16]{1,0:T(1,128)S(1)}, s32[1,16]{1,0:T(1,128)}, u32[]{:S(2)}) copy-start(s32[1,16]{1,0:T(1,128)} %param.17) | copy-start | bytes 196
  2.6 9.8 %copy-start.13 = (bf16[512,1024]{1,0:T(8,128)(2,1)S(1)}, bf16[512,1024]{1,0:T(8,128)(2,1)}, u32[]{:S(2)}) copy-start(bf16[512,1024]{1,0:T(8,128)(2,1)} %features_ref.1) | copy-start | bytes 3145732
  2.6 12.8 %copy-start.19 = (s32[12,4]{0,1:T(4,128)S(1)}, s32[12,4]{0,1:T(4,128)}, u32[]{:S(2)}) copy-start(s32[12,4]{0,1:T(4,128)} %param.13) | copy-start | bytes 580
  2.6 12.9 %copy-start.16 = (s32[1,16,128]{2,1,0:T(8,128)S(1)}, s32[1,16,128]{2,1,0:T(8,128)}, u32[]{:S(2)}) copy-start(s32[1,16,128]{2,1,0:T(8,128)} %param.15) | copy-start | bytes 24580
  2.6 12.9 %copy-start.17 = (f32[1,16,128]{2,1,0:T(8,128)S(1)}, f32[1,16,128]{2,1,0:T(8,128)}, u32[]{:S(2)}) copy-start(f32[1,16,128]{2,1,0:T(8,128)} %param.16) | copy-start | bytes 24580
  5.0 36.1 %all-to-all-start = ((bf16[16,128,256]{2,1,0:T(8,128)(2,1)}), bf16[16,128,256]{2,1,0:T(8,128)(2,1)S(1)}, u32[]{:S(2)}, u32[]{:S(2)}) async-start(bf16[16,128,256]{2,1,0:T(8,128)(2,1)} %shard_map.131), calls=%async_computation | async-start | bytes 2097152 | tf_op jit(solution)/shard_map/all_to_all | solution.py:225
  12.4 19.5 %collective-permute-start.3 = (bf16[256,1024]{1,0:T(8,128)(2,1)S(1)}, bf16[256,1024]{1,0:T(8,128)(2,1)S(1)}, u32[]{:S(2)}, u32[]{:S(2)}) collective-permute-start(bf16[256,1024]{1,0:T(8,128)(2,1)S(1)} %constant_dynamic-slice_fusion.own_ref), channel_id=1, source_target_pairs={{30,0},{0,2},{2,4},{4,6},{6,8},{8,10},{10,12},{12,14},{14,16},{16,... | collective-permute-start | bytes 1572872 | tf_op jit(solution)/shard_map/ppermute | solution.py:36
  14.1 17.9 %collective-permute-start.4 = (bf16[256,1024]{1,0:T(8,128)(2,1)S(1)}, bf16[256,1024]{1,0:T(8,128)(2,1)S(1)}, u32[]{:S(2)}, u32[]{:S(2)}) collective-permute-start(bf16[256,1024]{1,0:T(8,128)(2,1)S(1)} %constant_dynamic-slice_fusion.own_ref), channel_id=1, source_target_pairs={{2,0},{4,2},{6,4},{8,6},{10,8},{12,10},{14,12},{16,14},{18,16},{20... | collective-permute-start | bytes 1572872 | tf_op jit(solution)/shard_map/ppermute | solution.py:36
  14.1 42.4 %collective-permute-start.2 = (bf16[256,1024]{1,0:T(8,128)(2,1)}, bf16[256,1024]{1,0:T(8,128)(2,1)}, u32[]{:S(2)}, u32[]{:S(2)}) collective-permute-start(bf16[256,1024]{1,0:T(8,128)(2,1)} %refs_0_.1), channel_id=1, source_target_pairs={{1,0},{0,1},{3,2},{2,3},{5,4},{4,5},{7,6},{6,7},{9,8},{8,9},{11,10... | collective-permute-start | bytes 1572872 | tf_op jit(solution)/shard_map/ppermute | solution.py:36
  32.8 2.8 %copy-start = (bf16[3072,1024]{1,0:T(8,128)(2,1)S(1)}, bf16[3072,1024]{1,0:T(8,128)(2,1)}, u32[]{:S(2)}) copy-start(bf16[3072,1024]{1,0:T(8,128)(2,1)} %tiles_ref.5) | copy-start | bytes 18874372
  36.6 9.2 %copy-start.18 = (bf16[512,256]{1,0:T(8,128)(2,1)S(1)}, bf16[512,256]{1,0:T(8,128)(2,1)}, u32[]{:S(2)}) copy-start(bf16[512,256]{1,0:T(8,128)(2,1)} %param.11) | copy-start | bytes 786436
  39.3 6.8 %copy-start.20 = (f32[256]{0:T(256)S(1)}, f32[256]{0:T(256)}, u32[]{:S(2)}) copy-start(f32[256]{0:T(256)} %param.18) | copy-start | bytes 3076
  44.6 13.4 %collective-permute-start.5 = (bf16[1024,256]{1,0:T(8,128)(2,1)S(1)}, bf16[1024,256]{1,0:T(8,128)(2,1)S(1)}, u32[]{:S(2)}, u32[]{:S(2)}) collective-permute-start(bf16[1024,256]{1,0:T(8,128)(2,1)S(1)} %shard_map.133.refs_0_), channel_id=1, source_target_pairs={{1,0},{0,1},{3,2},{2,3},{5,4},{4,5},{7,6},{6,7},{9,8},{8,9},{11,10... | collective-permute-start | bytes 1572872 | tf_op jit(solution)/shard_map/ppermute | solution.py:36
  45.9 10.6 %collective-permute-start = (bf16[512,256]{1,0:T(8,128)(2,1)S(1)}, bf16[512,256]{1,0:T(8,128)(2,1)S(1)}, u32[]{:S(2)}, u32[]{:S(2)}) collective-permute-start(bf16[512,256]{1,0:T(8,128)(2,1)S(1)} %copy-done.18), channel_id=1, source_target_pairs={{1,0},{0,1},{3,2},{2,3},{5,4},{4,5},{7,6},{6,7},{9,8},{8,9},{11,10... | collective-permute-start | bytes 786440 | tf_op jit(solution)/shard_map/ppermute | solution.py:36
  46.1 10.3 %collective-permute-start.1 = (f32[256]{0:T(256)S(1)}, f32[256]{0:T(256)S(1)}, u32[]{:S(2)}, u32[]{:S(2)}) collective-permute-start(f32[256]{0:T(256)S(1)} %copy-done.20), channel_id=1, source_target_pairs={{1,0},{0,1},{3,2},{2,3},{5,4},{4,5},{7,6},{6,7},{9,8},{8,9},{11,10... | collective-permute-start | bytes 3080 | tf_op jit(solution)/shard_map/ppermute | solution.py:36
  66.1 16.0 %collective-permute-start.8 = (bf16[272,256]{1,0:T(8,128)(2,1)S(1)}, bf16[272,256]{1,0:T(8,128)(2,1)S(1)}, u32[]{:S(2)}, u32[]{:S(2)}) collective-permute-start(bf16[272,256]{1,0:T(8,128)(2,1)S(1)} %select_convert_fusion), channel_id=1, source_target_pairs={{0,2},{2,0},{4,6},{6,4},{8,10},{10,8},{12,14},{14,12},{16,18},{18,... | collective-permute-start | bytes 417800 | tf_op jit(solution)/shard_map/ppermute | solution.py:41
  74.4 61.3 %all-to-all-start.1 = ((bf16[16,128,256]{2,1,0:T(8,128)(2,1)}), bf16[16,128,256]{2,1,0:T(8,128)(2,1)S(1)}, u32[]{:S(2)}, u32[]{:S(2)}) async-start(bf16[16,128,256]{2,1,0:T(8,128)(2,1)} %get-tuple-element.20), calls=%async_computation.1 | async-start | bytes 2097152 | tf_op jit(solution)/shard_map/all_to_all | solution.py:266
  82.2 12.0 %collective-permute-start.9 = (bf16[272,256]{1,0:T(8,128)(2,1)S(1)}, bf16[272,256]{1,0:T(8,128)(2,1)S(1)}, u32[]{:S(2)}, u32[]{:S(2)}) collective-permute-start(bf16[272,256]{1,0:T(8,128)(2,1)S(1)} %add_convert_fusion.2), channel_id=1, source_target_pairs={{0,4},{2,6},{4,0},{6,2},{8,12},{10,14},{12,8},{14,10},{16,20},{18,... | collective-permute-start | bytes 417800 | tf_op jit(solution)/shard_map/ppermute | solution.py:41
  94.3 8.5 %collective-permute-start.10 = (bf16[272,256]{1,0:T(8,128)(2,1)S(1)}, bf16[272,256]{1,0:T(8,128)(2,1)S(1)}, u32[]{:S(2)}, u32[]{:S(2)}) collective-permute-start(bf16[272,256]{1,0:T(8,128)(2,1)S(1)} %add_convert_fusion.1), channel_id=1, source_target_pairs={{0,8},{2,10},{4,12},{6,14},{8,0},{10,2},{12,4},{14,6},{16,24},{18,... | collective-permute-start | bytes 417800 | tf_op jit(solution)/shard_map/ppermute | solution.py:41
  102.8 11.1 %collective-permute-start.11 = (bf16[272,256]{1,0:T(8,128)(2,1)S(1)}, bf16[272,256]{1,0:T(8,128)(2,1)S(1)}, u32[]{:S(2)}, u32[]{:S(2)}) collective-permute-start(bf16[272,256]{1,0:T(8,128)(2,1)S(1)} %add_convert_fusion), channel_id=1, source_target_pairs={{0,16},{2,18},{4,20},{6,22},{8,24},{10,26},{12,28},{14,30},{16,0},... | collective-permute-start | bytes 417800 | tf_op jit(solution)/shard_map/ppermute | solution.py:41
  113.9 8.2 %collective-permute-start.12 = (f32[272,256]{1,0:T(8,128)S(1)}, f32[272,256]{1,0:T(8,128)S(1)}, u32[]{:S(2)}, u32[]{:S(2)}) collective-permute-start(f32[272,256]{1,0:T(8,128)S(1)} %convert_add_fusion), channel_id=1, source_target_pairs={{0,2},{2,0},{4,6},{6,4},{8,10},{10,8},{12,14},{14,12},{16,18},{18,... | collective-permute-start | bytes 835592 | tf_op jit(solution)/shard_map/ppermute | solution.py:41
  119.5 12.9 %collective-permute-start.6 = (bf16[1024,256]{1,0:T(8,128)(2,1)S(1)}, bf16[1024,256]{1,0:T(8,128)(2,1)S(1)}, u32[]{:S(2)}, u32[]{:S(2)}) collective-permute-start(bf16[1024,256]{1,0:T(8,128)(2,1)S(1)} %get-tuple-element.23), channel_id=1, source_target_pairs={{30,0},{0,2},{2,4},{4,6},{6,8},{8,10},{10,12},{12,14},{14,16},{16,... | collective-permute-start | bytes 1572872 | tf_op jit(solution)/shard_map/ppermute | solution.py:36
  120.7 14.2 %collective-permute-start.7 = (bf16[1024,256]{1,0:T(8,128)(2,1)S(1)}, bf16[1024,256]{1,0:T(8,128)(2,1)S(1)}, u32[]{:S(2)}, u32[]{:S(2)}) collective-permute-start(bf16[1024,256]{1,0:T(8,128)(2,1)S(1)} %get-tuple-element.24), channel_id=1, source_target_pairs={{2,0},{4,2},{6,4},{8,6},{10,8},{12,10},{14,12},{16,14},{18,16},{20... | collective-permute-start | bytes 1572872 | tf_op jit(solution)/shard_map/ppermute | solution.py:36
  (13 other events, 21.0 us)

commit v2 on v0

v2 whole, which is shorter than its diff:
```python
import functools

import jax
import jax.numpy as jnp
from jax import lax
from jax.experimental import pallas as pl
from jax.experimental.pallas import tpu as pltpu
from jax.sharding import PartitionSpec as P

TILE = 256
F32 = jnp.float32
BF16 = jnp.bfloat16
VMEM = pl.BlockSpec(memory_space=pltpu.VMEM)
SMEM = pl.BlockSpec(memory_space=pltpu.SMEM)
HBM = pl.BlockSpec(memory_space=pltpu.HBM)


def call(kernel, outs, operands, scratch=(), us=1, mib=16, place=VMEM):
    arrays = [array for _, array in operands]
    return pl.pallas_call(
        kernel,
        out_shape=tuple(outs),
        in_specs=[place for place, _ in operands],
        out_specs=tuple(place for _ in outs),
        scratch_shapes=scratch,
        compiler_params=pltpu.CompilerParams(vmem_limit_bytes=mib * 1024 * 1024),
        cost_estimate=pl.CostEstimate(flops=us * 1000**3, bytes_accessed=1, transcendentals=0),
    )(*arrays)


def out(shape, dtype):
    return jax.ShapeDtypeStruct(shape, dtype)


def shifted(block, axis, distance):
    size = lax.axis_size(axis)
    return lax.ppermute(block, axis, [((i + distance) % size, i) for i in range(size)])


def swapped(block, axis, bit):
    size = lax.axis_size(axis)
    return lax.ppermute(block, axis, [(i, i ^ bit) for i in range(size)])


def dot(a, b):
    return jnp.dot(a, b, preferred_element_type=F32)


def slots_by_nodes(hot, rows_t, nodes, first, count, weights_t=None):
    slots = rows_t.shape[0]
    lanes = lax.broadcasted_iota(jnp.int32, (slots, nodes), 1)
    for p in range(first, first + count):
        value = 1.0 if weights_t is None else weights_t[:, p : p + 1]
        hot[p * slots : (p + 1) * slots, :] = jnp.where(
            rows_t[:, p : p + 1] == lanes, value, 0.0
        ).astype(BF16)


def nodes_by_slots(hot, rows, nodes, weights=None):
    peers, slots = rows.shape
    lines = lax.broadcasted_iota(jnp.int32, (nodes, slots), 0)
    for p in range(peers):
        value = 1.0 if weights is None else weights[p : p + 1, :]
        hot[:, p * slots : (p + 1) * slots] = jnp.where(
            rows[p : p + 1, :] == lines, value, 0.0
        ).astype(BF16)


def masked_weights(weight, counts):
    slots = lax.broadcasted_iota(jnp.int32, weight.shape, 1)
    return jnp.where(slots < counts, weight, 0.0)


class Copies:
    def __init__(self, sems):
        self.sems, self.started = sems, []

    def start(self, source, target):
        copy = pltpu.make_async_copy(source, target, self.sems.at[len(self.started)])
        copy.start()
        self.started.append(copy)
        return copy


def vmem(shape, dtype):
    return pltpu.VMEM(shape, dtype)


def sems(count):
    return pltpu.SemaphoreType.DMA((count,))


def gather_kernel(hid_ref, features_ref, send_ref, out_ref, hot, block, lists, picked, sems):
    peers, slots, rows = out_ref.shape
    nodes = features_ref.shape[1]
    copies = Copies(sems)
    start = pl.multiple_of(hid_ref[0] * rows, rows)
    lists_copy = copies.start(send_ref, lists)
    block_copy = copies.start(features_ref.at[pl.ds(start, rows), :], block)
    lists_copy.wait()
    send_t = lists[...].T
    group = 4
    slots_by_nodes(hot, send_t, nodes, 0, group)
    block_copy.wait()
    sent = []
    block_t = block[...].T
    for p in range(0, peers, group):
        part = dot(hot[p * slots : (p + group) * slots, :], block_t)
        picked[p : p + group] = part.astype(BF16).reshape(group, slots, rows)
        sent.append(copies.start(picked.at[pl.ds(p, group)], out_ref.at[pl.ds(p, group)]))
        if p + group < peers:
            slots_by_nodes(hot, send_t, nodes, p + group, group)
    for copy in sent:
        copy.wait()


def live_lines(live_ref, s, i, side, axis):
    shape = (1, side * TILE) if axis else (side * TILE, 1)
    place = lax.broadcasted_iota(jnp.int32, shape, axis) // TILE
    live = jnp.zeros(shape, F32)
    for j in range(side):
        live = jnp.where(place == j, live_ref[s * side + j, i].astype(F32), live)
    return live.astype(BF16)


def dense_forward(live_ref, tiles_ref, block_ref, s, i, first):
    nodes = block_ref.shape[1]
    side = nodes // TILE
    left = block_ref[...] * live_lines(live_ref, s, i, side, 1)
    return dot(left, tiles_ref[first : first + nodes, i * TILE : (i + 1) * TILE])


def dense_kernel(live_ref, tiles_ref, before_ref, own_ref, after_ref, out_ref):
    nodes = out_ref.shape[0]
    for i in range(nodes // TILE):
        total = None
        for s, ref in enumerate((before_ref, own_ref, after_ref)):
            term = dense_forward(live_ref, tiles_ref, ref, s, i, s * nodes)
            total = term if total is None else total + term
        out_ref[i * TILE : (i + 1) * TILE, :] = total.T


def aggregate_kernel(recv_ref, weight_ref, counts_ref, arrived_ref, dense_ref, out_ref, hot):
    peers, slots, rows = arrived_ref.shape
    nodes_by_slots(hot, recv_ref[...], out_ref.shape[0], masked_weights(weight_ref[...], counts_ref[...]))
    arrived = arrived_ref[...].reshape(peers * slots, rows)
    out_ref[...] = (dense_ref[...] + dot(hot[...], arrived)).astype(BF16)


def dense_backward(live_ref, tiles, block, s, first):
    nodes = block.shape[0]
    side = nodes // TILE
    place = lax.broadcasted_iota(jnp.int32, (nodes, 1), 0) // TILE
    for j in range(side):
        live = jnp.zeros((nodes, 1), F32)
        for i in range(side):
            live = jnp.where(place == i, live_ref[s * side + j, i].astype(F32), live)
        row = first + j * TILE
        yield j, dot(tiles[row : row + TILE, :], block * live.astype(BF16))


def dense_backward_kernel(parts, live_ref, tiles_ref, back_ref, *out_refs):
    nodes = back_ref.shape[0]
    for s, out_ref in zip(parts, out_refs):
        for j, term in dense_backward(live_ref, tiles_ref, back_ref[...], s, s * nodes):
            out_ref[j * TILE : (j + 1) * TILE, :] = term.astype(out_ref.dtype)


def weight_parts(hid_ref, grad, aggs, part_ref):
    n_hid, _, rows = aggs.shape
    for k in range(n_hid):
        start = pl.multiple_of(lax.rem(hid_ref[0] + k, n_hid) * rows, rows)
        part_ref[pl.ds(start, rows), :] = dot(aggs[k].T, grad)
    total = jnp.sum(grad.astype(F32), axis=0, keepdims=True)
    size = n_hid * rows
    part_ref[size:, :] = jnp.broadcast_to(total, (part_ref.shape[0] - size, part_ref.shape[1]))


def layer_kernel(n_hid, hid_ref, *refs):
    take = iter(refs)
    weights, biases, cotangents = ([next(take) for _ in range(n_hid)] for _ in range(3))
    aggs, recv_ref, weight_ref, counts_ref, output_ref, part_ref, back_ref, message_ref, hot = take
    peers, slots, rows = message_ref.shape
    width, nodes = output_ref.shape
    own = pl.ds(pl.multiple_of(hid_ref[0] * rows, rows), rows)
    total = None
    for k in range(n_hid):
        act = jnp.broadcast_to(biases[k][...], (nodes, width))
        for j in range(n_hid):
            start = pl.multiple_of(lax.rem(hid_ref[0] + j, n_hid) * rows, rows)
            act = act + dot(aggs[j], weights[k][pl.ds(start, rows), :])
        gate = 1.0 / (1.0 + jnp.exp(-act))
        slope = gate * (1.0 + act * (1.0 - gate))
        grad = (cotangents[k][...].T.astype(F32) * slope).astype(BF16)
        if k == 0:
            output_ref[...] = (act * gate).astype(BF16).T
            weight_parts(hid_ref, grad, aggs, part_ref)
        term = lax.dot_general(
            grad, weights[k][own, :], (((1,), (1,)), ((), ())), preferred_element_type=F32
        )
        total = term if total is None else total + term
    back = total.astype(BF16)
    back_ref[...] = back
    weights_t = masked_weights(weight_ref[...], counts_ref[...]).T
    recv_t = recv_ref[...].T
    group = 4
    for p in range(0, peers, group):
        slots_by_nodes(hot, recv_t, nodes, p, group, weights_t)
        picked = dot(hot[p * slots : (p + group) * slots, :], back)
        message_ref[p : p + group] = picked.astype(BF16).reshape(group, slots, rows)


def joined_kernel(odd_ref, mine_ref, other_ref, weight_ref, bias_ref):
    half = mine_ref.shape[0]
    odd = odd_ref[0] == 1
    low = jnp.where(odd, other_ref[...], mine_ref[...])
    high = jnp.where(odd, mine_ref[...], other_ref[...])
    size = weight_ref.shape[0]
    weight_ref[:half, :] = low
    weight_ref[half:, :] = high[: size - half, :]
    bias_ref[...] = high[size - half : size - half + 1, :]


def scatter_kernel(send_ref, returned_ref, own_ref, before_ref, after_ref, out_ref, hot):
    peers, slots, rows = returned_ref.shape
    nodes_by_slots(hot, send_ref[...], own_ref.shape[0])
    returned = returned_ref[...].reshape(peers * slots, rows)
    total = own_ref[...] + before_ref[...].astype(F32) + after_ref[...].astype(F32)
    total = total + dot(hot[...], returned)
    out_ref[...] = total.astype(BF16).T


def halved(part, axis, bits):
    place = lax.axis_index(axis)
    for bit in bits:
        odd = lax.rem(place // bit, 2) == 1
        half = part.shape[0] // 2
        low, high = part[:half], part[half:]
        arrived = swapped(jnp.where(odd, low, high).astype(BF16), axis, bit)
        part = jnp.where(odd, high, low) + arrived.astype(F32)
    return part


def doubled(part, axis, bits):
    for bit in bits:
        sent = part.astype(BF16)
        part = sent.astype(F32) + swapped(sent, axis, bit).astype(F32)
    return part


def joined(part, axis, bits):
    place = lax.axis_index(axis)
    for bit in reversed(bits):
        odd = lax.rem(place // bit, 2) == 1
        other = swapped(part, axis, bit)
        part = jnp.concatenate([jnp.where(odd, other, part), jnp.where(odd, part, other)])
    return part


def on_device(
    features,
    weight,
    band_tiles,
    tile_live,
    send_rows,
    recv_rows,
    edge_weight,
    live_slots,
    bias_terms,
    cotangent,
):
    n_hid = lax.axis_size("hid")
    hid = (SMEM, lax.axis_index("hid").astype(jnp.int32).reshape(1))
    peers, slots = send_rows.shape[1:]
    nodes = features.shape[1]
    width = weight.shape[1]
    rows = features.shape[0] // n_hid
    lists = peers * slots
    send, recv = (VMEM, send_rows[0]), (VMEM, recv_rows[0])
    edges = [recv, (VMEM, edge_weight[0]), (VMEM, live_slots.reshape(peers, 1))]
    tiles = [(SMEM, tile_live), (VMEM, band_tiles)]
    steps = range(1, n_hid)

    own = lax.dynamic_slice_in_dim(features, hid[1][0] * rows, rows, 0)
    before, after = shifted(own, "dom", -1), shifted(own, "dom", 1)
    (outgoing,) = call(
        gather_kernel,
        [out((peers, slots, rows), BF16)],
        [hid, (HBM, features), (HBM, send_rows[0])],
        [
            vmem((lists, nodes), BF16),
            vmem((rows, nodes), BF16),
            vmem((peers, slots), jnp.int32),
            vmem((peers, slots, rows), BF16),
            sems(peers + 2),
        ],
        mib=58,
        place=HBM,
    )
    arrived = lax.all_to_all(outgoing, "dom", split_axis=0, concat_axis=0, tiled=True)

    before, weight, bias_terms, cotangent = lax.optimization_barrier(
        (before, weight, bias_terms, cotangent)
    )
    weights = [weight] + [shifted(weight, "hid", k) for k in steps]
    biases = [bias_terms] + [shifted(bias_terms, "hid", k) for k in steps]
    cotangents = [cotangent] + [shifted(cotangent, "hid", k) for k in steps]
    (dense,) = call(
        dense_kernel,
        [out((nodes, rows), F32)],
        [*tiles, (VMEM, before), (VMEM, own), (VMEM, after)],
        us=60,
    )
    dense, weights, biases, cotangents = lax.optimization_barrier((dense, weights, biases, cotangents))
    (agg,) = call(
        aggregate_kernel,
        [out((nodes, rows), BF16)],
        [*edges, (VMEM, arrived), (VMEM, dense)],
        [vmem((nodes, lists), BF16)],
        us=4,
    )
    aggs = jnp.stack([agg] + [shifted(agg, "hid", k) for k in steps])
    pad = 64
    output, part, back, message = call(
        functools.partial(layer_kernel, n_hid),
        [
            out((width, nodes), BF16),
            out((n_hid * rows + pad, width), F32),
            out((nodes, rows), BF16),
            out((peers, slots, rows), BF16),
        ],
        [
            hid,
            *[(VMEM, w) for w in weights],
            *[(VMEM, b[None, :]) for b in biases],
            *[(VMEM, c) for c in cotangents],
            (VMEM, aggs),
            *edges,
        ],
        [vmem((lists, nodes), BF16)],
        us=6,
        mib=24,
    )
    returned = lax.all_to_all(message, "dom", split_axis=0, concat_axis=0, tiled=True)

    to_before, to_after = call(
        functools.partial(dense_backward_kernel, (0, 2)),
        [out((nodes, rows), BF16)] * 2,
        [*tiles, (VMEM, back)],
    )
    (kept,) = call(
        functools.partial(dense_backward_kernel, (1,)),
        [out((nodes, rows), F32)],
        [*tiles, (VMEM, back)],
    )
    bits = [1 << b for b in range((peers - 1).bit_length())]
    part = halved(part, "dom", bits[:1])
    part, to_before, to_after = lax.optimization_barrier((part, to_before, to_after))
    from_after, from_before = shifted(to_before, "dom", 1), shifted(to_after, "dom", -1)
    part = halved(part, "dom", bits[1:2])
    part = doubled(part, "dom", bits[2:3])
    part, from_after, from_before, kept = lax.optimization_barrier((part, from_after, from_before, kept))
    part = doubled(part, "dom", bits[3:])
    (feature_grad,) = call(
        scatter_kernel,
        [out((rows, nodes), BF16)],
        [send, (VMEM, returned), (VMEM, kept), (VMEM, from_before), (VMEM, from_after)],
        [vmem((nodes, lists), BF16)],
    )
    part = joined(part, "dom", bits[1:2])
    part, feature_grad = lax.optimization_barrier((part, feature_grad))
    odd = lax.rem(lax.axis_index("dom"), 2).astype(jnp.int32).reshape(1)
    weight_grad, bias_grad = call(
        joined_kernel,
        [out((n_hid * rows, width), F32), out((1, width), F32)],
        [(SMEM, odd), (VMEM, part), (VMEM, swapped(part, "dom", 1))],
    )
    return (output, feature_grad, weight_grad, bias_grad[0])


def solution(mesh):
    return jax.shard_map(
        on_device,
        mesh=mesh,
        in_specs=(
            P(None, "dom"),
            P(None, "hid"),
            P(None, "dom"),
            P(None, "dom"),
            P("dom", None, None),
            P("dom", None, None),
            P("dom", None, None),
            P("dom", None),
            P("hid"),
            P("hid", "dom"),
        ),
        out_specs=(P("hid", "dom"), P("hid", "dom"), P(None, "hid"), P("hid")),
        check_vma=False,
    )
```

time: 258 us -> 116 us (0.45)
  the two profiles are of different devices: /device:TPU:31 before, /device:TPU:0 now
where the time goes in v2:
time: 116 us; the launch traced here: 115 us
  waiting for transfers between devices  49.6 us (43%)
  starting transfers between devices  33.7 us (29%)
  Pallas kernels  18.9 us (16%)
  local copies, waits for them, and re-layouts  12 us (10%)
    ppermute x6, waiting for transfers between devices, swapped(): return lax.ppermute(block, axis, [(i, i ^ bit) for i in range(size)])  24.6 us
    ppermute x8, waiting for transfers between devices, shifted(): lax.ppermute(block, axis, [((i + distance) % size, i) for i in range(size)])  24.4 us
    pallas_call x8, Pallas kernels, call(): pl.pallas_call(kernel, out_shape=tuple(outs), in_specs=[place for place,...  18.9 us
    ppermute x8, starting transfers between devices, shifted(): lax.ppermute(block, axis, [((i + distance) % size, i) for i in range(size)])  14.1 us
    unnamed x33, local copies, waits for them, and re-layouts  10.8 us
    ppermute x6, starting transfers between devices, swapped(): return lax.ppermute(block, axis, [(i, i ^ bit) for i in range(size)])  9.29 us
    all_to_all x1, starting transfers between devices, on_device(): lax.all_to_all(message, 'dom', split_axis=0, concat_axis=0, tiled=True)  6.61 us
    all_to_all x1, starting transfers between devices, on_device(): lax.all_to_all(outgoing, 'dom', split_axis=0, concat_axis=0, tiled=True)  3.66 us
  transfers between devices with their start and end apart: 16, of which 9 were waited for; matrix products, arithmetic and copies ran while one was open for 0% of the time, Pallas kernels for 8%

profile of v2, /device:TPU:0, one launch (start us, length us, event | category | flops | bytes accessed | tf_op | source)
XLA Modules:
  0.0 115.4 jit_solution(3102442501728474772)
XLA Ops:
  2.3 5.1 %collective-permute-start.1 = (bf16[256,1024]{1,0:T(8,128)(2,1)S(1)}, bf16[256,1024]{1,0:T(8,128)(2,1)}, u32[]{:S(2)}, u32[]{:S(2)}) collective-permute-start(bf16[256,1024]{1,0:T(8,128)(2,1)S(1)} %constant_dynamic-slice_fusion.own_ref), channel_id=1, source_target_pairs={{2,0},{4,2},{6,4},{8,6},{10,8},{12,10},{14,12},{16,14},{18,16},{20... | collective-permute-start | bytes 1572872 | tf_op jit(solution)/shard_map/ppermute | solution.py:37
  7.4 3.3 %shard_map.130 = bf16[16,128,256]{2,1,0:T(8,128)(2,1)} custom-call(s32[1]{0:T(128)} %bitcast.hid_ref, bf16[512,1024]{1,0:T(8,128)(2,1)} %features_ref.1, s32[16,128]{1,0:T(8,128)} %bitcast.16), custom_call_target="tpu_custom_call" | custom-call | flops 1000000000 | bytes 1 | tf_op jit(solution)/shard_map/pallas_call | solution.py:20
  10.8 3.7 %all-to-all-start = ((bf16[16,128,256]{2,1,0:T(8,128)(2,1)}), bf16[16,128,256]{2,1,0:T(8,128)(2,1)S(1)}, u32[]{:S(2)}, u32[]{:S(2)}) async-start(bf16[16,128,256]{2,1,0:T(8,128)(2,1)} %shard_map.130), calls=%async_computation | async-start | bytes 2097152 | tf_op jit(solution)/shard_map/all_to_all | solution.py:300
  15.4 1.9 %collective-permute-start.3 = (f32[256]{0:T(256)S(1)}, f32[256]{0:T(256)S(1)}, u32[]{:S(2)}, u32[]{:S(2)}) collective-permute-start(f32[256]{0:T(256)S(1)} %copy-done.11), channel_id=1, source_target_pairs={{1,0},{0,1},{3,2},{2,3},{5,4},{4,5},{7,6},{6,7},{9,8},{8,9},{11,10... | collective-permute-start | bytes 3080 | tf_op jit(solution)/shard_map/ppermute | solution.py:37
  17.5 1.9 %collective-permute-start.4 = (bf16[256,1024]{1,0:T(8,128)(2,1)S(1)}, bf16[256,1024]{1,0:T(8,128)(2,1)S(1)}, u32[]{:S(2)}, u32[]{:S(2)}) collective-permute-start(bf16[256,1024]{1,0:T(8,128)(2,1)S(1)} %copy-done.2), channel_id=1, source_target_pairs={{1,0},{0,1},{3,2},{2,3},{5,4},{4,5},{7,6},{6,7},{9,8},{8,9},{11,10... | collective-permute-start | bytes 1572872 | tf_op jit(solution)/shard_map/ppermute | solution.py:37
  19.3 2.8 %copy-done = bf16[3072,1024]{1,0:T(8,128)(2,1)S(1)} copy-done((bf16[3072,1024]{1,0:T(8,128)(2,1)S(1)}, bf16[3072,1024]{1,0:T(8,128)(2,1)}, u32[]{:S(2)}) %copy-start) | copy-done | bytes 6291480
  23.2 3.0 %shard_map.129.dense_ref = f32[1024,256]{1,0:T(8,128)S(1)} custom-call(s32[12,4]{1,0:T(8,128)S(1)} %copy.14.live_ref, bf16[3072,1024]{1,0:T(8,128)(2,1)S(1)} %copy-done, bf16[256,1024]{1,0:T(8,128)(2,1)S(1)} %copy-done.6, bf16[256,1024]{1,0:T(8,128)(2,1)S(1)} %constant_dynamic-slice_fusion.own_ref, bf16[256,1024]{1,0:T(8,128)(2,1)} %collective-permute-done.1.after_ref), custom_call_target="tpu_custom_call" | custom-call | flops 60000002048 | bytes 1 | tf_op jit(solution)/shard_map/pallas_call | solution.py:20
  27.1 9.7 %collective-permute-done.4.refs_5_ = bf16[256,1024]{1,0:T(8,128)(2,1)S(1)} collective-permute-done((bf16[256,1024]{1,0:T(8,128)(2,1)S(1)}, bf16[256,1024]{1,0:T(8,128)(2,1)S(1)}, u32[]{:S(2)}, u32[]{:S(2)}) %collective-permute-start.4) | collective-permute-done | bytes 524320 | tf_op jit(solution)/shard_map/ppermute | solution.py:37
  40.1 1.9 %collective-permute-start.5 = (bf16[1024,256]{1,0:T(8,128)(2,1)S(1)}, bf16[1024,256]{1,0:T(8,128)(2,1)S(1)}, u32[]{:S(2)}, u32[]{:S(2)}) collective-permute-start(bf16[1024,256]{1,0:T(8,128)(2,1)S(1)} %shard_map.131), channel_id=1, source_target_pairs={{1,0},{0,1},{3,2},{2,3},{5,4},{4,5},{7,6},{6,7},{9,8},{8,9},{11,10... | collective-permute-start | bytes 1572872 | tf_op jit(solution)/shard_map/ppermute | solution.py:37
  42.0 12.7 %collective-permute-done.5 = bf16[1024,256]{1,0:T(8,128)(2,1)S(1)} collective-permute-done((bf16[1024,256]{1,0:T(8,128)(2,1)S(1)}, bf16[1024,256]{1,0:T(8,128)(2,1)S(1)}, u32[]{:S(2)}, u32[]{:S(2)}) %collective-permute-start.5) | collective-permute-done | bytes 524320 | tf_op jit(solution)/shard_map/ppermute | solution.py:37
  54.8 4.4 %shard_map.132 = (bf16[256,1024]{1,0:T(8,128)(2,1)}, f32[576,256]{1,0:T(8,128)S(1)}, bf16[1024,256]{1,0:T(8,128)(2,1)S(1)}, bf16[16,128,256]{2,1,0:T(8,128)(2,1)}) custom-call(s32[1]{0:T(128)} %bitcast.hid_ref, bf16[512,256]{1,0:T(8,128)(2,1)S(1)} %copy-done.7, bf16[512,256]{1,0:T(8,128)(2,1)S(1)} %collective-permute-done.2.refs_1_, f32[1,256]{1,0:T(1,128)S(1)} %bitcast.18, ...), custom_call_target="tpu_custom_call" | custom-call | flops 6000000000 | bytes 1 | tf_op jit(solution)/shard_map/pallas_call | solution.py:20
  59.3 6.6 %all-to-all-start.1 = ((bf16[16,128,256]{2,1,0:T(8,128)(2,1)}), bf16[16,128,256]{2,1,0:T(8,128)(2,1)S(1)}, u32[]{:S(2)}, u32[]{:S(2)}) async-start(bf16[16,128,256]{2,1,0:T(8,128)(2,1)} %get-tuple-element.52), calls=%async_computation.1 | async-start | bytes 2097152 | tf_op jit(solution)/shard_map/all_to_all | solution.py:344
  65.9 2.8 %copy-done.1 = bf16[3072,1024]{1,0:T(8,128)(2,1)S(1)} copy-done((bf16[3072,1024]{1,0:T(8,128)(2,1)S(1)}, bf16[3072,1024]{1,0:T(8,128)(2,1)}, u32[]{:S(2)}) %copy-start.1) | copy-done | bytes 6291480
  68.7 2.0 %shard_map.133 = (bf16[1024,256]{1,0:T(8,128)(2,1)S(1)}, bf16[1024,256]{1,0:T(8,128)(2,1)S(1)}) custom-call(s32[12,4]{1,0:T(8,128)S(1)} %copy.14.live_ref, bf16[3072,1024]{1,0:T(8,128)(2,1)S(1)} %copy-done.1, bf16[1024,256]{1,0:T(8,128)(2,1)S(1)} %get-tuple-element.45.back_ref), custom_call_target="tpu_custom_call" | custom-call | flops 1000000000 | bytes 1 | tf_op jit(solution)/shard_map/pallas_call | solution.py:20
  70.8 2.0 %collective-permute-start.7 = (bf16[144,256]{1,0:T(8,128)(2,1)S(1)}, bf16[144,256]{1,0:T(8,128)(2,1)S(1)}, u32[]{:S(2)}, u32[]{:S(2)}) collective-permute-start(bf16[144,256]{1,0:T(8,128)(2,1)S(1)} %select_convert_fusion.1), channel_id=1, source_target_pairs={{0,4},{2,6},{4,0},{6,2},{8,12},{10,14},{12,8},{14,10},{16,20},{18,... | collective-permute-start | bytes 221192 | tf_op jit(solution)/shard_map/ppermute | solution.py:42
  72.8 2.7 %collective-permute-start.9 = (bf16[1024,256]{1,0:T(8,128)(2,1)S(1)}, bf16[1024,256]{1,0:T(8,128)(2,1)S(1)}, u32[]{:S(2)}, u32[]{:S(2)}) collective-permute-start(bf16[1024,256]{1,0:T(8,128)(2,1)S(1)} %get-tuple-element.49), channel_id=1, source_target_pairs={{2,0},{4,2},{6,4},{8,6},{10,8},{12,10},{14,12},{16,14},{18,16},{20... | collective-permute-start | bytes 1572872 | tf_op jit(solution)/shard_map/ppermute | solution.py:37
  75.5 1.7 %collective-permute-done.7 = bf16[144,256]{1,0:T(8,128)(2,1)S(1)} collective-permute-done((bf16[144,256]{1,0:T(8,128)(2,1)S(1)}, bf16[144,256]{1,0:T(8,128)(2,1)S(1)}, u32[]{:S(2)}, u32[]{:S(2)}) %collective-permute-start.7) | collective-permute-done | bytes 73760 | tf_op jit(solution)/shard_map/ppermute | solution.py:42
  79.3 13.8 %collective-permute-done.8 = bf16[144,256]{1,0:T(8,128)(2,1)S(1)} collective-permute-done((bf16[144,256]{1,0:T(8,128)(2,1)S(1)}, bf16[144,256]{1,0:T(8,128)(2,1)S(1)}, u32[]{:S(2)}, u32[]{:S(2)}) %collective-permute-start.8) | collective-permute-done | bytes 73760 | tf_op jit(solution)/shard_map/ppermute | solution.py:42
  93.1 2.1 %collective-permute-done.10.before_ref = bf16[1024,256]{1,0:T(8,128)(2,1)S(1)} collective-permute-done((bf16[1024,256]{1,0:T(8,128)(2,1)S(1)}, bf16[1024,256]{1,0:T(8,128)(2,1)S(1)}, u32[]{:S(2)}, u32[]{:S(2)}) %collective-permute-start.10) | collective-permute-done | bytes 524320 | tf_op jit(solution)/shard_map/ppermute | solution.py:37
  95.2 6.5 %collective-permute-start.11 = (bf16[144,256]{1,0:T(8,128)(2,1)S(1)}, bf16[144,256]{1,0:T(8,128)(2,1)S(1)}, u32[]{:S(2)}, u32[]{:S(2)}) collective-permute-start(bf16[144,256]{1,0:T(8,128)(2,1)S(1)} %convert_add_fusion.2), channel_id=1, source_target_pairs={{0,16},{2,18},{4,20},{6,22},{8,24},{10,26},{12,28},{14,30},{16,0},... | collective-permute-start | bytes 221192 | tf_op jit(solution)/shard_map/ppermute | solution.py:42
  101.8 2.3 %collective-permute-done.11 = bf16[144,256]{1,0:T(8,128)(2,1)S(1)} collective-permute-done((bf16[144,256]{1,0:T(8,128)(2,1)S(1)}, bf16[144,256]{1,0:T(8,128)(2,1)S(1)}, u32[]{:S(2)}, u32[]{:S(2)}) %collective-permute-start.11) | collective-permute-done | bytes 73760 | tf_op jit(solution)/shard_map/ppermute | solution.py:42
  104.2 5.1 %collective-permute-done.12 = f32[144,256]{1,0:T(8,128)S(1)} collective-permute-done((f32[144,256]{1,0:T(8,128)S(1)}, f32[144,256]{1,0:T(8,128)S(1)}, u32[]{:S(2)}, u32[]{:S(2)}) %collective-permute-start.12) | collective-permute-done | bytes 147488 | tf_op jit(solution)/shard_map/ppermute | solution.py:42
  110.5 2.5 %shard_map.135 = bf16[256,1024]{1,0:T(8,128)(2,1)} custom-call(s32[16,128]{1,0:T(8,128)S(1)} %bitcast.17, bf16[16,128,256]{2,1,0:T(8,128)(2,1)S(1)} %all-to-all-done.1.returned_ref, f32[1024,256]{1,0:T(8,128)S(1)} %shard_map.134.own_ref, bf16[1024,256]{1,0:T(8,128)(2,1)S(1)} %copy-done.4, bf16[1024,256]{1,0:T(8,128)(2,1)S(1)} %collective-permute-done.9.after_ref), custom_call_target="tpu_custom_call" | custom-call | flops 1000000000 | bytes 1 | tf_op jit(solution)/shard_map/pallas_call | solution.py:20
  113.0 1.6 %collective-permute-done.13.other_ref = f32[288,256]{1,0:T(8,128)S(1)} collective-permute-done((f32[288,256]{1,0:T(8,128)S(1)}, f32[288,256]{1,0:T(8,128)S(1)}, u32[]{:S(2)}, u32[]{:S(2)}) %collective-permute-start.13) | collective-permute-done | bytes 294944 | tf_op jit(solution)/shard_map/ppermute | solution.py:42
  (60 shorter events, 12.5 us)
Async XLA Ops:
  0.6 13.9 %copy-start.15 = (s32[1,16]{1,0:T(1,128)S(1)}, s32[1,16]{1,0:T(1,128)}, u32[]{:S(2)}) copy-start(s32[1,16]{1,0:T(1,128)} %param.17) | copy-start | bytes 196
  0.7 16.8 %copy-start.2 = (bf16[256,1024]{1,0:T(8,128)(2,1)S(1)}, bf16[256,1024]{1,0:T(8,128)(2,1)}, u32[]{:S(2)}) copy-start(bf16[256,1024]{1,0:T(8,128)(2,1)} %refs_4_) | copy-start | bytes 1572868
  0.7 14.8 %copy-start.11 = (f32[256]{0:T(256)S(1)}, f32[256]{0:T(256)}, u32[]{:S(2)}) copy-start(f32[256]{0:T(256)} %param.18) | copy-start | bytes 3076
  0.7 16.6 %copy-start.7 = (bf16[512,256]{1,0:T(8,128)(2,1)S(1)}, bf16[512,256]{1,0:T(8,128)(2,1)}, u32[]{:S(2)}) copy-start(bf16[512,256]{1,0:T(8,128)(2,1)} %refs_0_) | copy-start | bytes 786436
  1.8 12.8 %collective-permute-start = (bf16[256,1024]{1,0:T(8,128)(2,1)S(1)}, bf16[256,1024]{1,0:T(8,128)(2,1)S(1)}, u32[]{:S(2)}, u32[]{:S(2)}) collective-permute-start(bf16[256,1024]{1,0:T(8,128)(2,1)S(1)} %constant_dynamic-slice_fusion.own_ref), channel_id=1, source_target_pairs={{30,0},{0,2},{2,4},{4,6},{6,8},{8,10},{10,12},{12,14},{14,16},{16,... | collective-permute-start | bytes 1572872 | tf_op jit(solution)/shard_map/ppermute | solution.py:37
  2.3 17.0 %collective-permute-start.1 = (bf16[256,1024]{1,0:T(8,128)(2,1)S(1)}, bf16[256,1024]{1,0:T(8,128)(2,1)}, u32[]{:S(2)}, u32[]{:S(2)}) collective-permute-start(bf16[256,1024]{1,0:T(8,128)(2,1)S(1)} %constant_dynamic-slice_fusion.own_ref), channel_id=1, source_target_pairs={{2,0},{4,2},{6,4},{8,6},{10,8},{12,10},{14,12},{16,14},{18,16},{20... | collective-permute-start | bytes 1572872 | tf_op jit(solution)/shard_map/ppermute | solution.py:37
  10.8 26.6 %all-to-all-start = ((bf16[16,128,256]{2,1,0:T(8,128)(2,1)}), bf16[16,128,256]{2,1,0:T(8,128)(2,1)S(1)}, u32[]{:S(2)}, u32[]{:S(2)}) async-start(bf16[16,128,256]{2,1,0:T(8,128)(2,1)} %shard_map.130), calls=%async_computation | async-start | bytes 2097152 | tf_op jit(solution)/shard_map/all_to_all | solution.py:300
  14.4 22.9 %copy-start.9 = (f32[1,16,128]{2,1,0:T(8,128)S(1)}, f32[1,16,128]{2,1,0:T(8,128)}, u32[]{:S(2)}) copy-start(f32[1,16,128]{2,1,0:T(8,128)} %param.16) | copy-start | bytes 24580
  14.6 22.8 %copy-start.8 = (s32[1,16,128]{2,1,0:T(8,128)S(1)}, s32[1,16,128]{2,1,0:T(8,128)}, u32[]{:S(2)}) copy-start(s32[1,16,128]{2,1,0:T(8,128)} %param.15) | copy-start | bytes 24580
  15.4 11.7 %collective-permute-start.3 = (f32[256]{0:T(256)S(1)}, f32[256]{0:T(256)S(1)}, u32[]{:S(2)}, u32[]{:S(2)}) collective-permute-start(f32[256]{0:T(256)S(1)} %copy-done.11), channel_id=1, source_target_pairs={{1,0},{0,1},{3,2},{2,3},{5,4},{4,5},{7,6},{6,7},{9,8},{8,9},{11,10... | collective-permute-start | bytes 3080 | tf_op jit(solution)/shard_map/ppermute | solution.py:37
  17.3 9.8 %collective-permute-start.2 = (bf16[512,256]{1,0:T(8,128)(2,1)S(1)}, bf16[512,256]{1,0:T(8,128)(2,1)S(1)}, u32[]{:S(2)}, u32[]{:S(2)}) collective-permute-start(bf16[512,256]{1,0:T(8,128)(2,1)S(1)} %copy-done.7), channel_id=1, source_target_pairs={{1,0},{0,1},{3,2},{2,3},{5,4},{4,5},{7,6},{6,7},{9,8},{8,9},{11,10... | collective-permute-start | bytes 786440 | tf_op jit(solution)/shard_map/ppermute | solution.py:37
  17.5 19.3 %collective-permute-start.4 = (bf16[256,1024]{1,0:T(8,128)(2,1)S(1)}, bf16[256,1024]{1,0:T(8,128)(2,1)S(1)}, u32[]{:S(2)}, u32[]{:S(2)}) collective-permute-start(bf16[256,1024]{1,0:T(8,128)(2,1)S(1)} %copy-done.2), channel_id=1, source_target_pairs={{1,0},{0,1},{3,2},{2,3},{5,4},{4,5},{7,6},{6,7},{9,8},{8,9},{11,10... | collective-permute-start | bytes 1572872 | tf_op jit(solution)/shard_map/ppermute | solution.py:37
  40.1 14.6 %collective-permute-start.5 = (bf16[1024,256]{1,0:T(8,128)(2,1)S(1)}, bf16[1024,256]{1,0:T(8,128)(2,1)S(1)}, u32[]{:S(2)}, u32[]{:S(2)}) collective-permute-start(bf16[1024,256]{1,0:T(8,128)(2,1)S(1)} %shard_map.131), channel_id=1, source_target_pairs={{1,0},{0,1},{3,2},{2,3},{5,4},{4,5},{7,6},{6,7},{9,8},{8,9},{11,10... | collective-permute-start | bytes 1572872 | tf_op jit(solution)/shard_map/ppermute | solution.py:37
  59.2 11.5 %collective-permute-start.6 = (bf16[288,256]{1,0:T(8,128)(2,1)S(1)}, bf16[288,256]{1,0:T(8,128)(2,1)S(1)}, u32[]{:S(2)}, u32[]{:S(2)}) collective-permute-start(bf16[288,256]{1,0:T(8,128)(2,1)S(1)} %select_convert_fusion), channel_id=1, source_target_pairs={{0,2},{2,0},{4,6},{6,4},{8,10},{10,8},{12,14},{14,12},{16,18},{18,... | collective-permute-start | bytes 442376 | tf_op jit(solution)/shard_map/ppermute | solution.py:42
  59.3 50.1 %all-to-all-start.1 = ((bf16[16,128,256]{2,1,0:T(8,128)(2,1)}), bf16[16,128,256]{2,1,0:T(8,128)(2,1)S(1)}, u32[]{:S(2)}, u32[]{:S(2)}) async-start(bf16[16,128,256]{2,1,0:T(8,128)(2,1)} %get-tuple-element.52), calls=%async_computation.1 | async-start | bytes 2097152 | tf_op jit(solution)/shard_map/all_to_all | solution.py:344
  70.7 38.7 %copy-start.10 = (s32[1,16,128]{2,1,0:T(8,128)S(1)}, s32[1,16,128]{2,1,0:T(8,128)}, u32[]{:S(2)}) copy-start(s32[1,16,128]{2,1,0:T(8,128)} %param.14) | copy-start | bytes 24580
  70.8 6.5 %collective-permute-start.7 = (bf16[144,256]{1,0:T(8,128)(2,1)S(1)}, bf16[144,256]{1,0:T(8,128)(2,1)S(1)}, u32[]{:S(2)}, u32[]{:S(2)}) collective-permute-start(bf16[144,256]{1,0:T(8,128)(2,1)S(1)} %select_convert_fusion.1), channel_id=1, source_target_pairs={{0,4},{2,6},{4,0},{6,2},{8,12},{10,14},{12,8},{14,10},{16,20},{18,... | collective-permute-start | bytes 221192 | tf_op jit(solution)/shard_map/ppermute | solution.py:42
  72.8 20.4 %collective-permute-start.9 = (bf16[1024,256]{1,0:T(8,128)(2,1)S(1)}, bf16[1024,256]{1,0:T(8,128)(2,1)S(1)}, u32[]{:S(2)}, u32[]{:S(2)}) collective-permute-start(bf16[1024,256]{1,0:T(8,128)(2,1)S(1)} %get-tuple-element.49), channel_id=1, source_target_pairs={{2,0},{4,2},{6,4},{8,6},{10,8},{12,10},{14,12},{16,14},{18,16},{20... | collective-permute-start | bytes 1572872 | tf_op jit(solution)/shard_map/ppermute | solution.py:37
  75.5 19.7 %collective-permute-start.10 = (bf16[1024,256]{1,0:T(8,128)(2,1)S(1)}, bf16[1024,256]{1,0:T(8,128)(2,1)S(1)}, u32[]{:S(2)}, u32[]{:S(2)}) collective-permute-start(bf16[1024,256]{1,0:T(8,128)(2,1)S(1)} %get-tuple-element.50), channel_id=1, source_target_pairs={{30,0},{0,2},{2,4},{4,6},{6,8},{8,10},{10,12},{12,14},{14,16},{16,... | collective-permute-start | bytes 1572872 | tf_op jit(solution)/shard_map/ppermute | solution.py:37
  77.3 15.8 %collective-permute-start.8 = (bf16[144,256]{1,0:T(8,128)(2,1)S(1)}, bf16[144,256]{1,0:T(8,128)(2,1)S(1)}, u32[]{:S(2)}, u32[]{:S(2)}) collective-permute-start(bf16[144,256]{1,0:T(8,128)(2,1)S(1)} %add_convert_fusion), channel_id=1, source_target_pairs={{0,8},{2,10},{4,12},{6,14},{8,0},{10,2},{12,4},{14,6},{16,24},{18,... | collective-permute-start | bytes 221192 | tf_op jit(solution)/shard_map/ppermute | solution.py:42
  95.2 14.1 %copy-start.3 = (bf16[1024,256]{1,0:T(8,128)(2,1)}, bf16[1024,256]{1,0:T(8,128)(2,1)S(1)}, u32[]{:S(2)}) copy-start(bf16[1024,256]{1,0:T(8,128)(2,1)S(1)} %collective-permute-done.10.before_ref) | copy-start | bytes 1572868
  95.2 8.9 %collective-permute-start.11 = (bf16[144,256]{1,0:T(8,128)(2,1)S(1)}, bf16[144,256]{1,0:T(8,128)(2,1)S(1)}, u32[]{:S(2)}, u32[]{:S(2)}) collective-permute-start(bf16[144,256]{1,0:T(8,128)(2,1)S(1)} %convert_add_fusion.2), channel_id=1, source_target_pairs={{0,16},{2,18},{4,20},{6,22},{8,24},{10,26},{12,28},{14,30},{16,0},... | collective-permute-start | bytes 221192 | tf_op jit(solution)/shard_map/ppermute | solution.py:42
  104.1 5.2 %collective-permute-start.12 = (f32[144,256]{1,0:T(8,128)S(1)}, f32[144,256]{1,0:T(8,128)S(1)}, u32[]{:S(2)}, u32[]{:S(2)}) collective-permute-start(f32[144,256]{1,0:T(8,128)S(1)} %convert_add_fusion.1), channel_id=1, source_target_pairs={{0,4},{2,6},{4,0},{6,2},{8,12},{10,14},{12,8},{14,10},{16,20},{18,... | collective-permute-start | bytes 442376 | tf_op jit(solution)/shard_map/ppermute | solution.py:42
  113.0 1.6 %collective-permute-start.13 = (f32[288,256]{1,0:T(8,128)S(1)}, f32[288,256]{1,0:T(8,128)S(1)}, u32[]{:S(2)}, u32[]{:S(2)}) collective-permute-start(f32[288,256]{1,0:T(8,128)S(1)} %pad_maximum_fusion.1.mine_ref), channel_id=1, source_target_pairs={{0,2},{2,0},{4,6},{6,4},{8,10},{10,8},{12,14},{14,12},{16,18},{18,... | collective-permute-start | bytes 884744 | tf_op jit(solution)/shard_map/ppermute | solution.py:42
  (8 other events, 24.5 us)

commit v3 on v2

--- a/solution.py
+++ b/solution.py
@@ -46,23 +46,21 @@
     return jnp.dot(a, b, preferred_element_type=F32)
 
 
-def slots_by_nodes(hot, rows_t, nodes, first, count, weights_t=None):
+def slots_by_nodes(hot, rows_t, nodes, first, count):
     slots = rows_t.shape[0]
     lanes = lax.broadcasted_iota(jnp.int32, (slots, nodes), 1)
     for p in range(first, first + count):
-        value = 1.0 if weights_t is None else weights_t[:, p : p + 1]
         hot[p * slots : (p + 1) * slots, :] = jnp.where(
-            rows_t[:, p : p + 1] == lanes, value, 0.0
+            rows_t[:, p : p + 1] == lanes, 1.0, 0.0
         ).astype(BF16)
 
 
-def nodes_by_slots(hot, rows, nodes, weights=None):
+def nodes_by_slots(hot, rows, nodes):
     peers, slots = rows.shape
     lines = lax.broadcasted_iota(jnp.int32, (nodes, slots), 0)
     for p in range(peers):
-        value = 1.0 if weights is None else weights[p : p + 1, :]
         hot[:, p * slots : (p + 1) * slots] = jnp.where(
-            rows[p : p + 1, :] == lines, value, 0.0
+            rows[p : p + 1, :] == lines, 1.0, 0.0
         ).astype(BF16)
 
 
@@ -140,11 +138,14 @@
         out_ref[i * TILE : (i + 1) * TILE, :] = total.T
 
 
-def aggregate_kernel(recv_ref, weight_ref, counts_ref, arrived_ref, dense_ref, out_ref, hot):
-    peers, slots, rows = arrived_ref.shape
-    nodes_by_slots(hot, recv_ref[...], out_ref.shape[0], masked_weights(weight_ref[...], counts_ref[...]))
-    arrived = arrived_ref[...].reshape(peers * slots, rows)
-    out_ref[...] = (dense_ref[...] + dot(hot[...], arrived)).astype(BF16)
+def aggregate_kernel(recv_ref, weight_ref, counts_ref, arrived_ref, out_ref, hot, weighted):
+    peers, slots, _ = arrived_ref.shape
+    nodes_by_slots(hot, recv_ref[...], out_ref.shape[0])
+    weights_t = masked_weights(weight_ref[...], counts_ref[...]).T
+    for p in range(peers):
+        row = arrived_ref[p].astype(F32) * weights_t[:, p : p + 1]
+        weighted[p * slots : (p + 1) * slots, :] = row.astype(BF16)
+    out_ref[...] = dot(hot[...], weighted[...])
 
 
 def dense_backward(live_ref, tiles, block, s, first):
@@ -179,9 +180,11 @@
 def layer_kernel(n_hid, hid_ref, *refs):
     take = iter(refs)
     weights, biases, cotangents = ([next(take) for _ in range(n_hid)] for _ in range(3))
-    aggs, recv_ref, weight_ref, counts_ref, output_ref, part_ref, back_ref, message_ref, hot = take
-    peers, slots, rows = message_ref.shape
+    aggs, output_ref, part_ref, back_ref, held, sems = take
+    copies = Copies(sems)
+    cotangents_in = [copies.start(ref, held.at[k]) for k, ref in enumerate(cotangents)]
     width, nodes = output_ref.shape
+    rows = back_ref.shape[1]
     own = pl.ds(pl.multiple_of(hid_ref[0] * rows, rows), rows)
     total = None
     for k in range(n_hid):
@@ -191,7 +194,8 @@
             act = act + dot(aggs[j], weights[k][pl.ds(start, rows), :])
         gate = 1.0 / (1.0 + jnp.exp(-act))
         slope = gate * (1.0 + act * (1.0 - gate))
-        grad = (cotangents[k][...].T.astype(F32) * slope).astype(BF16)
+        cotangents_in[k].wait()
+        grad = (held[k].T.astype(F32) * slope).astype(BF16)
         if k == 0:
             output_ref[...] = (act * gate).astype(BF16).T
             weight_parts(hid_ref, grad, aggs, part_ref)
@@ -199,15 +203,22 @@
             grad, weights[k][own, :], (((1,), (1,)), ((), ())), preferred_element_type=F32
         )
         total = term if total is None else total + term
-    back = total.astype(BF16)
-    back_ref[...] = back
+    back_ref[...] = total.astype(BF16)
+
+
+def message_kernel(recv_ref, weight_ref, counts_ref, back_ref, message_ref, hot):
+    peers, slots, _ = message_ref.shape
+    back = back_ref[...]
+    nodes = back.shape[0]
     weights_t = masked_weights(weight_ref[...], counts_ref[...]).T
     recv_t = recv_ref[...].T
     group = 4
     for p in range(0, peers, group):
-        slots_by_nodes(hot, recv_t, nodes, p, group, weights_t)
+        slots_by_nodes(hot, recv_t, nodes, p, group)
         picked = dot(hot[p * slots : (p + group) * slots, :], back)
-        message_ref[p : p + group] = picked.astype(BF16).reshape(group, slots, rows)
+        for n in range(group):
+            row = picked[n * slots : (n + 1) * slots] * weights_t[:, p + n : p + n + 1]
+            message_ref[p + n] = row.astype(BF16)
 
 
 def joined_kernel(odd_ref, mine_ref, other_ref, weight_ref, bias_ref):
@@ -221,12 +232,11 @@
     bias_ref[...] = high[size - half : size - half + 1, :]
 
 
-def scatter_kernel(send_ref, returned_ref, own_ref, before_ref, after_ref, out_ref, hot):
+def scatter_kernel(send_ref, returned_ref, dense_ref, out_ref, hot):
     peers, slots, rows = returned_ref.shape
-    nodes_by_slots(hot, send_ref[...], own_ref.shape[0])
+    nodes_by_slots(hot, send_ref[...], dense_ref.shape[0])
     returned = returned_ref[...].reshape(peers * slots, rows)
-    total = own_ref[...] + before_ref[...].astype(F32) + after_ref[...].astype(F32)
-    total = total + dot(hot[...], returned)
+    total = dense_ref[...] + dot(hot[...], returned)
     out_ref[...] = total.astype(BF16).T
 
 
@@ -241,20 +251,21 @@
     return part
 
 
-def doubled(part, axis, bits):
+def sum_kernel(mine_ref, other_ref, out_ref):
+    out_ref[...] = mine_ref[...].astype(F32) + other_ref[...].astype(F32)
+
+
+def doubled(part, axis, bits, us=1):
     for bit in bits:
         sent = part.astype(BF16)
-        part = sent.astype(F32) + swapped(sent, axis, bit).astype(F32)
+        (part,) = call(
+            sum_kernel, [out(part.shape, F32)], [(VMEM, sent), (VMEM, swapped(sent, axis, bit))], us=us
+        )
     return part
 
 
-def joined(part, axis, bits):
-    place = lax.axis_index(axis)
-    for bit in reversed(bits):
-        odd = lax.rem(place // bit, 2) == 1
-        other = swapped(part, axis, bit)
-        part = jnp.concatenate([jnp.where(odd, other, part), jnp.where(odd, part, other)])
-    return part
+def paired(mine, other, odd):
+    return jnp.where(odd == 1, jnp.concatenate([other, mine]), jnp.concatenate([mine, other]))
 
 
 def on_device(
@@ -312,35 +323,43 @@
         us=60,
     )
     dense, weights, biases, cotangents = lax.optimization_barrier((dense, weights, biases, cotangents))
-    (agg,) = call(
+    (sparse,) = call(
         aggregate_kernel,
-        [out((nodes, rows), BF16)],
-        [*edges, (VMEM, arrived), (VMEM, dense)],
-        [vmem((nodes, lists), BF16)],
+        [out((nodes, rows), F32)],
+        [*edges, (VMEM, arrived)],
+        [vmem((nodes, lists), BF16), vmem((lists, rows), BF16)],
         us=4,
     )
+    agg = (dense + sparse).astype(BF16)
     aggs = jnp.stack([agg] + [shifted(agg, "hid", k) for k in steps])
+    bits = [1 << b for b in range((peers - 1).bit_length())]
     pad = 64
-    output, part, back, message = call(
+    output, part, back = call(
         functools.partial(layer_kernel, n_hid),
         [
             out((width, nodes), BF16),
             out((n_hid * rows + pad, width), F32),
             out((nodes, rows), BF16),
-            out((peers, slots, rows), BF16),
         ],
         [
             hid,
             *[(VMEM, w) for w in weights],
             *[(VMEM, b[None, :]) for b in biases],
-            *[(VMEM, c) for c in cotangents],
+            *[(HBM, c) for c in cotangents],
             (VMEM, aggs),
-            *edges,
         ],
+        [vmem((n_hid, width, nodes), BF16), sems(n_hid)],
+        us=2,
+    )
+    (message,) = call(
+        message_kernel,
+        [out((peers, slots, rows), BF16)],
+        [*edges, (VMEM, back)],
         [vmem((lists, nodes), BF16)],
-        us=6,
-        mib=24,
-    )
+        us=2,
+    )
+    part = halved(part, "dom", bits[:1])
+    message, part, back = lax.optimization_barrier((message, part, back))
     returned = lax.all_to_all(message, "dom", split_axis=0, concat_axis=0, tiled=True)
 
     to_before, to_after = call(
@@ -353,27 +372,28 @@
         [out((nodes, rows), F32)],
         [*tiles, (VMEM, back)],
     )
-    bits = [1 << b for b in range((peers - 1).bit_length())]
-    part = halved(part, "dom", bits[:1])
+    part = halved(part, "dom", bits[1:2])
     part, to_before, to_after = lax.optimization_barrier((part, to_before, to_after))
     from_after, from_before = shifted(to_before, "dom", 1), shifted(to_after, "dom", -1)
-    part = halved(part, "dom", bits[1:2])
-    part = doubled(part, "dom", bits[2:3])
-    part, from_after, from_before, kept = lax.optimization_barrier((part, from_after, from_before, kept))
+    part = doubled(part, "dom", bits[2:3], 5)
+    part, kept = lax.optimization_barrier((part, kept))
     part = doubled(part, "dom", bits[3:])
+    base = kept + from_after.astype(F32) + from_before.astype(F32)
     (feature_grad,) = call(
         scatter_kernel,
         [out((rows, nodes), BF16)],
-        [send, (VMEM, returned), (VMEM, kept), (VMEM, from_before), (VMEM, from_after)],
+        [send, (VMEM, returned), (VMEM, base)],
         [vmem((nodes, lists), BF16)],
     )
-    part = joined(part, "dom", bits[1:2])
-    part, feature_grad = lax.optimization_barrier((part, feature_grad))
-    odd = lax.rem(lax.axis_index("dom"), 2).astype(jnp.int32).reshape(1)
+    place = lax.axis_index("dom")
+    far = swapped(part, "dom", 2)
+    far, feature_grad = lax.optimization_barrier((far, feature_grad))
+    part = paired(part, far, place // 2 % 2)
+    other = swapped(part, "dom", 1)
     weight_grad, bias_grad = call(
         joined_kernel,
         [out((n_hid * rows, width), F32), out((1, width), F32)],
-        [(SMEM, odd), (VMEM, part), (VMEM, swapped(part, "dom", 1))],
+        [(SMEM, (place % 2).astype(jnp.int32).reshape(1)), (VMEM, part), (VMEM, other)],
     )
     return (output, feature_grad, weight_grad, bias_grad[0])
 

time: 116 us -> 110 us (0.948)
  waiting for transfers between devices: 49.6 us -> 43.4 us
  starting transfers between devices: 33.7 us -> 31.4 us
  Pallas kernels: 18.9 us -> 20.4 us
  other arithmetic: 0.32 us -> 1.82 us
    ppermute x8, waiting for transfers between devices: 24.4 us -> 19.3 us  [shifted(): lax.ppermute(block, axis, [((i + distance) % size, i) for i in range(size)])]
    ppermute x6, waiting for transfers between devices: 24.6 us -> 21.8 us  [swapped(): return lax.ppermute(block, axis, [(i, i ^ bit) for i in range(size)])]
    all_to_all x1, waiting for transfers between devices: 0.53 us -> 2.3 us  [on_device(): lax.all_to_all(outgoing, 'dom', split_axis=0, concat_axis=0, tiled=True)]
    pallas_call x8 -> x11, Pallas kernels: 18.9 us -> 20.4 us  [call(): pl.pallas_call(kernel, out_shape=tuple(outs), in_specs=[place for place,...]
    add x2 -> x1, other arithmetic: 0.04 us -> 1.34 us  [on_device(): base = kept + from_after.astype(F32) + from_before.astype(F32)]
    unnamed x33 -> x31, local copies, waits for them, and re-layouts: 10.8 us -> 10.2 us
  transfers between devices with their start and end apart: 16 -> 16, of which waited for: 9 -> 8; matrix products, arithmetic and copies ran while one was open for 0% -> 1% of each run, Pallas kernels for 8% -> 14%
where the time goes in v3:
time: 110 us; the launch traced here: 109 us
  waiting for transfers between devices  43.4 us (39%)
  starting transfers between devices  31.4 us (29%)
  Pallas kernels  20.4 us (19%)
  local copies, waits for them, and re-layouts  11.4 us (10%)
  other arithmetic  1.82 us (2%)
    ppermute x6, waiting for transfers between devices, swapped(): return lax.ppermute(block, axis, [(i, i ^ bit) for i in range(size)])  21.8 us
    pallas_call x11, Pallas kernels, call(): pl.pallas_call(kernel, out_shape=tuple(outs), in_specs=[place for place,...  20.4 us
    ppermute x8, waiting for transfers between devices, shifted(): lax.ppermute(block, axis, [((i + distance) % size, i) for i in range(size)])  19.3 us
    ppermute x8, starting transfers between devices, shifted(): lax.ppermute(block, axis, [((i + distance) % size, i) for i in range(size)])  13 us
    unnamed x31, local copies, waits for them, and re-layouts  10.2 us
    ppermute x6, starting transfers between devices, swapped(): return lax.ppermute(block, axis, [(i, i ^ bit) for i in range(size)])  8.14 us
    all_to_all x1, starting transfers between devices, on_device(): lax.all_to_all(message, 'dom', split_axis=0, concat_axis=0, tiled=True)  6.64 us
    all_to_all x1, starting transfers between devices, on_device(): lax.all_to_all(outgoing, 'dom', split_axis=0, concat_axis=0, tiled=True)  3.66 us
  transfers between devices with their start and end apart: 16, of which 8 were waited for; matrix products, arithmetic and copies ran while one was open for 1% of the time, Pallas kernels for 14%

profile of v3, /device:TPU:0, one launch (start us, length us, event | category | flops | bytes accessed | tf_op | source)
XLA Modules:
  0.0 109.4 jit_solution(9670276678531884731)
XLA Ops:
  2.3 5.1 %collective-permute-start.1 = (bf16[256,1024]{1,0:T(8,128)(2,1)S(1)}, bf16[256,1024]{1,0:T(8,128)(2,1)S(1)}, u32[]{:S(2)}, u32[]{:S(2)}) collective-permute-start(bf16[256,1024]{1,0:T(8,128)(2,1)S(1)} %constant_dynamic-slice_fusion.own_ref), channel_id=1, source_target_pairs={{2,0},{4,2},{6,4},{8,6},{10,8},{12,10},{14,12},{16,14},{18,16},{20... | collective-permute-start | bytes 1572872 | tf_op jit(solution)/shard_map/ppermute | solution.py:37
  7.4 3.3 %shard_map.130 = bf16[16,128,256]{2,1,0:T(8,128)(2,1)} custom-call(s32[1]{0:T(128)} %bitcast.hid_ref, bf16[512,1024]{1,0:T(8,128)(2,1)} %features_ref.1, s32[16,128]{1,0:T(8,128)} %bitcast.15), custom_call_target="tpu_custom_call" | custom-call | flops 1000000000 | bytes 1 | tf_op jit(solution)/shard_map/pallas_call | solution.py:20
  10.7 3.7 %all-to-all-start = ((bf16[16,128,256]{2,1,0:T(8,128)(2,1)}), bf16[16,128,256]{2,1,0:T(8,128)(2,1)S(1)}, u32[]{:S(2)}, u32[]{:S(2)}) async-start(bf16[16,128,256]{2,1,0:T(8,128)(2,1)} %shard_map.130), calls=%async_computation | async-start | bytes 2097152 | tf_op jit(solution)/shard_map/all_to_all | solution.py:311
  15.4 1.9 %collective-permute-start.4 = (bf16[256,1024]{1,0:T(8,128)(2,1)}, bf16[256,1024]{1,0:T(8,128)(2,1)S(1)}, u32[]{:S(2)}, u32[]{:S(2)}) collective-permute-start(bf16[256,1024]{1,0:T(8,128)(2,1)} %refs_4_), channel_id=1, source_target_pairs={{1,0},{0,1},{3,2},{2,3},{5,4},{4,5},{7,6},{6,7},{9,8},{8,9},{11,10... | collective-permute-start | bytes 1572872 | tf_op jit(solution)/shard_map/ppermute | solution.py:37
  17.4 1.9 %collective-permute-start.3 = (f32[256]{0:T(256)S(1)}, f32[256]{0:T(256)S(1)}, u32[]{:S(2)}, u32[]{:S(2)}) collective-permute-start(f32[256]{0:T(256)S(1)} %copy-done.12), channel_id=1, source_target_pairs={{1,0},{0,1},{3,2},{2,3},{5,4},{4,5},{7,6},{6,7},{9,8},{8,9},{11,10... | collective-permute-start | bytes 3080 | tf_op jit(solution)/shard_map/ppermute | solution.py:37
  20.1 2.8 %copy-done = bf16[3072,1024]{1,0:T(8,128)(2,1)S(1)} copy-done((bf16[3072,1024]{1,0:T(8,128)(2,1)S(1)}, bf16[3072,1024]{1,0:T(8,128)(2,1)}, u32[]{:S(2)}) %copy-start) | copy-done | bytes 6291480
  25.0 2.6 %shard_map.129 = f32[1024,256]{1,0:T(8,128)S(1)} custom-call(s32[12,4]{1,0:T(8,128)S(1)} %copy.14.live_ref, bf16[3072,1024]{1,0:T(8,128)(2,1)S(1)} %copy-done, bf16[256,1024]{1,0:T(8,128)(2,1)S(1)} %copy-done.5, bf16[256,1024]{1,0:T(8,128)(2,1)S(1)} %constant_dynamic-slice_fusion.own_ref, bf16[256,1024]{1,0:T(8,128)(2,1)S(1)} %copy-done.7), custom_call_target="tpu_custom_call" | custom-call | flops 60000002048 | bytes 1 | tf_op jit(solution)/shard_map/pallas_call | solution.py:20
  27.6 6.6 %collective-permute-done.3 = f32[256]{0:T(256)S(1)} collective-permute-done((f32[256]{0:T(256)S(1)}, f32[256]{0:T(256)S(1)}, u32[]{:S(2)}, u32[]{:S(2)}) %collective-permute-start.3) | collective-permute-done | bytes 1056 | tf_op jit(solution)/shard_map/ppermute | solution.py:37
  35.0 2.3 %all-to-all-done.arrived_ref = bf16[16,128,256]{2,1,0:T(8,128)(2,1)S(1)} async-done(((bf16[16,128,256]{2,1,0:T(8,128)(2,1)}), bf16[16,128,256]{2,1,0:T(8,128)(2,1)S(1)}, u32[]{:S(2)}, u32[]{:S(2)}) %all-to-all-start) | async-done | bytes 1048608 | tf_op jit(solution)/shard_map/all_to_all | solution.py:311
  37.3 1.9 %shard_map.131 = f32[1024,256]{1,0:T(8,128)S(1)} custom-call(s32[16,128]{1,0:T(8,128)S(1)} %bitcast.11, f32[16,128]{1,0:T(8,128)S(1)} %bitcast.13, s32[16,1]{1,0:T(8,128)S(1)} %copy.15.counts_ref, bf16[16,128,256]{2,1,0:T(8,128)(2,1)S(1)} %all-to-all-done.arrived_ref), custom_call_target="tpu_custom_call" | custom-call | flops 4000000000 | bytes 1 | tf_op jit(solution)/shard_map/pallas_call | solution.py:20
  39.5 1.9 %collective-permute-start.5 = (bf16[1024,256]{1,0:T(8,128)(2,1)S(1)}, bf16[1024,256]{1,0:T(8,128)(2,1)S(1)}, u32[]{:S(2)}, u32[]{:S(2)}) collective-permute-start(bf16[1024,256]{1,0:T(8,128)(2,1)S(1)} %add_convert_fusion), channel_id=1, source_target_pairs={{1,0},{0,1},{3,2},{2,3},{5,4},{4,5},{7,6},{6,7},{9,8},{8,9},{11,10... | collective-permute-start | bytes 1572872 | tf_op jit(solution)/shard_map/ppermute | solution.py:37
  41.4 12.7 %collective-permute-done.5 = bf16[1024,256]{1,0:T(8,128)(2,1)S(1)} collective-permute-done((bf16[1024,256]{1,0:T(8,128)(2,1)S(1)}, bf16[1024,256]{1,0:T(8,128)(2,1)S(1)}, u32[]{:S(2)}, u32[]{:S(2)}) %collective-permute-start.5) | collective-permute-done | bytes 524320 | tf_op jit(solution)/shard_map/ppermute | solution.py:37
  54.2 2.8 %shard_map.132 = (bf16[256,1024]{1,0:T(8,128)(2,1)}, f32[576,256]{1,0:T(8,128)S(1)}, bf16[1024,256]{1,0:T(8,128)(2,1)S(1)}) custom-call(s32[1]{0:T(128)} %bitcast.hid_ref, bf16[512,256]{1,0:T(8,128)(2,1)S(1)} %copy-done.8, bf16[512,256]{1,0:T(8,128)(2,1)S(1)} %collective-permute-done.2.refs_1_, f32[1,256]{1,0:T(1,128)S(1)} %bitcast.17, ...), custom_call_target="tpu_custom_call" | custom-call | flops 2000000000 | bytes 1 | tf_op jit(solution)/shard_map/pallas_call | solution.py:20
  57.1 2.4 %shard_map.133 = bf16[16,128,256]{2,1,0:T(8,128)(2,1)} custom-call(s32[16,128]{1,0:T(8,128)S(1)} %bitcast.12, f32[16,128]{1,0:T(8,128)S(1)} %bitcast.14, s32[16,1]{1,0:T(8,128)S(1)} %copy.15.counts_ref, bf16[1024,256]{1,0:T(8,128)(2,1)S(1)} %get-tuple-element.47.back_ref), custom_call_target="tpu_custom_call" | custom-call | flops 2000000000 | bytes 1 | tf_op jit(solution)/shard_map/pallas_call | solution.py:20
  59.6 6.6 %all-to-all-start.1 = ((bf16[16,128,256]{2,1,0:T(8,128)(2,1)}), bf16[16,128,256]{2,1,0:T(8,128)(2,1)S(1)}, u32[]{:S(2)}, u32[]{:S(2)}) async-start(bf16[16,128,256]{2,1,0:T(8,128)(2,1)} %shard_map.133), calls=%async_computation.1 | async-start | bytes 2097152 | tf_op jit(solution)/shard_map/all_to_all | solution.py:363
  66.3 2.0 %collective-permute-start.7 = (bf16[144,256]{1,0:T(8,128)(2,1)S(1)}, bf16[144,256]{1,0:T(8,128)(2,1)S(1)}, u32[]{:S(2)}, u32[]{:S(2)}) collective-permute-start(bf16[144,256]{1,0:T(8,128)(2,1)S(1)} %select_convert_fusion.1), channel_id=1, source_target_pairs={{0,4},{2,6},{4,0},{6,2},{8,12},{10,14},{12,8},{14,10},{16,20},{18,... | collective-permute-start | bytes 221192 | tf_op jit(solution)/shard_map/ppermute | solution.py:42
  68.3 2.8 %copy-done.1 = bf16[3072,1024]{1,0:T(8,128)(2,1)S(1)} copy-done((bf16[3072,1024]{1,0:T(8,128)(2,1)S(1)}, bf16[3072,1024]{1,0:T(8,128)(2,1)}, u32[]{:S(2)}) %copy-start.1) | copy-done | bytes 6291480
  71.1 2.8 %shard_map.134 = (bf16[1024,256]{1,0:T(8,128)(2,1)}, bf16[1024,256]{1,0:T(8,128)(2,1)}) custom-call(s32[12,4]{1,0:T(8,128)S(1)} %copy.14.live_ref, bf16[3072,1024]{1,0:T(8,128)(2,1)S(1)} %copy-done.1, bf16[1024,256]{1,0:T(8,128)(2,1)S(1)} %get-tuple-element.47.back_ref), custom_call_target="tpu_custom_call" | custom-call | flops 1000000000 | bytes 1 | tf_op jit(solution)/shard_map/pallas_call | solution.py:20
  73.8 3.8 %collective-permute-done.7 = bf16[144,256]{1,0:T(8,128)(2,1)S(1)} collective-permute-done((bf16[144,256]{1,0:T(8,128)(2,1)S(1)}, bf16[144,256]{1,0:T(8,128)(2,1)S(1)}, u32[]{:S(2)}, u32[]{:S(2)}) %collective-permute-start.7) | collective-permute-done | bytes 73760 | tf_op jit(solution)/shard_map/ppermute | solution.py:42
  79.1 1.6 %collective-permute-start.11 = (bf16[1024,256]{1,0:T(8,128)(2,1)}, bf16[1024,256]{1,0:T(8,128)(2,1)}, u32[]{:S(2)}, u32[]{:S(2)}) collective-permute-start(bf16[1024,256]{1,0:T(8,128)(2,1)} %get-tuple-element.54), channel_id=1, source_target_pairs={{2,0},{4,2},{6,4},{8,6},{10,8},{12,10},{14,12},{16,14},{18,16},{20... | collective-permute-start | bytes 1572872 | tf_op jit(solution)/shard_map/ppermute | solution.py:37
  80.7 5.3 %collective-permute-done.8.other_ref = bf16[144,256]{1,0:T(8,128)(2,1)S(1)} collective-permute-done((bf16[144,256]{1,0:T(8,128)(2,1)S(1)}, bf16[144,256]{1,0:T(8,128)(2,1)S(1)}, u32[]{:S(2)}, u32[]{:S(2)}) %collective-permute-start.8) | collective-permute-done | bytes 73760 | tf_op jit(solution)/shard_map/ppermute | solution.py:42
  86.0 4.5 %collective-permute-start.9 = (bf16[144,256]{1,0:T(8,128)(2,1)S(1)}, bf16[144,256]{1,0:T(8,128)(2,1)S(1)}, u32[]{:S(2)}, u32[]{:S(2)}) collective-permute-start(bf16[144,256]{1,0:T(8,128)(2,1)S(1)} %convert_element_type.33.mine_ref), channel_id=1, source_target_pairs={{0,16},{2,18},{4,20},{6,22},{8,24},{10,26},{12,28},{14,30},{16,0},... | collective-permute-start | bytes 221192 | tf_op jit(solution)/shard_map/ppermute | solution.py:42
  90.4 11.2 %collective-permute-done.9.other_ref = bf16[144,256]{1,0:T(8,128)(2,1)S(1)} collective-permute-done((bf16[144,256]{1,0:T(8,128)(2,1)S(1)}, bf16[144,256]{1,0:T(8,128)(2,1)S(1)}, u32[]{:S(2)}, u32[]{:S(2)}) %collective-permute-start.9) | collective-permute-done | bytes 73760 | tf_op jit(solution)/shard_map/ppermute | solution.py:42
  104.5 2.3 %shard_map.138 = bf16[256,1024]{1,0:T(8,128)(2,1)} custom-call(s32[16,128]{1,0:T(8,128)S(1)} %bitcast.16, bf16[16,128,256]{2,1,0:T(8,128)(2,1)S(1)} %all-to-all-done.1.returned_ref, f32[1024,256]{1,0:T(8,128)S(1)} %convert_add_fusion.dense_ref), custom_call_target="tpu_custom_call" | custom-call | flops 1000000000 | bytes 1 | tf_op jit(solution)/shard_map/pallas_call | solution.py:20
  (61 shorter events, 13.9 us)
Async XLA Ops:
  0.6 13.8 %copy-start.13 = (s32[12,4]{0,1:T(4,128)S(1)}, s32[12,4]{0,1:T(4,128)}, u32[]{:S(2)}) copy-start(s32[12,4]{0,1:T(4,128)} %param.13) | copy-start | bytes 580
  0.6 13.9 %copy-start.14 = (s32[1,16]{1,0:T(1,128)S(1)}, s32[1,16]{1,0:T(1,128)}, u32[]{:S(2)}) copy-start(s32[1,16]{1,0:T(1,128)} %param.17) | copy-start | bytes 196
  0.7 16.6 %copy-start.8 = (bf16[512,256]{1,0:T(8,128)(2,1)S(1)}, bf16[512,256]{1,0:T(8,128)(2,1)}, u32[]{:S(2)}) copy-start(bf16[512,256]{1,0:T(8,128)(2,1)} %refs_0_) | copy-start | bytes 786436
  0.7 16.8 %copy-start.12 = (f32[256]{0:T(256)S(1)}, f32[256]{0:T(256)}, u32[]{:S(2)}) copy-start(f32[256]{0:T(256)} %param.18) | copy-start | bytes 3076
  1.8 12.8 %collective-permute-start = (bf16[256,1024]{1,0:T(8,128)(2,1)S(1)}, bf16[256,1024]{1,0:T(8,128)(2,1)S(1)}, u32[]{:S(2)}, u32[]{:S(2)}) collective-permute-start(bf16[256,1024]{1,0:T(8,128)(2,1)S(1)} %constant_dynamic-slice_fusion.own_ref), channel_id=1, source_target_pairs={{30,0},{0,2},{2,4},{4,6},{6,8},{8,10},{10,12},{12,14},{14,16},{16,... | collective-permute-start | bytes 1572872 | tf_op jit(solution)/shard_map/ppermute | solution.py:37
  2.3 17.0 %collective-permute-start.1 = (bf16[256,1024]{1,0:T(8,128)(2,1)S(1)}, bf16[256,1024]{1,0:T(8,128)(2,1)S(1)}, u32[]{:S(2)}, u32[]{:S(2)}) collective-permute-start(bf16[256,1024]{1,0:T(8,128)(2,1)S(1)} %constant_dynamic-slice_fusion.own_ref), channel_id=1, source_target_pairs={{2,0},{4,2},{6,4},{8,6},{10,8},{12,10},{14,12},{16,14},{18,16},{20... | collective-permute-start | bytes 1572872 | tf_op jit(solution)/shard_map/ppermute | solution.py:37
  10.7 26.6 %all-to-all-start = ((bf16[16,128,256]{2,1,0:T(8,128)(2,1)}), bf16[16,128,256]{2,1,0:T(8,128)(2,1)S(1)}, u32[]{:S(2)}, u32[]{:S(2)}) async-start(bf16[16,128,256]{2,1,0:T(8,128)(2,1)} %shard_map.130), calls=%async_computation | async-start | bytes 2097152 | tf_op jit(solution)/shard_map/all_to_all | solution.py:311
  14.4 22.9 %copy-start.10 = (f32[1,16,128]{2,1,0:T(8,128)S(1)}, f32[1,16,128]{2,1,0:T(8,128)}, u32[]{:S(2)}) copy-start(f32[1,16,128]{2,1,0:T(8,128)} %param.16) | copy-start | bytes 24580
  14.5 22.8 %copy-start.9 = (s32[1,16,128]{2,1,0:T(8,128)S(1)}, s32[1,16,128]{2,1,0:T(8,128)}, u32[]{:S(2)}) copy-start(s32[1,16,128]{2,1,0:T(8,128)} %param.15) | copy-start | bytes 24580
  15.4 18.8 %collective-permute-start.4 = (bf16[256,1024]{1,0:T(8,128)(2,1)}, bf16[256,1024]{1,0:T(8,128)(2,1)S(1)}, u32[]{:S(2)}, u32[]{:S(2)}) collective-permute-start(bf16[256,1024]{1,0:T(8,128)(2,1)} %refs_4_), channel_id=1, source_target_pairs={{1,0},{0,1},{3,2},{2,3},{5,4},{4,5},{7,6},{6,7},{9,8},{8,9},{11,10... | collective-permute-start | bytes 1572872 | tf_op jit(solution)/shard_map/ppermute | solution.py:37
  17.3 16.9 %collective-permute-start.2 = (bf16[512,256]{1,0:T(8,128)(2,1)S(1)}, bf16[512,256]{1,0:T(8,128)(2,1)S(1)}, u32[]{:S(2)}, u32[]{:S(2)}) collective-permute-start(bf16[512,256]{1,0:T(8,128)(2,1)S(1)} %copy-done.8), channel_id=1, source_target_pairs={{1,0},{0,1},{3,2},{2,3},{5,4},{4,5},{7,6},{6,7},{9,8},{8,9},{11,10... | collective-permute-start | bytes 786440 | tf_op jit(solution)/shard_map/ppermute | solution.py:37
  17.4 16.8 %collective-permute-start.3 = (f32[256]{0:T(256)S(1)}, f32[256]{0:T(256)S(1)}, u32[]{:S(2)}, u32[]{:S(2)}) collective-permute-start(f32[256]{0:T(256)S(1)} %copy-done.12), channel_id=1, source_target_pairs={{1,0},{0,1},{3,2},{2,3},{5,4},{4,5},{7,6},{6,7},{9,8},{8,9},{11,10... | collective-permute-start | bytes 3080 | tf_op jit(solution)/shard_map/ppermute | solution.py:37
  37.3 16.9 %copy-start.3 = (bf16[256,1024]{1,0:T(8,128)(2,1)S(1)}, bf16[256,1024]{1,0:T(8,128)(2,1)}, u32[]{:S(2)}) copy-start(bf16[256,1024]{1,0:T(8,128)(2,1)} %copy-done.2) | copy-start | bytes 1572868
  39.5 14.6 %collective-permute-start.5 = (bf16[1024,256]{1,0:T(8,128)(2,1)S(1)}, bf16[1024,256]{1,0:T(8,128)(2,1)S(1)}, u32[]{:S(2)}, u32[]{:S(2)}) collective-permute-start(bf16[1024,256]{1,0:T(8,128)(2,1)S(1)} %add_convert_fusion), channel_id=1, source_target_pairs={{1,0},{0,1},{3,2},{2,3},{5,4},{4,5},{7,6},{6,7},{9,8},{8,9},{11,10... | collective-permute-start | bytes 1572872 | tf_op jit(solution)/shard_map/ppermute | solution.py:37
  57.0 2.5 %collective-permute-start.6 = (bf16[288,256]{1,0:T(8,128)(2,1)S(1)}, bf16[288,256]{1,0:T(8,128)(2,1)S(1)}, u32[]{:S(2)}, u32[]{:S(2)}) collective-permute-start(bf16[288,256]{1,0:T(8,128)(2,1)S(1)} %select_convert_fusion), channel_id=1, source_target_pairs={{0,2},{2,0},{4,6},{6,4},{8,10},{10,8},{12,14},{14,12},{16,18},{18,... | collective-permute-start | bytes 442376 | tf_op jit(solution)/shard_map/ppermute | solution.py:42
  59.6 44.9 %all-to-all-start.1 = ((bf16[16,128,256]{2,1,0:T(8,128)(2,1)}), bf16[16,128,256]{2,1,0:T(8,128)(2,1)S(1)}, u32[]{:S(2)}, u32[]{:S(2)}) async-start(bf16[16,128,256]{2,1,0:T(8,128)(2,1)} %shard_map.133), calls=%async_computation.1 | async-start | bytes 2097152 | tf_op jit(solution)/shard_map/all_to_all | solution.py:363
  66.3 11.3 %collective-permute-start.7 = (bf16[144,256]{1,0:T(8,128)(2,1)S(1)}, bf16[144,256]{1,0:T(8,128)(2,1)S(1)}, u32[]{:S(2)}, u32[]{:S(2)}) collective-permute-start(bf16[144,256]{1,0:T(8,128)(2,1)S(1)} %select_convert_fusion.1), channel_id=1, source_target_pairs={{0,4},{2,6},{4,0},{6,2},{8,12},{10,14},{12,8},{14,10},{16,20},{18,... | collective-permute-start | bytes 221192 | tf_op jit(solution)/shard_map/ppermute | solution.py:42
  77.6 8.3 %collective-permute-start.8 = (bf16[144,256]{1,0:T(8,128)(2,1)S(1)}, bf16[144,256]{1,0:T(8,128)(2,1)S(1)}, u32[]{:S(2)}, u32[]{:S(2)}) collective-permute-start(bf16[144,256]{1,0:T(8,128)(2,1)S(1)} %convert_add_fusion.2.mine_ref), channel_id=1, source_target_pairs={{0,8},{2,10},{4,12},{6,14},{8,0},{10,2},{12,4},{14,6},{16,24},{18,... | collective-permute-start | bytes 221192 | tf_op jit(solution)/shard_map/ppermute | solution.py:42
  79.1 24.1 %collective-permute-start.11 = (bf16[1024,256]{1,0:T(8,128)(2,1)}, bf16[1024,256]{1,0:T(8,128)(2,1)}, u32[]{:S(2)}, u32[]{:S(2)}) collective-permute-start(bf16[1024,256]{1,0:T(8,128)(2,1)} %get-tuple-element.54), channel_id=1, source_target_pairs={{2,0},{4,2},{6,4},{8,6},{10,8},{12,10},{14,12},{16,14},{18,16},{20... | collective-permute-start | bytes 1572872 | tf_op jit(solution)/shard_map/ppermute | solution.py:37
  80.7 22.5 %collective-permute-start.12 = (bf16[1024,256]{1,0:T(8,128)(2,1)}, bf16[1024,256]{1,0:T(8,128)(2,1)}, u32[]{:S(2)}, u32[]{:S(2)}) collective-permute-start(bf16[1024,256]{1,0:T(8,128)(2,1)} %get-tuple-element.55), channel_id=1, source_target_pairs={{30,0},{0,2},{2,4},{4,6},{6,8},{8,10},{10,12},{12,14},{14,16},{16,... | collective-permute-start | bytes 1572872 | tf_op jit(solution)/shard_map/ppermute | solution.py:37
  86.0 18.6 %copy-start.11 = (s32[1,16,128]{2,1,0:T(8,128)S(1)}, s32[1,16,128]{2,1,0:T(8,128)}, u32[]{:S(2)}) copy-start(s32[1,16,128]{2,1,0:T(8,128)} %param.14) | copy-start | bytes 24580
  86.0 15.6 %collective-permute-start.9 = (bf16[144,256]{1,0:T(8,128)(2,1)S(1)}, bf16[144,256]{1,0:T(8,128)(2,1)S(1)}, u32[]{:S(2)}, u32[]{:S(2)}) collective-permute-start(bf16[144,256]{1,0:T(8,128)(2,1)S(1)} %convert_element_type.33.mine_ref), channel_id=1, source_target_pairs={{0,16},{2,18},{4,20},{6,22},{8,24},{10,26},{12,28},{14,30},{16,0},... | collective-permute-start | bytes 221192 | tf_op jit(solution)/shard_map/ppermute | solution.py:42
  101.6 5.2 %collective-permute-start.10 = (f32[144,256]{1,0:T(8,128)S(1)}, f32[144,256]{1,0:T(8,128)S(1)}, u32[]{:S(2)}, u32[]{:S(2)}) collective-permute-start(f32[144,256]{1,0:T(8,128)S(1)} %shard_map.137), channel_id=1, source_target_pairs={{0,4},{2,6},{4,0},{6,2},{8,12},{10,14},{12,8},{14,10},{16,20},{18,... | collective-permute-start | bytes 442376 | tf_op jit(solution)/shard_map/ppermute | solution.py:42
  106.9 1.6 %collective-permute-start.13 = (f32[288,256]{1,0:T(8,128)S(1)}, f32[288,256]{1,0:T(8,128)S(1)}, u32[]{:S(2)}, u32[]{:S(2)}) collective-permute-start(f32[288,256]{1,0:T(8,128)S(1)} %maximum_select_fusion.mine_ref), channel_id=1, source_target_pairs={{0,2},{2,0},{4,6},{6,4},{8,10},{10,8},{12,14},{14,12},{16,18},{18,... | collective-permute-start | bytes 884744 | tf_op jit(solution)/shard_map/ppermute | solution.py:42
  (7 other events, 10.0 us)

commit v4 on v3

--- a/solution.py
+++ b/solution.py
@@ -21,7 +21,7 @@
         kernel,
         out_shape=tuple(outs),
         in_specs=[place for place, _ in operands],
-        out_specs=tuple(place for _ in outs),
+        out_specs=tuple(place) if isinstance(place, list) else tuple(place for _ in outs),
         scratch_shapes=scratch,
         compiler_params=pltpu.CompilerParams(vmem_limit_bytes=mib * 1024 * 1024),
         cost_estimate=pl.CostEstimate(flops=us * 1000**3, bytes_accessed=1, transcendentals=0),
@@ -46,9 +46,9 @@
     return jnp.dot(a, b, preferred_element_type=F32)
 
 
-def slots_by_nodes(hot, rows_t, nodes, first, count):
+def slots_by_nodes(hot, rows_t, first_node, first, count):
     slots = rows_t.shape[0]
-    lanes = lax.broadcasted_iota(jnp.int32, (slots, nodes), 1)
+    lanes = lax.broadcasted_iota(jnp.int32, (slots, hot.shape[1]), 1) + first_node
     for p in range(first, first + count):
         hot[p * slots : (p + 1) * slots, :] = jnp.where(
             rows_t[:, p : p + 1] == lanes, 1.0, 0.0
@@ -97,8 +97,8 @@
     block_copy = copies.start(features_ref.at[pl.ds(start, rows), :], block)
     lists_copy.wait()
     send_t = lists[...].T
-    group = 4
-    slots_by_nodes(hot, send_t, nodes, 0, group)
+    group = 2
+    slots_by_nodes(hot, send_t, 0, 0, group)
     block_copy.wait()
     sent = []
     block_t = block[...].T
@@ -107,7 +107,7 @@
         picked[p : p + group] = part.astype(BF16).reshape(group, slots, rows)
         sent.append(copies.start(picked.at[pl.ds(p, group)], out_ref.at[pl.ds(p, group)]))
         if p + group < peers:
-            slots_by_nodes(hot, send_t, nodes, p + group, group)
+            slots_by_nodes(hot, send_t, 0, p + group, group)
     for copy in sent:
         copy.wait()
 
@@ -177,14 +177,19 @@
     part_ref[size:, :] = jnp.broadcast_to(total, (part_ref.shape[0] - size, part_ref.shape[1]))
 
 
-def layer_kernel(n_hid, hid_ref, *refs):
+def layer_kernel(n_hid, first, hid_ref, *refs):
     take = iter(refs)
     weights, biases, cotangents = ([next(take) for _ in range(n_hid)] for _ in range(3))
-    aggs, output_ref, part_ref, back_ref, held, sems = take
+    aggs, recv_ref, weight_ref, counts_ref = (next(take) for _ in range(4))
+    earlier_ref = next(take) if first else None
+    output_ref, part_ref, back_ref, message_ref, held, earlier, hot, sems = take
     copies = Copies(sems)
-    cotangents_in = [copies.start(ref, held.at[k]) for k, ref in enumerate(cotangents)]
+    earlier_in = copies.start(earlier_ref, earlier) if first else None
     width, nodes = output_ref.shape
     rows = back_ref.shape[1]
+    cotangents_in = [
+        copies.start(ref.at[:, pl.ds(first, nodes)], held.at[k]) for k, ref in enumerate(cotangents)
+    ]
     own = pl.ds(pl.multiple_of(hid_ref[0] * rows, rows), rows)
     total = None
     for k in range(n_hid):
@@ -204,21 +209,26 @@
         )
         total = term if total is None else total + term
     back_ref[...] = total.astype(BF16)
-
-
-def message_kernel(recv_ref, weight_ref, counts_ref, back_ref, message_ref, hot):
+    back = back_ref[...]
     peers, slots, _ = message_ref.shape
-    back = back_ref[...]
-    nodes = back.shape[0]
     weights_t = masked_weights(weight_ref[...], counts_ref[...]).T
     recv_t = recv_ref[...].T
+    if first:
+        earlier_in.wait()
+    sent = []
     group = 4
     for p in range(0, peers, group):
-        slots_by_nodes(hot, recv_t, nodes, p, group)
+        slots_by_nodes(hot, recv_t, first, p, group)
         picked = dot(hot[p * slots : (p + group) * slots, :], back)
         for n in range(group):
             row = picked[n * slots : (n + 1) * slots] * weights_t[:, p + n : p + n + 1]
-            message_ref[p + n] = row.astype(BF16)
+            if first:
+                row = row + earlier[p + n].astype(F32)
+            earlier[p + n] = row.astype(BF16)
+        lines = pl.ds(p, group)
+        sent.append(copies.start(earlier.at[lines], message_ref.at[lines]))
+    for copy in sent:
+        copy.wait()
 
 
 def joined_kernel(odd_ref, mine_ref, other_ref, weight_ref, bias_ref):
@@ -251,16 +261,14 @@
     return part
 
 
-def sum_kernel(mine_ref, other_ref, out_ref):
-    out_ref[...] = mine_ref[...].astype(F32) + other_ref[...].astype(F32)
-
-
-def doubled(part, axis, bits, us=1):
-    for bit in bits:
-        sent = part.astype(BF16)
-        (part,) = call(
-            sum_kernel, [out(part.shape, F32)], [(VMEM, sent), (VMEM, swapped(sent, axis, bit))], us=us
-        )
+def exchanged(part, axis, bits):
+    while bits:
+        sent, near, bits = part.astype(BF16), bits[0], bits[1:]
+        part = sent.astype(F32) + swapped(sent, axis, near).astype(F32)
+        if bits:
+            far, bits = bits[0], bits[1:]
+            others = [swapped(sent, axis, bit).astype(F32) for bit in (far, far ^ near)]
+            part = part + (others[0] + others[1])
     return part
 
 
@@ -330,43 +338,60 @@
         [vmem((nodes, lists), BF16), vmem((lists, rows), BF16)],
         us=4,
     )
-    agg = (dense + sparse).astype(BF16)
-    aggs = jnp.stack([agg] + [shifted(agg, "hid", k) for k in steps])
     bits = [1 << b for b in range((peers - 1).bit_length())]
     pad = 64
-    output, part, back = call(
-        functools.partial(layer_kernel, n_hid),
-        [
-            out((width, nodes), BF16),
-            out((n_hid * rows + pad, width), F32),
-            out((nodes, rows), BF16),
-        ],
-        [
-            hid,
-            *[(VMEM, w) for w in weights],
-            *[(VMEM, b[None, :]) for b in biases],
-            *[(HBM, c) for c in cotangents],
-            (VMEM, aggs),
-        ],
-        [vmem((n_hid, width, nodes), BF16), sems(n_hid)],
-        us=2,
-    )
-    (message,) = call(
-        message_kernel,
-        [out((peers, slots, rows), BF16)],
-        [*edges, (VMEM, back)],
-        [vmem((lists, nodes), BF16)],
-        us=2,
-    )
+    cuts = 2
+    size = nodes // cuts
+    outputs, parts, backs, message = [], [], [], None
+    for cut in range(cuts):
+        lines = slice(cut * size, (cut + 1) * size)
+        agg = (dense[lines] + sparse[lines]).astype(BF16)
+        others = [shifted(agg, "hid", k) for k in steps]
+        if backs:
+            agg, _ = lax.optimization_barrier((agg, backs[-1]))
+        aggs = jnp.stack([agg] + others)
+        output, part, back, message = call(
+            functools.partial(layer_kernel, n_hid, cut * size),
+            [
+                out((width, size), BF16),
+                out((n_hid * rows + pad, width), F32),
+                out((size, rows), BF16),
+                out((peers, slots, rows), BF16),
+            ],
+            [
+                hid,
+                *[(VMEM, w) for w in weights],
+                *[(VMEM, b[None, :]) for b in biases],
+                *[(HBM, c) for c in cotangents],
+                (VMEM, aggs),
+                *edges,
+                *([(HBM, message)] if cut else []),
+            ],
+            [
+                vmem((n_hid, width, size), BF16),
+                vmem((peers, slots, rows), BF16),
+                vmem((lists, size), BF16),
+                sems(n_hid + 1 + peers),
+            ],
+            us=2,
+            mib=24,
+            place=[VMEM, VMEM, VMEM, HBM],
+        )
+        outputs.append(output)
+        parts.append(part)
+        backs.append(back)
+    part = sum(parts[1:], parts[0])
     part = halved(part, "dom", bits[:1])
-    message, part, back = lax.optimization_barrier((message, part, back))
-    returned = lax.all_to_all(message, "dom", split_axis=0, concat_axis=0, tiled=True)
-
+    back = jnp.concatenate(backs)
     to_before, to_after = call(
         functools.partial(dense_backward_kernel, (0, 2)),
         [out((nodes, rows), BF16)] * 2,
         [*tiles, (VMEM, back)],
-    )
+        us=2,
+    )
+    from_after, from_before = shifted(to_before, "dom", 1), shifted(to_after, "dom", -1)
+    message, _ = lax.optimization_barrier((message, to_before))
+    returned = lax.all_to_all(message, "dom", split_axis=0, concat_axis=0, tiled=True)
     (kept,) = call(
         functools.partial(dense_backward_kernel, (1,)),
         [out((nodes, rows), F32)],
@@ -374,26 +399,27 @@
     )
     part = halved(part, "dom", bits[1:2])
     part, to_before, to_after = lax.optimization_barrier((part, to_before, to_after))
-    from_after, from_before = shifted(to_before, "dom", 1), shifted(to_after, "dom", -1)
-    part = doubled(part, "dom", bits[2:3], 5)
-    part, kept = lax.optimization_barrier((part, kept))
-    part = doubled(part, "dom", bits[3:])
-    base = kept + from_after.astype(F32) + from_before.astype(F32)
+    part = exchanged(part, "dom", bits[2:])
+    place = lax.axis_index("dom")
+    far = swapped(part, "dom", 2)
+    part = paired(part, far, place // 2 % 2)
+    output = jnp.concatenate(outputs, axis=1)
+    part, output, kept, from_before, from_after = lax.optimization_barrier(
+        (part, output, kept, from_before, from_after)
+    )
+    base = kept + from_before.astype(F32) + from_after.astype(F32)
+    other = swapped(part, "dom", 1)
+    weight_grad, bias_grad = call(
+        joined_kernel,
+        [out((n_hid * rows, width), F32), out((1, width), F32)],
+        [(SMEM, (place % 2).astype(jnp.int32).reshape(1)), (VMEM, part), (VMEM, other)],
+        us=15,
+    )
     (feature_grad,) = call(
         scatter_kernel,
         [out((rows, nodes), BF16)],
         [send, (VMEM, returned), (VMEM, base)],
         [vmem((nodes, lists), BF16)],
-    )
-    place = lax.axis_index("dom")
-    far = swapped(part, "dom", 2)
-    far, feature_grad = lax.optimization_barrier((far, feature_grad))
-    part = paired(part, far, place // 2 % 2)
-    other = swapped(part, "dom", 1)
-    weight_grad, bias_grad = call(
-        joined_kernel,
-        [out((n_hid * rows, width), F32), out((1, width), F32)],
-        [(SMEM, (place % 2).astype(jnp.int32).reshape(1)), (VMEM, part), (VMEM, other)],
     )
     return (output, feature_grad, weight_grad, bias_grad[0])
 

time: 110 us -> 105 us (0.955)
  the two profiles are of different devices: /device:TPU:0 before, /device:TPU:31 now
where the time goes in v4:
time: 105 us; the launch traced here: 104 us
  waiting for transfers between devices  38.5 us (37%)
  starting transfers between devices  27.5 us (26%)
  Pallas kernels  21.2 us (20%)
  local copies, waits for them, and re-layouts  13.1 us (12%)
  other arithmetic  2.74 us (3%)
    pallas_call x9, Pallas kernels, call(): pl.pallas_call(kernel, out_shape=tuple(outs), in_specs=[place for place,...  21.2 us
    ppermute x7, waiting for transfers between devices, swapped(): return lax.ppermute(block, axis, [(i, i ^ bit) for i in range(size)])  14.7 us
    unnamed x42, local copies, waits for them, and re-layouts  11.8 us
    ppermute x9, waiting for transfers between devices, shifted(): lax.ppermute(block, axis, [((i + distance) % size, i) for i in range(size)])  11.4 us
    all_to_all x1, starting transfers between devices, on_device(): lax.all_to_all(message, 'dom', split_axis=0, concat_axis=0, tiled=True)  7.78 us
    all_to_all x1, starting transfers between devices, on_device(): lax.all_to_all(outgoing, 'dom', split_axis=0, concat_axis=0, tiled=True)  7.72 us
    all_to_all x1, waiting for transfers between devices, on_device(): lax.all_to_all(outgoing, 'dom', split_axis=0, concat_axis=0, tiled=True)  7.49 us
    ppermute x9, starting transfers between devices, shifted(): lax.ppermute(block, axis, [((i + distance) % size, i) for i in range(size)])  6.18 us
  transfers between devices with their start and end apart: 18, of which 8 were waited for; matrix products, arithmetic and copies ran while one was open for 2% of the time, Pallas kernels for 13%

profile of v4, /device:TPU:31, one launch (start us, length us, event | category | flops | bytes accessed | tf_op | source)
XLA Modules:
  0.0 104.0 jit_solution(10290123937125495911)
XLA Ops:
  2.6 3.2 %shard_map.130 = bf16[16,128,256]{2,1,0:T(8,128)(2,1)} custom-call(s32[1]{0:T(128)} %bitcast.hid_ref, bf16[512,1024]{1,0:T(8,128)(2,1)} %features_ref.1, s32[16,128]{1,0:T(8,128)} %bitcast.21), custom_call_target="tpu_custom_call" | custom-call | flops 1000000000 | bytes 1 | tf_op jit(solution)/shard_map/pallas_call | solution.py:20
  5.9 7.7 %all-to-all-start = ((bf16[16,128,256]{2,1,0:T(8,128)(2,1)}), bf16[16,128,256]{2,1,0:T(8,128)(2,1)S(1)}, u32[]{:S(2)}, u32[]{:S(2)}) async-start(bf16[16,128,256]{2,1,0:T(8,128)(2,1)} %shard_map.130), calls=%async_computation | async-start | bytes 2097152 | tf_op jit(solution)/shard_map/all_to_all | solution.py:319
  14.6 1.5 %collective-permute-start.3 = (f32[256]{0:T(256)S(1)}, f32[256]{0:T(256)S(1)}, u32[]{:S(2)}, u32[]{:S(2)}) collective-permute-start(f32[256]{0:T(256)S(1)} %copy-done.15), channel_id=1, source_target_pairs={{1,0},{0,1},{3,2},{2,3},{5,4},{4,5},{7,6},{6,7},{9,8},{8,9},{11,10... | collective-permute-start | bytes 3080 | tf_op jit(solution)/shard_map/ppermute | solution.py:37
  17.0 2.8 %copy-done = bf16[3072,1024]{1,0:T(8,128)(2,1)S(1)} copy-done((bf16[3072,1024]{1,0:T(8,128)(2,1)S(1)}, bf16[3072,1024]{1,0:T(8,128)(2,1)}, u32[]{:S(2)}) %copy-start) | copy-done | bytes 6291480
  21.8 2.6 %shard_map.129 = f32[1024,256]{1,0:T(8,128)S(1)} custom-call(s32[12,4]{1,0:T(8,128)S(1)} %copy.14.live_ref, bf16[3072,1024]{1,0:T(8,128)(2,1)S(1)} %copy-done, bf16[256,1024]{1,0:T(8,128)(2,1)S(1)} %copy-done.6, bf16[256,1024]{1,0:T(8,128)(2,1)S(1)} %constant_dynamic-slice_fusion.own_ref, bf16[256,1024]{1,0:T(8,128)(2,1)S(1)} %copy-done.8), custom_call_target="tpu_custom_call" | custom-call | flops 60000002048 | bytes 1 | tf_op jit(solution)/shard_map/pallas_call | solution.py:20
  25.2 4.1 %collective-permute-done.4.refs_5_ = bf16[256,1024]{1,0:T(8,128)(2,1)S(1)} collective-permute-done((bf16[256,1024]{1,0:T(8,128)(2,1)S(1)}, bf16[256,1024]{1,0:T(8,128)(2,1)S(1)}, u32[]{:S(2)}, u32[]{:S(2)}) %collective-permute-start.4) | collective-permute-done | bytes 524320 | tf_op jit(solution)/shard_map/ppermute | solution.py:37
  30.0 7.5 %all-to-all-done.arrived_ref = bf16[16,128,256]{2,1,0:T(8,128)(2,1)S(1)} async-done(((bf16[16,128,256]{2,1,0:T(8,128)(2,1)}), bf16[16,128,256]{2,1,0:T(8,128)(2,1)S(1)}, u32[]{:S(2)}, u32[]{:S(2)}) %all-to-all-start) | async-done | bytes 1048608 | tf_op jit(solution)/shard_map/all_to_all | solution.py:319
  37.5 1.9 %shard_map.131 = f32[1024,256]{1,0:T(8,128)S(1)} custom-call(s32[16,128]{1,0:T(8,128)S(1)} %bitcast.15, f32[16,128]{1,0:T(8,128)S(1)} %bitcast.18, s32[16,1]{1,0:T(8,128)S(1)} %copy.15.counts_ref.refs_9_, bf16[16,128,256]{2,1,0:T(8,128)(2,1)S(1)} %all-to-all-done.arrived_ref), custom_call_target="tpu_custom_call" | custom-call | flops 4000000000 | bytes 1 | tf_op jit(solution)/shard_map/pallas_call | solution.py:20
  39.7 1.4 %collective-permute-start.6 = (bf16[512,256]{1,0:T(8,128)(2,1)S(1)}, bf16[512,256]{1,0:T(8,128)(2,1)S(1)}, u32[]{:S(2)}, u32[]{:S(2)}) collective-permute-start(bf16[512,256]{1,0:T(8,128)(2,1)S(1)} %get-tuple-element.48), channel_id=1, source_target_pairs={{1,0},{0,1},{3,2},{2,3},{5,4},{4,5},{7,6},{6,7},{9,8},{8,9},{11,10... | collective-permute-start | bytes 786440 | tf_op jit(solution)/shard_map/ppermute | solution.py:37
  41.2 6.2 %collective-permute-done.5 = bf16[512,256]{1,0:T(8,128)(2,1)S(1)} collective-permute-done((bf16[512,256]{1,0:T(8,128)(2,1)S(1)}, bf16[512,256]{1,0:T(8,128)(2,1)S(1)}, u32[]{:S(2)}, u32[]{:S(2)}) %collective-permute-start.5) | collective-permute-done | bytes 262176 | tf_op jit(solution)/shard_map/ppermute | solution.py:37
  48.4 3.5 %shard_map.132 = (bf16[256,512]{1,0:T(8,128)(2,1)S(1)}, f32[576,256]{1,0:T(8,128)S(1)}, bf16[512,256]{1,0:T(8,128)(2,1)S(1)}, bf16[16,128,256]{2,1,0:T(8,128)(2,1)S(1)}) custom-call(s32[1]{0:T(128)} %bitcast.hid_ref, bf16[512,256]{1,0:T(8,128)(2,1)S(1)} %copy-done.9, bf16[512,256]{1,0:T(8,128)(2,1)S(1)} %copy-done.11, f32[1,256]{1,0:T(1,128)S(1)} %bitcast.23, ...), custom_call_target="tpu_custom_call" | custom-call | flops 2000000000 | bytes 1 | tf_op jit(solution)/shard_map/pallas_call | solution.py:20
  53.1 3.4 %shard_map.133 = (bf16[256,512]{1,0:T(8,128)(2,1)S(1)}, f32[576,256]{1,0:T(8,128)S(1)}, bf16[512,256]{1,0:T(8,128)(2,1)S(1)}, bf16[16,128,256]{2,1,0:T(8,128)(2,1)}) custom-call(s32[1]{0:T(128)} %bitcast.hid_ref, bf16[512,256]{1,0:T(8,128)(2,1)S(1)} %copy-done.9, bf16[512,256]{1,0:T(8,128)(2,1)S(1)} %copy-done.11, f32[1,256]{1,0:T(1,128)S(1)} %bitcast.24, ...), custom_call_target="tpu_custom_call" | custom-call | flops 2000000000 | bytes 1 | tf_op jit(solution)/shard_map/pallas_call | solution.py:20
  58.9 2.0 %shard_map.134 = (bf16[1024,256]{1,0:T(8,128)(2,1)S(1)}, bf16[1024,256]{1,0:T(8,128)(2,1)S(1)}) custom-call(s32[12,4]{1,0:T(8,128)S(1)} %copy.14.live_ref, bf16[3072,1024]{1,0:T(8,128)(2,1)S(1)} %bitcast.14, bf16[1024,256]{1,0:T(8,128)(2,1)S(1)} %constant_dynamic-update-slice_fusion.back_ref), custom_call_target="tpu_custom_call" | custom-call | flops 2000000000 | bytes 1 | tf_op jit(solution)/shard_map/pallas_call | solution.py:20
  60.8 1.2 %collective-permute-done.8 = bf16[144,256]{1,0:T(8,128)(2,1)S(1)} collective-permute-done((bf16[144,256]{1,0:T(8,128)(2,1)S(1)}, bf16[144,256]{1,0:T(8,128)(2,1)S(1)}, u32[]{:S(2)}, u32[]{:S(2)}) %collective-permute-start.8) | collective-permute-done | bytes 73760 | tf_op jit(solution)/shard_map/ppermute | solution.py:42
  62.2 1.9 %collective-permute-start.10 = (bf16[144,256]{1,0:T(8,128)(2,1)S(1)}, bf16[144,256]{1,0:T(8,128)(2,1)S(1)}, u32[]{:S(2)}, u32[]{:S(2)}) collective-permute-start(bf16[144,256]{1,0:T(8,128)(2,1)S(1)} %convert_add_fusion.2), channel_id=1, source_target_pairs={{0,16},{2,18},{4,20},{6,22},{8,24},{10,26},{12,28},{14,30},{16,0},... | collective-permute-start | bytes 221192 | tf_op jit(solution)/shard_map/ppermute | solution.py:42
  64.1 1.6 %collective-permute-start.9 = (bf16[144,256]{1,0:T(8,128)(2,1)S(1)}, bf16[144,256]{1,0:T(8,128)(2,1)S(1)}, u32[]{:S(2)}, u32[]{:S(2)}) collective-permute-start(bf16[144,256]{1,0:T(8,128)(2,1)S(1)} %convert_add_fusion.2), channel_id=1, source_target_pairs={{0,8},{2,10},{4,12},{6,14},{8,0},{10,2},{12,4},{14,6},{16,24},{18,... | collective-permute-start | bytes 221192 | tf_op jit(solution)/shard_map/ppermute | solution.py:42
  65.7 2.1 %collective-permute-start.13 = (bf16[1024,256]{1,0:T(8,128)(2,1)S(1)}, bf16[1024,256]{1,0:T(8,128)(2,1)}, u32[]{:S(2)}, u32[]{:S(2)}) collective-permute-start(bf16[1024,256]{1,0:T(8,128)(2,1)S(1)} %get-tuple-element.53), channel_id=1, source_target_pairs={{30,0},{0,2},{2,4},{4,6},{6,8},{8,10},{10,12},{12,14},{14,16},{16,... | collective-permute-start | bytes 1572872 | tf_op jit(solution)/shard_map/ppermute | solution.py:37
  68.0 7.8 %all-to-all-start.1 = ((bf16[16,128,256]{2,1,0:T(8,128)(2,1)}), bf16[16,128,256]{2,1,0:T(8,128)(2,1)S(1)}, u32[]{:S(2)}, u32[]{:S(2)}) async-start(bf16[16,128,256]{2,1,0:T(8,128)(2,1)} %get-tuple-element.59), calls=%async_computation.1 | async-start | bytes 2097152 | tf_op jit(solution)/shard_map/all_to_all | solution.py:394
  76.2 2.8 %copy-done.1 = bf16[3072,1024]{1,0:T(8,128)(2,1)S(1)} copy-done((bf16[3072,1024]{1,0:T(8,128)(2,1)S(1)}, bf16[3072,1024]{1,0:T(8,128)(2,1)}, u32[]{:S(2)}) %copy-start.1) | copy-done | bytes 6291480
  79.0 1.4 %shard_map.135 = f32[1024,256]{1,0:T(8,128)S(1)} custom-call(s32[12,4]{1,0:T(8,128)S(1)} %copy.14.live_ref, bf16[3072,1024]{1,0:T(8,128)(2,1)S(1)} %copy-done.1, bf16[1024,256]{1,0:T(8,128)(2,1)S(1)} %constant_dynamic-update-slice_fusion.back_ref), custom_call_target="tpu_custom_call" | custom-call | flops 1000000000 | bytes 1 | tf_op jit(solution)/shard_map/pallas_call | solution.py:20
  81.3 12.5 %collective-permute-done.12 = f32[144,256]{1,0:T(8,128)S(1)} collective-permute-done((f32[144,256]{1,0:T(8,128)S(1)}, f32[144,256]{1,0:T(8,128)S(1)}, u32[]{:S(2)}, u32[]{:S(2)}) %collective-permute-start.12) | collective-permute-done | bytes 147488 | tf_op jit(solution)/shard_map/ppermute | solution.py:42
  94.5 1.3 %convert_add_fusion.dense_ref = f32[1024,256]{1,0:T(8,128)S(1)} fusion(bf16[1024,256]{1,0:T(8,128)(2,1)} %collective-permute-done.14, f32[1024,256]{1,0:T(8,128)S(1)} %shard_map.135, bf16[1024,256]{1,0:T(8,128)(2,1)} %collective-permute-done.13), kind=kLoop, calls=%fused_computation | loop fusion | flops 1048576 | bytes 3145728 | tf_op jit(solution)/shard_map/add | solution.py:410
  96.8 4.9 %all-to-all-done.1.returned_ref = bf16[16,128,256]{2,1,0:T(8,128)(2,1)S(1)} async-done(((bf16[16,128,256]{2,1,0:T(8,128)(2,1)}), bf16[16,128,256]{2,1,0:T(8,128)(2,1)S(1)}, u32[]{:S(2)}, u32[]{:S(2)}) %all-to-all-start.1) | async-done | bytes 1048608 | tf_op jit(solution)/shard_map/all_to_all | solution.py:394
  101.7 2.3 %shard_map.136 = bf16[256,1024]{1,0:T(8,128)(2,1)} custom-call(s32[16,128]{1,0:T(8,128)S(1)} %bitcast.22, bf16[16,128,256]{2,1,0:T(8,128)(2,1)S(1)} %all-to-all-done.1.returned_ref, f32[1024,256]{1,0:T(8,128)S(1)} %convert_add_fusion.dense_ref), custom_call_target="tpu_custom_call" | custom-call | flops 1000000000 | bytes 1 | tf_op jit(solution)/shard_map/pallas_call | solution.py:20
  (79 shorter events, 15.3 us)
Async XLA Ops:
  0.6 13.1 %copy-start.17 = (s32[1,16]{1,0:T(1,128)S(1)}, s32[1,16]{1,0:T(1,128)}, u32[]{:S(2)}) copy-start(s32[1,16]{1,0:T(1,128)} %param.17) | copy-start | bytes 196
  0.7 14.0 %copy-start.9 = (bf16[512,256]{1,0:T(8,128)(2,1)S(1)}, bf16[512,256]{1,0:T(8,128)(2,1)}, u32[]{:S(2)}) copy-start(bf16[512,256]{1,0:T(8,128)(2,1)} %refs_0_.1) | copy-start | bytes 786436
  0.7 14.0 %copy-start.15 = (f32[256]{0:T(256)S(1)}, f32[256]{0:T(256)}, u32[]{:S(2)}) copy-start(f32[256]{0:T(256)} %param.18) | copy-start | bytes 3076
  0.7 15.4 %copy-start.2 = (bf16[256,1024]{1,0:T(8,128)(2,1)S(1)}, bf16[256,1024]{1,0:T(8,128)(2,1)}, u32[]{:S(2)}) copy-start(bf16[256,1024]{1,0:T(8,128)(2,1)} %refs_4_.1) | copy-start | bytes 1572868
  1.8 12.0 %collective-permute-start = (bf16[256,1024]{1,0:T(8,128)(2,1)S(1)}, bf16[256,1024]{1,0:T(8,128)(2,1)S(1)}, u32[]{:S(2)}, u32[]{:S(2)}) collective-permute-start(bf16[256,1024]{1,0:T(8,128)(2,1)S(1)} %constant_dynamic-slice_fusion.own_ref), channel_id=1, source_target_pairs={{30,0},{0,2},{2,4},{4,6},{6,8},{8,10},{10,12},{12,14},{14,16},{16,... | collective-permute-start | bytes 1572872 | tf_op jit(solution)/shard_map/ppermute | solution.py:37
  2.3 13.8 %collective-permute-start.1 = (bf16[256,1024]{1,0:T(8,128)(2,1)S(1)}, bf16[256,1024]{1,0:T(8,128)(2,1)S(1)}, u32[]{:S(2)}, u32[]{:S(2)}) collective-permute-start(bf16[256,1024]{1,0:T(8,128)(2,1)S(1)} %constant_dynamic-slice_fusion.own_ref), channel_id=1, source_target_pairs={{2,0},{4,2},{6,4},{8,6},{10,8},{12,10},{14,12},{16,14},{18,16},{20... | collective-permute-start | bytes 1572872 | tf_op jit(solution)/shard_map/ppermute | solution.py:37
  5.9 31.6 %all-to-all-start = ((bf16[16,128,256]{2,1,0:T(8,128)(2,1)}), bf16[16,128,256]{2,1,0:T(8,128)(2,1)S(1)}, u32[]{:S(2)}, u32[]{:S(2)}) async-start(bf16[16,128,256]{2,1,0:T(8,128)(2,1)} %shard_map.130), calls=%async_computation | async-start | bytes 2097152 | tf_op jit(solution)/shard_map/all_to_all | solution.py:319
  13.6 23.9 %copy-start.13 = (f32[1,16,128]{2,1,0:T(8,128)S(1)}, f32[1,16,128]{2,1,0:T(8,128)}, u32[]{:S(2)}) copy-start(f32[1,16,128]{2,1,0:T(8,128)} %param.16) | copy-start | bytes 24580
  13.7 23.8 %copy-start.12 = (s32[1,16,128]{2,1,0:T(8,128)S(1)}, s32[1,16,128]{2,1,0:T(8,128)}, u32[]{:S(2)}) copy-start(s32[1,16,128]{2,1,0:T(8,128)} %param.15) | copy-start | bytes 24580
  14.6 9.8 %collective-permute-start.2 = (bf16[512,256]{1,0:T(8,128)(2,1)S(1)}, bf16[512,256]{1,0:T(8,128)(2,1)S(1)}, u32[]{:S(2)}, u32[]{:S(2)}) collective-permute-start(bf16[512,256]{1,0:T(8,128)(2,1)S(1)} %copy-done.9), channel_id=1, source_target_pairs={{1,0},{0,1},{3,2},{2,3},{5,4},{4,5},{7,6},{6,7},{9,8},{8,9},{11,10... | collective-permute-start | bytes 786440 | tf_op jit(solution)/shard_map/ppermute | solution.py:37
  14.6 9.8 %collective-permute-start.3 = (f32[256]{0:T(256)S(1)}, f32[256]{0:T(256)S(1)}, u32[]{:S(2)}, u32[]{:S(2)}) collective-permute-start(f32[256]{0:T(256)S(1)} %copy-done.15), channel_id=1, source_target_pairs={{1,0},{0,1},{3,2},{2,3},{5,4},{4,5},{7,6},{6,7},{9,8},{8,9},{11,10... | collective-permute-start | bytes 3080 | tf_op jit(solution)/shard_map/ppermute | solution.py:37
  16.1 13.1 %collective-permute-start.4 = (bf16[256,1024]{1,0:T(8,128)(2,1)S(1)}, bf16[256,1024]{1,0:T(8,128)(2,1)S(1)}, u32[]{:S(2)}, u32[]{:S(2)}) collective-permute-start(bf16[256,1024]{1,0:T(8,128)(2,1)S(1)} %copy-done.2), channel_id=1, source_target_pairs={{1,0},{0,1},{3,2},{2,3},{5,4},{4,5},{7,6},{6,7},{9,8},{8,9},{11,10... | collective-permute-start | bytes 1572872 | tf_op jit(solution)/shard_map/ppermute | solution.py:37
  39.6 7.8 %collective-permute-start.5 = (bf16[512,256]{1,0:T(8,128)(2,1)S(1)}, bf16[512,256]{1,0:T(8,128)(2,1)S(1)}, u32[]{:S(2)}, u32[]{:S(2)}) collective-permute-start(bf16[512,256]{1,0:T(8,128)(2,1)S(1)} %get-tuple-element.67), channel_id=1, source_target_pairs={{1,0},{0,1},{3,2},{2,3},{5,4},{4,5},{7,6},{6,7},{9,8},{8,9},{11,10... | collective-permute-start | bytes 786440 | tf_op jit(solution)/shard_map/ppermute | solution.py:37
  39.7 13.3 %collective-permute-start.6 = (bf16[512,256]{1,0:T(8,128)(2,1)S(1)}, bf16[512,256]{1,0:T(8,128)(2,1)S(1)}, u32[]{:S(2)}, u32[]{:S(2)}) collective-permute-start(bf16[512,256]{1,0:T(8,128)(2,1)S(1)} %get-tuple-element.48), channel_id=1, source_target_pairs={{1,0},{0,1},{3,2},{2,3},{5,4},{4,5},{7,6},{6,7},{9,8},{8,9},{11,10... | collective-permute-start | bytes 786440 | tf_op jit(solution)/shard_map/ppermute | solution.py:37
  56.6 2.1 %collective-permute-start.7 = (bf16[288,256]{1,0:T(8,128)(2,1)S(1)}, bf16[288,256]{1,0:T(8,128)(2,1)S(1)}, u32[]{:S(2)}, u32[]{:S(2)}) collective-permute-start(bf16[288,256]{1,0:T(8,128)(2,1)S(1)} %select_convert_fusion), channel_id=1, source_target_pairs={{0,2},{2,0},{4,6},{6,4},{8,10},{10,8},{12,14},{14,12},{16,18},{18,... | collective-permute-start | bytes 442376 | tf_op jit(solution)/shard_map/ppermute | solution.py:42
  58.8 3.3 %collective-permute-start.8 = (bf16[144,256]{1,0:T(8,128)(2,1)S(1)}, bf16[144,256]{1,0:T(8,128)(2,1)S(1)}, u32[]{:S(2)}, u32[]{:S(2)}) collective-permute-start(bf16[144,256]{1,0:T(8,128)(2,1)S(1)} %select_convert_fusion.1), channel_id=1, source_target_pairs={{0,4},{2,6},{4,0},{6,2},{8,12},{10,14},{12,8},{14,10},{16,20},{18,... | collective-permute-start | bytes 221192 | tf_op jit(solution)/shard_map/ppermute | solution.py:42
  62.1 13.8 %collective-permute-start.11 = (bf16[144,256]{1,0:T(8,128)(2,1)S(1)}, bf16[144,256]{1,0:T(8,128)(2,1)S(1)}, u32[]{:S(2)}, u32[]{:S(2)}) collective-permute-start(bf16[144,256]{1,0:T(8,128)(2,1)S(1)} %convert_add_fusion.2), channel_id=1, source_target_pairs={{0,24},{2,26},{4,28},{6,30},{8,16},{10,18},{12,20},{14,22},{16,8},... | collective-permute-start | bytes 221192 | tf_op jit(solution)/shard_map/ppermute | solution.py:42
  62.2 13.7 %collective-permute-start.10 = (bf16[144,256]{1,0:T(8,128)(2,1)S(1)}, bf16[144,256]{1,0:T(8,128)(2,1)S(1)}, u32[]{:S(2)}, u32[]{:S(2)}) collective-permute-start(bf16[144,256]{1,0:T(8,128)(2,1)S(1)} %convert_add_fusion.2), channel_id=1, source_target_pairs={{0,16},{2,18},{4,20},{6,22},{8,24},{10,26},{12,28},{14,30},{16,0},... | collective-permute-start | bytes 221192 | tf_op jit(solution)/shard_map/ppermute | solution.py:42
  64.1 11.7 %collective-permute-start.9 = (bf16[144,256]{1,0:T(8,128)(2,1)S(1)}, bf16[144,256]{1,0:T(8,128)(2,1)S(1)}, u32[]{:S(2)}, u32[]{:S(2)}) collective-permute-start(bf16[144,256]{1,0:T(8,128)(2,1)S(1)} %convert_add_fusion.2), channel_id=1, source_target_pairs={{0,8},{2,10},{4,12},{6,14},{8,0},{10,2},{12,4},{14,6},{16,24},{18,... | collective-permute-start | bytes 221192 | tf_op jit(solution)/shard_map/ppermute | solution.py:42
  65.7 28.1 %collective-permute-start.13 = (bf16[1024,256]{1,0:T(8,128)(2,1)S(1)}, bf16[1024,256]{1,0:T(8,128)(2,1)}, u32[]{:S(2)}, u32[]{:S(2)}) collective-permute-start(bf16[1024,256]{1,0:T(8,128)(2,1)S(1)} %get-tuple-element.53), channel_id=1, source_target_pairs={{30,0},{0,2},{2,4},{4,6},{6,8},{8,10},{10,12},{12,14},{14,16},{16,... | collective-permute-start | bytes 1572872 | tf_op jit(solution)/shard_map/ppermute | solution.py:37
  67.8 26.0 %collective-permute-start.14 = (bf16[1024,256]{1,0:T(8,128)(2,1)S(1)}, bf16[1024,256]{1,0:T(8,128)(2,1)}, u32[]{:S(2)}, u32[]{:S(2)}) collective-permute-start(bf16[1024,256]{1,0:T(8,128)(2,1)S(1)} %get-tuple-element.52), channel_id=1, source_target_pairs={{2,0},{4,2},{6,4},{8,6},{10,8},{12,10},{14,12},{16,14},{18,16},{20... | collective-permute-start | bytes 1572872 | tf_op jit(solution)/shard_map/ppermute | solution.py:37
  68.0 33.6 %all-to-all-start.1 = ((bf16[16,128,256]{2,1,0:T(8,128)(2,1)}), bf16[16,128,256]{2,1,0:T(8,128)(2,1)S(1)}, u32[]{:S(2)}, u32[]{:S(2)}) async-start(bf16[16,128,256]{2,1,0:T(8,128)(2,1)} %get-tuple-element.59), calls=%async_computation.1 | async-start | bytes 2097152 | tf_op jit(solution)/shard_map/all_to_all | solution.py:394
  75.9 17.9 %collective-permute-start.12 = (f32[144,256]{1,0:T(8,128)S(1)}, f32[144,256]{1,0:T(8,128)S(1)}, u32[]{:S(2)}, u32[]{:S(2)}) collective-permute-start(f32[144,256]{1,0:T(8,128)S(1)} %add_add_fusion), channel_id=1, source_target_pairs={{0,4},{2,6},{4,0},{6,2},{8,12},{10,14},{12,8},{14,10},{16,20},{18,... | collective-permute-start | bytes 442376 | tf_op jit(solution)/shard_map/ppermute | solution.py:42
  93.8 2.1 %collective-permute-start.15 = (f32[288,256]{1,0:T(8,128)S(1)}, f32[288,256]{1,0:T(8,128)S(1)}, u32[]{:S(2)}, u32[]{:S(2)}) collective-permute-start(f32[288,256]{1,0:T(8,128)S(1)} %maximum_select_fusion.mine_ref), channel_id=1, source_target_pairs={{0,2},{2,0},{4,6},{6,4},{8,10},{10,8},{12,14},{14,12},{16,18},{18,... | collective-permute-start | bytes 884744 | tf_op jit(solution)/shard_map/ppermute | solution.py:42
  (14 other events, 52.1 us)

commit v5 on v4

--- a/solution.py
+++ b/solution.py
@@ -88,26 +88,17 @@
     return pltpu.SemaphoreType.DMA((count,))
 
 
-def gather_kernel(hid_ref, features_ref, send_ref, out_ref, hot, block, lists, picked, sems):
+def gather_kernel(block_ref, send_ref, out_ref, hot, picked, sems):
     peers, slots, rows = out_ref.shape
-    nodes = features_ref.shape[1]
-    copies = Copies(sems)
-    start = pl.multiple_of(hid_ref[0] * rows, rows)
-    lists_copy = copies.start(send_ref, lists)
-    block_copy = copies.start(features_ref.at[pl.ds(start, rows), :], block)
-    lists_copy.wait()
-    send_t = lists[...].T
+    copies, sent = Copies(sems), []
+    send_t = send_ref[...].T
+    block_t = block_ref[...].T
     group = 2
-    slots_by_nodes(hot, send_t, 0, 0, group)
-    block_copy.wait()
-    sent = []
-    block_t = block[...].T
     for p in range(0, peers, group):
+        slots_by_nodes(hot, send_t, 0, p, group)
         part = dot(hot[p * slots : (p + group) * slots, :], block_t)
         picked[p : p + group] = part.astype(BF16).reshape(group, slots, rows)
         sent.append(copies.start(picked.at[pl.ds(p, group)], out_ref.at[pl.ds(p, group)]))
-        if p + group < peers:
-            slots_by_nodes(hot, send_t, 0, p + group, group)
     for copy in sent:
         copy.wait()
 
@@ -182,9 +173,8 @@
     weights, biases, cotangents = ([next(take) for _ in range(n_hid)] for _ in range(3))
     aggs, recv_ref, weight_ref, counts_ref = (next(take) for _ in range(4))
     earlier_ref = next(take) if first else None
-    output_ref, part_ref, back_ref, message_ref, held, earlier, hot, sems = take
+    output_ref, part_ref, back_ref, message_ref, held, held_message, hot, sems = take
     copies = Copies(sems)
-    earlier_in = copies.start(earlier_ref, earlier) if first else None
     width, nodes = output_ref.shape
     rows = back_ref.shape[1]
     cotangents_in = [
@@ -213,20 +203,20 @@
     peers, slots, _ = message_ref.shape
     weights_t = masked_weights(weight_ref[...], counts_ref[...]).T
     recv_t = recv_ref[...].T
-    if first:
-        earlier_in.wait()
+    group = 8
     sent = []
-    group = 4
     for p in range(0, peers, group):
         slots_by_nodes(hot, recv_t, first, p, group)
         picked = dot(hot[p * slots : (p + group) * slots, :], back)
         for n in range(group):
             row = picked[n * slots : (n + 1) * slots] * weights_t[:, p + n : p + n + 1]
             if first:
-                row = row + earlier[p + n].astype(F32)
-            earlier[p + n] = row.astype(BF16)
-        lines = pl.ds(p, group)
-        sent.append(copies.start(earlier.at[lines], message_ref.at[lines]))
+                held_message[p + n] = (row + earlier_ref[p + n].astype(F32)).astype(BF16)
+            else:
+                message_ref[p + n] = row.astype(BF16)
+        if first:
+            lines = pl.ds(p, group)
+            sent.append(copies.start(held_message.at[lines], message_ref.at[lines]))
     for copy in sent:
         copy.wait()
 
@@ -305,15 +295,8 @@
     (outgoing,) = call(
         gather_kernel,
         [out((peers, slots, rows), BF16)],
-        [hid, (HBM, features), (HBM, send_rows[0])],
-        [
-            vmem((lists, nodes), BF16),
-            vmem((rows, nodes), BF16),
-            vmem((peers, slots), jnp.int32),
-            vmem((peers, slots, rows), BF16),
-            sems(peers + 2),
-        ],
-        mib=58,
+        [(VMEM, own), send],
+        [vmem((lists, nodes), BF16), vmem((peers, slots, rows), BF16), sems(peers)],
         place=HBM,
     )
     arrived = lax.all_to_all(outgoing, "dom", split_axis=0, concat_axis=0, tiled=True)
@@ -365,7 +348,7 @@
                 *[(HBM, c) for c in cotangents],
                 (VMEM, aggs),
                 *edges,
-                *([(HBM, message)] if cut else []),
+                *([(VMEM, message)] if cut else []),
             ],
             [
                 vmem((n_hid, width, size), BF16),
@@ -375,7 +358,7 @@
             ],
             us=2,
             mib=24,
-            place=[VMEM, VMEM, VMEM, HBM],
+            place=[VMEM, VMEM, VMEM, HBM if cut else VMEM],
         )
         outputs.append(output)
         parts.append(part)

time: 105 us -> 106 us (level)
    unnamed x42 -> x44, local copies, waits for them, and re-layouts: 11.8 us -> 14 us
    dynamic_slice x1, local copies, waits for them, and re-layouts: 1.15 us -> 0.03 us  [on_device(): own = lax.dynamic_slice_in_dim(features, hid[1][0] * rows, rows, 0)]
    ppermute x7, waiting for transfers between devices: 14.7 us -> 13.6 us  [swapped(): return lax.ppermute(block, axis, [(i, i ^ bit) for i in range(size)])]
where the time goes in v5:
time: 106 us; the launch traced here: 105 us
  waiting for transfers between devices  37.6 us (35%)
  starting transfers between devices  28.2 us (27%)
  Pallas kernels  21.3 us (20%)
  local copies, waits for them, and re-layouts  14.1 us (13%)
  other arithmetic  2.74 us (3%)
    pallas_call x9, Pallas kernels, call(): pl.pallas_call(kernel, out_shape=tuple(outs), in_specs=[place for place,...  21.3 us
    unnamed x44, local copies, waits for them, and re-layouts  14 us
    ppermute x7, waiting for transfers between devices, swapped(): return lax.ppermute(block, axis, [(i, i ^ bit) for i in range(size)])  13.6 us
    ppermute x9, waiting for transfers between devices, shifted(): lax.ppermute(block, axis, [((i + distance) % size, i) for i in range(size)])  10.5 us
    all_to_all x1, waiting for transfers between devices, on_device(): lax.all_to_all(outgoing, 'dom', split_axis=0, concat_axis=0, tiled=True)  8.39 us
    all_to_all x1, starting transfers between devices, on_device(): lax.all_to_all(message, 'dom', split_axis=0, concat_axis=0, tiled=True)  8 us
    all_to_all x1, starting transfers between devices, on_device(): lax.all_to_all(outgoing, 'dom', split_axis=0, concat_axis=0, tiled=True)  7.72 us
    ppermute x9, starting transfers between devices, shifted(): lax.ppermute(block, axis, [((i + distance) % size, i) for i in range(size)])  6.31 us
  transfers between devices with their start and end apart: 18, of which 8 were waited for; matrix products, arithmetic and copies ran while one was open for 2% of the time, Pallas kernels for 13%

profile of v5, /device:TPU:31, one launch (start us, length us, event | category | flops | bytes accessed | tf_op | source)
XLA Modules:
  0.0 104.9 jit_solution(2876383847865801326)
XLA Ops:
  0.7 1.2 %copy-done = bf16[512,1024]{1,0:T(8,128)(2,1)S(1)} copy-done((bf16[512,1024]{1,0:T(8,128)(2,1)S(1)}, bf16[512,1024]{1,0:T(8,128)(2,1)}, u32[]{:S(2)}) %copy-start) | copy-done | bytes 1048600
  3.4 2.3 %shard_map.130 = bf16[16,128,256]{2,1,0:T(8,128)(2,1)} custom-call(bf16[256,1024]{1,0:T(8,128)(2,1)S(1)} %constant_dynamic-slice_fusion.own_ref.block_ref, s32[16,128]{1,0:T(8,128)S(1)} %bitcast.21), custom_call_target="tpu_custom_call" | custom-call | flops 1000000000 | bytes 1 | tf_op jit(solution)/shard_map/pallas_call | solution.py:20
  5.7 7.7 %all-to-all-start = ((bf16[16,128,256]{2,1,0:T(8,128)(2,1)}), bf16[16,128,256]{2,1,0:T(8,128)(2,1)S(1)}, u32[]{:S(2)}, u32[]{:S(2)}) async-start(bf16[16,128,256]{2,1,0:T(8,128)(2,1)} %shard_map.130), calls=%async_computation | async-start | bytes 2097152 | tf_op jit(solution)/shard_map/all_to_all | solution.py:302
  14.4 1.5 %collective-permute-start.3 = (f32[256]{0:T(256)S(1)}, f32[256]{0:T(256)S(1)}, u32[]{:S(2)}, u32[]{:S(2)}) collective-permute-start(f32[256]{0:T(256)S(1)} %copy-done.16), channel_id=1, source_target_pairs={{1,0},{0,1},{3,2},{2,3},{5,4},{4,5},{7,6},{6,7},{9,8},{8,9},{11,10... | collective-permute-start | bytes 3080 | tf_op jit(solution)/shard_map/ppermute | solution.py:37
  16.0 2.8 %copy-done.1 = bf16[3072,1024]{1,0:T(8,128)(2,1)S(1)} copy-done((bf16[3072,1024]{1,0:T(8,128)(2,1)S(1)}, bf16[3072,1024]{1,0:T(8,128)(2,1)}, u32[]{:S(2)}) %copy-start.1) | copy-done | bytes 6291480
  20.8 3.0 %shard_map.129 = f32[1024,256]{1,0:T(8,128)S(1)} custom-call(s32[12,4]{1,0:T(8,128)S(1)} %copy.14.live_ref, bf16[3072,1024]{1,0:T(8,128)(2,1)S(1)} %copy-done.1, bf16[256,1024]{1,0:T(8,128)(2,1)S(1)} %copy-done.8, bf16[256,1024]{1,0:T(8,128)(2,1)S(1)} %copy-done.4, bf16[256,1024]{1,0:T(8,128)(2,1)} %collective-permute-done.1.after_ref), custom_call_target="tpu_custom_call" | custom-call | flops 60000002048 | bytes 1 | tf_op jit(solution)/shard_map/pallas_call | solution.py:20
  24.6 3.6 %collective-permute-done.4.refs_5_ = bf16[256,1024]{1,0:T(8,128)(2,1)S(1)} collective-permute-done((bf16[256,1024]{1,0:T(8,128)(2,1)}, bf16[256,1024]{1,0:T(8,128)(2,1)S(1)}, u32[]{:S(2)}, u32[]{:S(2)}) %collective-permute-start.4) | collective-permute-done | bytes 524320 | tf_op jit(solution)/shard_map/ppermute | solution.py:37
  28.9 8.4 %all-to-all-done.arrived_ref = bf16[16,128,256]{2,1,0:T(8,128)(2,1)S(1)} async-done(((bf16[16,128,256]{2,1,0:T(8,128)(2,1)}), bf16[16,128,256]{2,1,0:T(8,128)(2,1)S(1)}, u32[]{:S(2)}, u32[]{:S(2)}) %all-to-all-start) | async-done | bytes 1048608 | tf_op jit(solution)/shard_map/all_to_all | solution.py:302
  37.3 1.9 %shard_map.131 = f32[1024,256]{1,0:T(8,128)S(1)} custom-call(s32[16,128]{1,0:T(8,128)S(1)} %bitcast.15, f32[16,128]{1,0:T(8,128)S(1)} %bitcast.18, s32[16,1]{1,0:T(8,128)S(1)} %copy.15.counts_ref.refs_9_, bf16[16,128,256]{2,1,0:T(8,128)(2,1)S(1)} %all-to-all-done.arrived_ref), custom_call_target="tpu_custom_call" | custom-call | flops 4000000000 | bytes 1 | tf_op jit(solution)/shard_map/pallas_call | solution.py:20
  39.5 1.4 %collective-permute-start.6 = (bf16[512,256]{1,0:T(8,128)(2,1)S(1)}, bf16[512,256]{1,0:T(8,128)(2,1)S(1)}, u32[]{:S(2)}, u32[]{:S(2)}) collective-permute-start(bf16[512,256]{1,0:T(8,128)(2,1)S(1)} %get-tuple-element.48), channel_id=1, source_target_pairs={{1,0},{0,1},{3,2},{2,3},{5,4},{4,5},{7,6},{6,7},{9,8},{8,9},{11,10... | collective-permute-start | bytes 786440 | tf_op jit(solution)/shard_map/ppermute | solution.py:37
  41.0 6.2 %collective-permute-done.5 = bf16[512,256]{1,0:T(8,128)(2,1)S(1)} collective-permute-done((bf16[512,256]{1,0:T(8,128)(2,1)S(1)}, bf16[512,256]{1,0:T(8,128)(2,1)S(1)}, u32[]{:S(2)}, u32[]{:S(2)}) %collective-permute-start.5) | collective-permute-done | bytes 262176 | tf_op jit(solution)/shard_map/ppermute | solution.py:37
  49.3 2.8 %shard_map.132 = (bf16[256,512]{1,0:T(8,128)(2,1)S(1)}, f32[576,256]{1,0:T(8,128)S(1)}, bf16[512,256]{1,0:T(8,128)(2,1)S(1)}, bf16[16,128,256]{2,1,0:T(8,128)(2,1)S(1)}) custom-call(s32[1]{0:T(128)} %bitcast.hid_ref, bf16[512,256]{1,0:T(8,128)(2,1)S(1)} %copy-done.9, bf16[512,256]{1,0:T(8,128)(2,1)S(1)} %copy-done.11, f32[1,256]{1,0:T(1,128)S(1)} %bitcast.23, ...), custom_call_target="tpu_custom_call" | custom-call | flops 2000000000 | bytes 1 | tf_op jit(solution)/shard_map/pallas_call | solution.py:20
  52.9 4.0 %shard_map.133 = (bf16[256,512]{1,0:T(8,128)(2,1)S(1)}, f32[576,256]{1,0:T(8,128)S(1)}, bf16[512,256]{1,0:T(8,128)(2,1)S(1)}, bf16[16,128,256]{2,1,0:T(8,128)(2,1)}) custom-call(s32[1]{0:T(128)} %bitcast.hid_ref, bf16[512,256]{1,0:T(8,128)(2,1)S(1)} %copy-done.9, bf16[512,256]{1,0:T(8,128)(2,1)S(1)} %copy-done.11, f32[1,256]{1,0:T(1,128)S(1)} %bitcast.24, ...), custom_call_target="tpu_custom_call" | custom-call | flops 2000000000 | bytes 1 | tf_op jit(solution)/shard_map/pallas_call | solution.py:20
  57.0 1.1 %collective-permute-start.7 = (bf16[288,256]{1,0:T(8,128)(2,1)S(1)}, bf16[288,256]{1,0:T(8,128)(2,1)S(1)}, u32[]{:S(2)}, u32[]{:S(2)}) collective-permute-start(bf16[288,256]{1,0:T(8,128)(2,1)S(1)} %select_convert_fusion), channel_id=1, source_target_pairs={{0,2},{2,0},{4,6},{6,4},{8,10},{10,8},{12,14},{14,12},{16,18},{18,... | collective-permute-start | bytes 442376 | tf_op jit(solution)/shard_map/ppermute | solution.py:42
  59.3 2.8 %shard_map.134 = (bf16[1024,256]{1,0:T(8,128)(2,1)}, bf16[1024,256]{1,0:T(8,128)(2,1)}) custom-call(s32[12,4]{1,0:T(8,128)S(1)} %copy.14.live_ref, bf16[3072,1024]{1,0:T(8,128)(2,1)S(1)} %bitcast.14, bf16[1024,256]{1,0:T(8,128)(2,1)S(1)} %constant_dynamic-update-slice_fusion.back_ref), custom_call_target="tpu_custom_call" | custom-call | flops 2000000000 | bytes 1 | tf_op jit(solution)/shard_map/pallas_call | solution.py:20
  62.5 2.7 %collective-permute-start.10 = (bf16[144,256]{1,0:T(8,128)(2,1)S(1)}, bf16[144,256]{1,0:T(8,128)(2,1)S(1)}, u32[]{:S(2)}, u32[]{:S(2)}) collective-permute-start(bf16[144,256]{1,0:T(8,128)(2,1)S(1)} %convert_add_fusion.2), channel_id=1, source_target_pairs={{0,16},{2,18},{4,20},{6,22},{8,24},{10,26},{12,28},{14,30},{16,0},... | collective-permute-start | bytes 221192 | tf_op jit(solution)/shard_map/ppermute | solution.py:42
  66.1 2.5 %collective-permute-start.13 = (bf16[1024,256]{1,0:T(8,128)(2,1)}, bf16[1024,256]{1,0:T(8,128)(2,1)}, u32[]{:S(2)}, u32[]{:S(2)}) collective-permute-start(bf16[1024,256]{1,0:T(8,128)(2,1)} %get-tuple-element.53), channel_id=1, source_target_pairs={{30,0},{0,2},{2,4},{4,6},{6,8},{8,10},{10,12},{12,14},{14,16},{16,... | collective-permute-start | bytes 1572872 | tf_op jit(solution)/shard_map/ppermute | solution.py:37
  68.5 8.0 %all-to-all-start.1 = ((bf16[16,128,256]{2,1,0:T(8,128)(2,1)}), bf16[16,128,256]{2,1,0:T(8,128)(2,1)S(1)}, u32[]{:S(2)}, u32[]{:S(2)}) async-start(bf16[16,128,256]{2,1,0:T(8,128)(2,1)} %get-tuple-element.59), calls=%async_computation.1 | async-start | bytes 2097152 | tf_op jit(solution)/shard_map/all_to_all | solution.py:377
  77.0 2.8 %copy-done.2 = bf16[3072,1024]{1,0:T(8,128)(2,1)S(1)} copy-done((bf16[3072,1024]{1,0:T(8,128)(2,1)S(1)}, bf16[3072,1024]{1,0:T(8,128)(2,1)}, u32[]{:S(2)}) %copy-start.2) | copy-done | bytes 6291480
  79.7 1.4 %shard_map.135 = f32[1024,256]{1,0:T(8,128)S(1)} custom-call(s32[12,4]{1,0:T(8,128)S(1)} %copy.14.live_ref, bf16[3072,1024]{1,0:T(8,128)(2,1)S(1)} %copy-done.2, bf16[1024,256]{1,0:T(8,128)(2,1)S(1)} %constant_dynamic-update-slice_fusion.back_ref), custom_call_target="tpu_custom_call" | custom-call | flops 1000000000 | bytes 1 | tf_op jit(solution)/shard_map/pallas_call | solution.py:20
  82.0 12.2 %collective-permute-done.12 = f32[144,256]{1,0:T(8,128)S(1)} collective-permute-done((f32[144,256]{1,0:T(8,128)S(1)}, f32[144,256]{1,0:T(8,128)S(1)}, u32[]{:S(2)}, u32[]{:S(2)}) %collective-permute-start.12) | collective-permute-done | bytes 147488 | tf_op jit(solution)/shard_map/ppermute | solution.py:42
  95.3 1.3 %convert_add_fusion.dense_ref = f32[1024,256]{1,0:T(8,128)S(1)} fusion(bf16[1024,256]{1,0:T(8,128)(2,1)} %collective-permute-done.14, f32[1024,256]{1,0:T(8,128)S(1)} %shard_map.135, bf16[1024,256]{1,0:T(8,128)(2,1)} %collective-permute-done.13), kind=kLoop, calls=%fused_computation | loop fusion | flops 1048576 | bytes 3145728 | tf_op jit(solution)/shard_map/add | solution.py:393
  97.5 5.1 %all-to-all-done.1.returned_ref = bf16[16,128,256]{2,1,0:T(8,128)(2,1)S(1)} async-done(((bf16[16,128,256]{2,1,0:T(8,128)(2,1)}), bf16[16,128,256]{2,1,0:T(8,128)(2,1)S(1)}, u32[]{:S(2)}, u32[]{:S(2)}) %all-to-all-start.1) | async-done | bytes 1048608 | tf_op jit(solution)/shard_map/all_to_all | solution.py:377
  102.6 2.3 %shard_map.136 = bf16[256,1024]{1,0:T(8,128)(2,1)} custom-call(s32[16,128]{1,0:T(8,128)S(1)} %bitcast.22, bf16[16,128,256]{2,1,0:T(8,128)(2,1)S(1)} %all-to-all-done.1.returned_ref, f32[1024,256]{1,0:T(8,128)S(1)} %convert_add_fusion.dense_ref), custom_call_target="tpu_custom_call" | custom-call | flops 1000000000 | bytes 1 | tf_op jit(solution)/shard_map/pallas_call | solution.py:20
  (81 shorter events, 15.0 us)
Async XLA Ops:
  0.7 12.9 %copy-start.18 = (s32[1,16]{1,0:T(1,128)S(1)}, s32[1,16]{1,0:T(1,128)}, u32[]{:S(2)}) copy-start(s32[1,16]{1,0:T(1,128)} %param.17) | copy-start | bytes 196
  0.7 13.8 %copy-start.9 = (bf16[512,256]{1,0:T(8,128)(2,1)S(1)}, bf16[512,256]{1,0:T(8,128)(2,1)}, u32[]{:S(2)}) copy-start(bf16[512,256]{1,0:T(8,128)(2,1)} %refs_0_.1) | copy-start | bytes 786436
  0.7 13.8 %copy-start.16 = (f32[256]{0:T(256)S(1)}, f32[256]{0:T(256)}, u32[]{:S(2)}) copy-start(f32[256]{0:T(256)} %param.18) | copy-start | bytes 3076
  1.9 14.1 %copy-start.3 = (bf16[256,1024]{1,0:T(8,128)(2,1)}, bf16[256,1024]{1,0:T(8,128)(2,1)S(1)}, u32[]{:S(2)}) copy-start(bf16[256,1024]{1,0:T(8,128)(2,1)S(1)} %constant_dynamic-slice_fusion.own_ref.block_ref) | copy-start | bytes 1572868
  1.9 11.7 %collective-permute-start = (bf16[256,1024]{1,0:T(8,128)(2,1)S(1)}, bf16[256,1024]{1,0:T(8,128)(2,1)S(1)}, u32[]{:S(2)}, u32[]{:S(2)}) collective-permute-start(bf16[256,1024]{1,0:T(8,128)(2,1)S(1)} %constant_dynamic-slice_fusion.own_ref.block_ref), channel_id=1, source_target_pairs={{30,0},{0,2},{2,4},{4,6},{6,8},{8,10},{10,12},{12,14},{14,16},{16,... | collective-permute-start | bytes 1572872 | tf_op jit(solution)/shard_map/ppermute | solution.py:37
  2.4 13.6 %collective-permute-start.1 = (bf16[256,1024]{1,0:T(8,128)(2,1)S(1)}, bf16[256,1024]{1,0:T(8,128)(2,1)}, u32[]{:S(2)}, u32[]{:S(2)}) collective-permute-start(bf16[256,1024]{1,0:T(8,128)(2,1)S(1)} %constant_dynamic-slice_fusion.own_ref.block_ref), channel_id=1, source_target_pairs={{2,0},{4,2},{6,4},{8,6},{10,8},{12,10},{14,12},{16,14},{18,16},{20... | collective-permute-start | bytes 1572872 | tf_op jit(solution)/shard_map/ppermute | solution.py:37
  5.7 31.6 %all-to-all-start = ((bf16[16,128,256]{2,1,0:T(8,128)(2,1)}), bf16[16,128,256]{2,1,0:T(8,128)(2,1)S(1)}, u32[]{:S(2)}, u32[]{:S(2)}) async-start(bf16[16,128,256]{2,1,0:T(8,128)(2,1)} %shard_map.130), calls=%async_computation | async-start | bytes 2097152 | tf_op jit(solution)/shard_map/all_to_all | solution.py:302
  13.4 23.9 %copy-start.13 = (f32[1,16,128]{2,1,0:T(8,128)S(1)}, f32[1,16,128]{2,1,0:T(8,128)}, u32[]{:S(2)}) copy-start(f32[1,16,128]{2,1,0:T(8,128)} %param.16) | copy-start | bytes 24580
  13.5 23.8 %copy-start.12 = (s32[1,16,128]{2,1,0:T(8,128)S(1)}, s32[1,16,128]{2,1,0:T(8,128)}, u32[]{:S(2)}) copy-start(s32[1,16,128]{2,1,0:T(8,128)} %param.15) | copy-start | bytes 24580
  14.4 9.4 %collective-permute-start.2 = (bf16[512,256]{1,0:T(8,128)(2,1)S(1)}, bf16[512,256]{1,0:T(8,128)(2,1)S(1)}, u32[]{:S(2)}, u32[]{:S(2)}) collective-permute-start(bf16[512,256]{1,0:T(8,128)(2,1)S(1)} %copy-done.9), channel_id=1, source_target_pairs={{1,0},{0,1},{3,2},{2,3},{5,4},{4,5},{7,6},{6,7},{9,8},{8,9},{11,10... | collective-permute-start | bytes 786440 | tf_op jit(solution)/shard_map/ppermute | solution.py:37
  14.4 9.4 %collective-permute-start.3 = (f32[256]{0:T(256)S(1)}, f32[256]{0:T(256)S(1)}, u32[]{:S(2)}, u32[]{:S(2)}) collective-permute-start(f32[256]{0:T(256)S(1)} %copy-done.16), channel_id=1, source_target_pairs={{1,0},{0,1},{3,2},{2,3},{5,4},{4,5},{7,6},{6,7},{9,8},{8,9},{11,10... | collective-permute-start | bytes 3080 | tf_op jit(solution)/shard_map/ppermute | solution.py:37
  15.9 12.2 %collective-permute-start.4 = (bf16[256,1024]{1,0:T(8,128)(2,1)}, bf16[256,1024]{1,0:T(8,128)(2,1)S(1)}, u32[]{:S(2)}, u32[]{:S(2)}) collective-permute-start(bf16[256,1024]{1,0:T(8,128)(2,1)} %refs_4_.1), channel_id=1, source_target_pairs={{1,0},{0,1},{3,2},{2,3},{5,4},{4,5},{7,6},{6,7},{9,8},{8,9},{11,10... | collective-permute-start | bytes 1572872 | tf_op jit(solution)/shard_map/ppermute | solution.py:37
  39.4 7.8 %collective-permute-start.5 = (bf16[512,256]{1,0:T(8,128)(2,1)S(1)}, bf16[512,256]{1,0:T(8,128)(2,1)S(1)}, u32[]{:S(2)}, u32[]{:S(2)}) collective-permute-start(bf16[512,256]{1,0:T(8,128)(2,1)S(1)} %get-tuple-element.67), channel_id=1, source_target_pairs={{1,0},{0,1},{3,2},{2,3},{5,4},{4,5},{7,6},{6,7},{9,8},{8,9},{11,10... | collective-permute-start | bytes 786440 | tf_op jit(solution)/shard_map/ppermute | solution.py:37
  39.5 13.3 %collective-permute-start.6 = (bf16[512,256]{1,0:T(8,128)(2,1)S(1)}, bf16[512,256]{1,0:T(8,128)(2,1)S(1)}, u32[]{:S(2)}, u32[]{:S(2)}) collective-permute-start(bf16[512,256]{1,0:T(8,128)(2,1)S(1)} %get-tuple-element.48), channel_id=1, source_target_pairs={{1,0},{0,1},{3,2},{2,3},{5,4},{4,5},{7,6},{6,7},{9,8},{8,9},{11,10... | collective-permute-start | bytes 786440 | tf_op jit(solution)/shard_map/ppermute | solution.py:37
  57.0 2.1 %collective-permute-start.7 = (bf16[288,256]{1,0:T(8,128)(2,1)S(1)}, bf16[288,256]{1,0:T(8,128)(2,1)S(1)}, u32[]{:S(2)}, u32[]{:S(2)}) collective-permute-start(bf16[288,256]{1,0:T(8,128)(2,1)S(1)} %select_convert_fusion), channel_id=1, source_target_pairs={{0,2},{2,0},{4,6},{6,4},{8,10},{10,8},{12,14},{14,12},{16,18},{18,... | collective-permute-start | bytes 442376 | tf_op jit(solution)/shard_map/ppermute | solution.py:42
  59.2 3.3 %collective-permute-start.8 = (bf16[144,256]{1,0:T(8,128)(2,1)S(1)}, bf16[144,256]{1,0:T(8,128)(2,1)S(1)}, u32[]{:S(2)}, u32[]{:S(2)}) collective-permute-start(bf16[144,256]{1,0:T(8,128)(2,1)S(1)} %select_convert_fusion.1), channel_id=1, source_target_pairs={{0,4},{2,6},{4,0},{6,2},{8,12},{10,14},{12,8},{14,10},{16,20},{18,... | collective-permute-start | bytes 221192 | tf_op jit(solution)/shard_map/ppermute | solution.py:42
  62.5 14.1 %collective-permute-start.11 = (bf16[144,256]{1,0:T(8,128)(2,1)S(1)}, bf16[144,256]{1,0:T(8,128)(2,1)S(1)}, u32[]{:S(2)}, u32[]{:S(2)}) collective-permute-start(bf16[144,256]{1,0:T(8,128)(2,1)S(1)} %convert_add_fusion.2), channel_id=1, source_target_pairs={{0,24},{2,26},{4,28},{6,30},{8,16},{10,18},{12,20},{14,22},{16,8},... | collective-permute-start | bytes 221192 | tf_op jit(solution)/shard_map/ppermute | solution.py:42
  62.5 14.0 %collective-permute-start.10 = (bf16[144,256]{1,0:T(8,128)(2,1)S(1)}, bf16[144,256]{1,0:T(8,128)(2,1)S(1)}, u32[]{:S(2)}, u32[]{:S(2)}) collective-permute-start(bf16[144,256]{1,0:T(8,128)(2,1)S(1)} %convert_add_fusion.2), channel_id=1, source_target_pairs={{0,16},{2,18},{4,20},{6,22},{8,24},{10,26},{12,28},{14,30},{16,0},... | collective-permute-start | bytes 221192 | tf_op jit(solution)/shard_map/ppermute | solution.py:42
  65.2 11.3 %collective-permute-start.9 = (bf16[144,256]{1,0:T(8,128)(2,1)S(1)}, bf16[144,256]{1,0:T(8,128)(2,1)S(1)}, u32[]{:S(2)}, u32[]{:S(2)}) collective-permute-start(bf16[144,256]{1,0:T(8,128)(2,1)S(1)} %convert_add_fusion.2), channel_id=1, source_target_pairs={{0,8},{2,10},{4,12},{6,14},{8,0},{10,2},{12,4},{14,6},{16,24},{18,... | collective-permute-start | bytes 221192 | tf_op jit(solution)/shard_map/ppermute | solution.py:42
  66.1 28.2 %collective-permute-start.13 = (bf16[1024,256]{1,0:T(8,128)(2,1)}, bf16[1024,256]{1,0:T(8,128)(2,1)}, u32[]{:S(2)}, u32[]{:S(2)}) collective-permute-start(bf16[1024,256]{1,0:T(8,128)(2,1)} %get-tuple-element.53), channel_id=1, source_target_pairs={{30,0},{0,2},{2,4},{4,6},{6,8},{8,10},{10,12},{12,14},{14,16},{16,... | collective-permute-start | bytes 1572872 | tf_op jit(solution)/shard_map/ppermute | solution.py:37
  68.5 25.7 %collective-permute-start.14 = (bf16[1024,256]{1,0:T(8,128)(2,1)}, bf16[1024,256]{1,0:T(8,128)(2,1)}, u32[]{:S(2)}, u32[]{:S(2)}) collective-permute-start(bf16[1024,256]{1,0:T(8,128)(2,1)} %get-tuple-element.52), channel_id=1, source_target_pairs={{2,0},{4,2},{6,4},{8,6},{10,8},{12,10},{14,12},{16,14},{18,16},{20... | collective-permute-start | bytes 1572872 | tf_op jit(solution)/shard_map/ppermute | solution.py:37
  68.5 34.1 %all-to-all-start.1 = ((bf16[16,128,256]{2,1,0:T(8,128)(2,1)}), bf16[16,128,256]{2,1,0:T(8,128)(2,1)S(1)}, u32[]{:S(2)}, u32[]{:S(2)}) async-start(bf16[16,128,256]{2,1,0:T(8,128)(2,1)} %get-tuple-element.59), calls=%async_computation.1 | async-start | bytes 2097152 | tf_op jit(solution)/shard_map/all_to_all | solution.py:377
  76.6 17.6 %collective-permute-start.12 = (f32[144,256]{1,0:T(8,128)S(1)}, f32[144,256]{1,0:T(8,128)S(1)}, u32[]{:S(2)}, u32[]{:S(2)}) collective-permute-start(f32[144,256]{1,0:T(8,128)S(1)} %add_add_fusion), channel_id=1, source_target_pairs={{0,4},{2,6},{4,0},{6,2},{8,12},{10,14},{12,8},{14,10},{16,20},{18,... | collective-permute-start | bytes 442376 | tf_op jit(solution)/shard_map/ppermute | solution.py:42
  94.3 2.4 %collective-permute-start.15 = (f32[288,256]{1,0:T(8,128)S(1)}, f32[288,256]{1,0:T(8,128)S(1)}, u32[]{:S(2)}, u32[]{:S(2)}) collective-permute-start(f32[288,256]{1,0:T(8,128)S(1)} %maximum_select_fusion.mine_ref), channel_id=1, source_target_pairs={{0,2},{2,0},{4,6},{6,4},{8,10},{10,8},{12,14},{14,12},{16,18},{18,... | collective-permute-start | bytes 884744 | tf_op jit(solution)/shard_map/ppermute | solution.py:42
  (15 other events, 45.4 us)

commit v6 on v4

--- a/solution.py
+++ b/solution.py
@@ -182,9 +182,8 @@
     weights, biases, cotangents = ([next(take) for _ in range(n_hid)] for _ in range(3))
     aggs, recv_ref, weight_ref, counts_ref = (next(take) for _ in range(4))
     earlier_ref = next(take) if first else None
-    output_ref, part_ref, back_ref, message_ref, held, earlier, hot, sems = take
+    output_ref, part_ref, back_ref, message_ref, held, held_message, hot, sems = take
     copies = Copies(sems)
-    earlier_in = copies.start(earlier_ref, earlier) if first else None
     width, nodes = output_ref.shape
     rows = back_ref.shape[1]
     cotangents_in = [
@@ -213,20 +212,20 @@
     peers, slots, _ = message_ref.shape
     weights_t = masked_weights(weight_ref[...], counts_ref[...]).T
     recv_t = recv_ref[...].T
-    if first:
-        earlier_in.wait()
+    group = 8
     sent = []
-    group = 4
     for p in range(0, peers, group):
         slots_by_nodes(hot, recv_t, first, p, group)
         picked = dot(hot[p * slots : (p + group) * slots, :], back)
         for n in range(group):
             row = picked[n * slots : (n + 1) * slots] * weights_t[:, p + n : p + n + 1]
             if first:
-                row = row + earlier[p + n].astype(F32)
-            earlier[p + n] = row.astype(BF16)
-        lines = pl.ds(p, group)
-        sent.append(copies.start(earlier.at[lines], message_ref.at[lines]))
+                held_message[p + n] = (row + earlier_ref[p + n].astype(F32)).astype(BF16)
+            else:
+                message_ref[p + n] = row.astype(BF16)
+        if first:
+            lines = pl.ds(p, group)
+            sent.append(copies.start(held_message.at[lines], message_ref.at[lines]))
     for copy in sent:
         copy.wait()
 
@@ -365,7 +364,7 @@
                 *[(HBM, c) for c in cotangents],
                 (VMEM, aggs),
                 *edges,
-                *([(HBM, message)] if cut else []),
+                *([(VMEM, message)] if cut else []),
             ],
             [
                 vmem((n_hid, width, size), BF16),
@@ -375,7 +374,7 @@
             ],
             us=2,
             mib=24,
-            place=[VMEM, VMEM, VMEM, HBM],
+            place=[VMEM, VMEM, VMEM, HBM if cut else VMEM],
         )
         outputs.append(output)
         parts.append(part)

time: 105 us -> 104 us (level)
  Pallas kernels: 21.2 us -> 20.1 us
    pallas_call x9, Pallas kernels: 21.2 us -> 20.1 us  [call(): pl.pallas_call(kernel, out_shape=tuple(outs), in_specs=[place for place,...]
    ppermute x9, waiting for transfers between devices: 11.4 us -> 12.5 us  [shifted(): lax.ppermute(block, axis, [((i + distance) % size, i) for i in range(size)])]
  transfers between devices with their start and end apart: 18 -> 18, of which waited for: 8 -> 8; matrix products, arithmetic and copies ran while one was open for 2% -> 2% of each run, Pallas kernels for 13% -> 12%
where the time goes in v6:
time: 104 us
  waiting for transfers between devices  39.4 us (38%)
  starting transfers between devices  27.6 us (27%)
  Pallas kernels  20.1 us (19%)
  local copies, waits for them, and re-layouts  13.1 us (13%)
  other arithmetic  2.74 us (3%)
    pallas_call x9, Pallas kernels, call(): pl.pallas_call(kernel, out_shape=tuple(outs), in_specs=[place for place,...  20.1 us
    ppermute x7, waiting for transfers between devices, swapped(): return lax.ppermute(block, axis, [(i, i ^ bit) for i in range(size)])  14.9 us
    ppermute x9, waiting for transfers between devices, shifted(): lax.ppermute(block, axis, [((i + distance) % size, i) for i in range(size)])  12.5 us
    unnamed x42, local copies, waits for them, and re-layouts  11.8 us
    all_to_all x1, starting transfers between devices, on_device(): lax.all_to_all(outgoing, 'dom', split_axis=0, concat_axis=0, tiled=True)  7.72 us
    all_to_all x1, starting transfers between devices, on_device(): lax.all_to_all(message, 'dom', split_axis=0, concat_axis=0, tiled=True)  7.64 us
    all_to_all x1, waiting for transfers between devices, on_device(): lax.all_to_all(outgoing, 'dom', split_axis=0, concat_axis=0, tiled=True)  7.49 us
    ppermute x9, starting transfers between devices, shifted(): lax.ppermute(block, axis, [((i + distance) % size, i) for i in range(size)])  6.18 us
  transfers between devices with their start and end apart: 18, of which 8 were waited for; matrix products, arithmetic and copies ran while one was open for 2% of the time, Pallas kernels for 12%

profile of v6, /device:TPU:31, one launch (start us, length us, event | category | flops | bytes accessed | tf_op | source)
XLA Modules:
  0.0 103.8 jit_solution(9798446319278943279)
XLA Ops:
  2.6 3.2 %shard_map.130 = bf16[16,128,256]{2,1,0:T(8,128)(2,1)} custom-call(s32[1]{0:T(128)} %bitcast.hid_ref, bf16[512,1024]{1,0:T(8,128)(2,1)} %features_ref.1, s32[16,128]{1,0:T(8,128)} %bitcast.21), custom_call_target="tpu_custom_call" | custom-call | flops 1000000000 | bytes 1 | tf_op jit(solution)/shard_map/pallas_call | solution.py:20
  5.9 7.7 %all-to-all-start = ((bf16[16,128,256]{2,1,0:T(8,128)(2,1)}), bf16[16,128,256]{2,1,0:T(8,128)(2,1)S(1)}, u32[]{:S(2)}, u32[]{:S(2)}) async-start(bf16[16,128,256]{2,1,0:T(8,128)(2,1)} %shard_map.130), calls=%async_computation | async-start | bytes 2097152 | tf_op jit(solution)/shard_map/all_to_all | solution.py:318
  14.6 1.5 %collective-permute-start.3 = (f32[256]{0:T(256)S(1)}, f32[256]{0:T(256)S(1)}, u32[]{:S(2)}, u32[]{:S(2)}) collective-permute-start(f32[256]{0:T(256)S(1)} %copy-done.15), channel_id=1, source_target_pairs={{1,0},{0,1},{3,2},{2,3},{5,4},{4,5},{7,6},{6,7},{9,8},{8,9},{11,10... | collective-permute-start | bytes 3080 | tf_op jit(solution)/shard_map/ppermute | solution.py:37
  17.0 2.8 %copy-done = bf16[3072,1024]{1,0:T(8,128)(2,1)S(1)} copy-done((bf16[3072,1024]{1,0:T(8,128)(2,1)S(1)}, bf16[3072,1024]{1,0:T(8,128)(2,1)}, u32[]{:S(2)}) %copy-start) | copy-done | bytes 6291480
  21.8 2.6 %shard_map.129 = f32[1024,256]{1,0:T(8,128)S(1)} custom-call(s32[12,4]{1,0:T(8,128)S(1)} %copy.14.live_ref, bf16[3072,1024]{1,0:T(8,128)(2,1)S(1)} %copy-done, bf16[256,1024]{1,0:T(8,128)(2,1)S(1)} %copy-done.6, bf16[256,1024]{1,0:T(8,128)(2,1)S(1)} %constant_dynamic-slice_fusion.own_ref, bf16[256,1024]{1,0:T(8,128)(2,1)S(1)} %copy-done.8), custom_call_target="tpu_custom_call" | custom-call | flops 60000002048 | bytes 1 | tf_op jit(solution)/shard_map/pallas_call | solution.py:20
  25.2 4.1 %collective-permute-done.4.refs_5_ = bf16[256,1024]{1,0:T(8,128)(2,1)S(1)} collective-permute-done((bf16[256,1024]{1,0:T(8,128)(2,1)S(1)}, bf16[256,1024]{1,0:T(8,128)(2,1)S(1)}, u32[]{:S(2)}, u32[]{:S(2)}) %collective-permute-start.4) | collective-permute-done | bytes 524320 | tf_op jit(solution)/shard_map/ppermute | solution.py:37
  30.0 7.5 %all-to-all-done.arrived_ref = bf16[16,128,256]{2,1,0:T(8,128)(2,1)S(1)} async-done(((bf16[16,128,256]{2,1,0:T(8,128)(2,1)}), bf16[16,128,256]{2,1,0:T(8,128)(2,1)S(1)}, u32[]{:S(2)}, u32[]{:S(2)}) %all-to-all-start) | async-done | bytes 1048608 | tf_op jit(solution)/shard_map/all_to_all | solution.py:318
  37.5 1.9 %shard_map.131 = f32[1024,256]{1,0:T(8,128)S(1)} custom-call(s32[16,128]{1,0:T(8,128)S(1)} %bitcast.15, f32[16,128]{1,0:T(8,128)S(1)} %bitcast.18, s32[16,1]{1,0:T(8,128)S(1)} %copy.15.counts_ref.refs_9_, bf16[16,128,256]{2,1,0:T(8,128)(2,1)S(1)} %all-to-all-done.arrived_ref), custom_call_target="tpu_custom_call" | custom-call | flops 4000000000 | bytes 1 | tf_op jit(solution)/shard_map/pallas_call | solution.py:20
  39.7 1.4 %collective-permute-start.6 = (bf16[512,256]{1,0:T(8,128)(2,1)S(1)}, bf16[512,256]{1,0:T(8,128)(2,1)S(1)}, u32[]{:S(2)}, u32[]{:S(2)}) collective-permute-start(bf16[512,256]{1,0:T(8,128)(2,1)S(1)} %get-tuple-element.48), channel_id=1, source_target_pairs={{1,0},{0,1},{3,2},{2,3},{5,4},{4,5},{7,6},{6,7},{9,8},{8,9},{11,10... | collective-permute-start | bytes 786440 | tf_op jit(solution)/shard_map/ppermute | solution.py:37
  41.2 6.2 %collective-permute-done.5 = bf16[512,256]{1,0:T(8,128)(2,1)S(1)} collective-permute-done((bf16[512,256]{1,0:T(8,128)(2,1)S(1)}, bf16[512,256]{1,0:T(8,128)(2,1)S(1)}, u32[]{:S(2)}, u32[]{:S(2)}) %collective-permute-start.5) | collective-permute-done | bytes 262176 | tf_op jit(solution)/shard_map/ppermute | solution.py:37
  48.4 2.4 %shard_map.132 = (bf16[256,512]{1,0:T(8,128)(2,1)S(1)}, f32[576,256]{1,0:T(8,128)S(1)}, bf16[512,256]{1,0:T(8,128)(2,1)S(1)}, bf16[16,128,256]{2,1,0:T(8,128)(2,1)S(1)}) custom-call(s32[1]{0:T(128)} %bitcast.hid_ref, bf16[512,256]{1,0:T(8,128)(2,1)S(1)} %copy-done.9, bf16[512,256]{1,0:T(8,128)(2,1)S(1)} %copy-done.11, f32[1,256]{1,0:T(1,128)S(1)} %bitcast.23, ...), custom_call_target="tpu_custom_call" | custom-call | flops 2000000000 | bytes 1 | tf_op jit(solution)/shard_map/pallas_call | solution.py:20
  50.8 2.2 %collective-permute-done.6 = bf16[512,256]{1,0:T(8,128)(2,1)S(1)} collective-permute-done((bf16[512,256]{1,0:T(8,128)(2,1)S(1)}, bf16[512,256]{1,0:T(8,128)(2,1)S(1)}, u32[]{:S(2)}, u32[]{:S(2)}) %collective-permute-start.6) | collective-permute-done | bytes 262176 | tf_op jit(solution)/shard_map/ppermute | solution.py:37
  53.1 3.4 %shard_map.133 = (bf16[256,512]{1,0:T(8,128)(2,1)S(1)}, f32[576,256]{1,0:T(8,128)S(1)}, bf16[512,256]{1,0:T(8,128)(2,1)S(1)}, bf16[16,128,256]{2,1,0:T(8,128)(2,1)}) custom-call(s32[1]{0:T(128)} %bitcast.hid_ref, bf16[512,256]{1,0:T(8,128)(2,1)S(1)} %copy-done.9, bf16[512,256]{1,0:T(8,128)(2,1)S(1)} %copy-done.11, f32[1,256]{1,0:T(1,128)S(1)} %bitcast.24, ...), custom_call_target="tpu_custom_call" | custom-call | flops 2000000000 | bytes 1 | tf_op jit(solution)/shard_map/pallas_call | solution.py:20
  58.9 2.0 %shard_map.134 = (bf16[1024,256]{1,0:T(8,128)(2,1)S(1)}, bf16[1024,256]{1,0:T(8,128)(2,1)S(1)}) custom-call(s32[12,4]{1,0:T(8,128)S(1)} %copy.14.live_ref, bf16[3072,1024]{1,0:T(8,128)(2,1)S(1)} %bitcast.14, bf16[1024,256]{1,0:T(8,128)(2,1)S(1)} %constant_dynamic-update-slice_fusion.back_ref), custom_call_target="tpu_custom_call" | custom-call | flops 2000000000 | bytes 1 | tf_op jit(solution)/shard_map/pallas_call | solution.py:20
  62.1 1.6 %collective-permute-start.10 = (bf16[144,256]{1,0:T(8,128)(2,1)S(1)}, bf16[144,256]{1,0:T(8,128)(2,1)S(1)}, u32[]{:S(2)}, u32[]{:S(2)}) collective-permute-start(bf16[144,256]{1,0:T(8,128)(2,1)S(1)} %convert_add_fusion.2), channel_id=1, source_target_pairs={{0,16},{2,18},{4,20},{6,22},{8,24},{10,26},{12,28},{14,30},{16,0},... | collective-permute-start | bytes 221192 | tf_op jit(solution)/shard_map/ppermute | solution.py:42
  63.8 1.9 %collective-permute-start.9 = (bf16[144,256]{1,0:T(8,128)(2,1)S(1)}, bf16[144,256]{1,0:T(8,128)(2,1)S(1)}, u32[]{:S(2)}, u32[]{:S(2)}) collective-permute-start(bf16[144,256]{1,0:T(8,128)(2,1)S(1)} %convert_add_fusion.2), channel_id=1, source_target_pairs={{0,8},{2,10},{4,12},{6,14},{8,0},{10,2},{12,4},{14,6},{16,24},{18,... | collective-permute-start | bytes 221192 | tf_op jit(solution)/shard_map/ppermute | solution.py:42
  65.7 2.0 %collective-permute-start.13 = (bf16[1024,256]{1,0:T(8,128)(2,1)S(1)}, bf16[1024,256]{1,0:T(8,128)(2,1)}, u32[]{:S(2)}, u32[]{:S(2)}) collective-permute-start(bf16[1024,256]{1,0:T(8,128)(2,1)S(1)} %get-tuple-element.53), channel_id=1, source_target_pairs={{30,0},{0,2},{2,4},{4,6},{6,8},{8,10},{10,12},{12,14},{14,16},{16,... | collective-permute-start | bytes 1572872 | tf_op jit(solution)/shard_map/ppermute | solution.py:37
  68.0 7.6 %all-to-all-start.1 = ((bf16[16,128,256]{2,1,0:T(8,128)(2,1)}), bf16[16,128,256]{2,1,0:T(8,128)(2,1)S(1)}, u32[]{:S(2)}, u32[]{:S(2)}) async-start(bf16[16,128,256]{2,1,0:T(8,128)(2,1)} %get-tuple-element.59), calls=%async_computation.1 | async-start | bytes 2097152 | tf_op jit(solution)/shard_map/all_to_all | solution.py:393
  76.1 2.8 %copy-done.1 = bf16[3072,1024]{1,0:T(8,128)(2,1)S(1)} copy-done((bf16[3072,1024]{1,0:T(8,128)(2,1)S(1)}, bf16[3072,1024]{1,0:T(8,128)(2,1)}, u32[]{:S(2)}) %copy-start.1) | copy-done | bytes 6291480
  78.9 1.4 %shard_map.135 = f32[1024,256]{1,0:T(8,128)S(1)} custom-call(s32[12,4]{1,0:T(8,128)S(1)} %copy.14.live_ref, bf16[3072,1024]{1,0:T(8,128)(2,1)S(1)} %copy-done.1, bf16[1024,256]{1,0:T(8,128)(2,1)S(1)} %constant_dynamic-update-slice_fusion.back_ref), custom_call_target="tpu_custom_call" | custom-call | flops 1000000000 | bytes 1 | tf_op jit(solution)/shard_map/pallas_call | solution.py:20
  81.1 12.8 %collective-permute-done.12 = f32[144,256]{1,0:T(8,128)S(1)} collective-permute-done((f32[144,256]{1,0:T(8,128)S(1)}, f32[144,256]{1,0:T(8,128)S(1)}, u32[]{:S(2)}, u32[]{:S(2)}) %collective-permute-start.12) | collective-permute-done | bytes 147488 | tf_op jit(solution)/shard_map/ppermute | solution.py:42
  94.9 1.3 %convert_add_fusion.dense_ref = f32[1024,256]{1,0:T(8,128)S(1)} fusion(bf16[1024,256]{1,0:T(8,128)(2,1)} %collective-permute-done.14, f32[1024,256]{1,0:T(8,128)S(1)} %shard_map.135, bf16[1024,256]{1,0:T(8,128)(2,1)} %collective-permute-done.13), kind=kLoop, calls=%fused_computation | loop fusion | flops 1048576 | bytes 3145728 | tf_op jit(solution)/shard_map/add | solution.py:409
  97.1 4.4 %all-to-all-done.1.returned_ref = bf16[16,128,256]{2,1,0:T(8,128)(2,1)S(1)} async-done(((bf16[16,128,256]{2,1,0:T(8,128)(2,1)}), bf16[16,128,256]{2,1,0:T(8,128)(2,1)S(1)}, u32[]{:S(2)}, u32[]{:S(2)}) %all-to-all-start.1) | async-done | bytes 1048608 | tf_op jit(solution)/shard_map/all_to_all | solution.py:393
  101.5 2.3 %shard_map.136 = bf16[256,1024]{1,0:T(8,128)(2,1)} custom-call(s32[16,128]{1,0:T(8,128)S(1)} %bitcast.22, bf16[16,128,256]{2,1,0:T(8,128)(2,1)S(1)} %all-to-all-done.1.returned_ref, f32[1024,256]{1,0:T(8,128)S(1)} %convert_add_fusion.dense_ref), custom_call_target="tpu_custom_call" | custom-call | flops 1000000000 | bytes 1 | tf_op jit(solution)/shard_map/pallas_call | solution.py:20
  (79 shorter events, 15.7 us)
Async XLA Ops:
  0.6 13.1 %copy-start.17 = (s32[1,16]{1,0:T(1,128)S(1)}, s32[1,16]{1,0:T(1,128)}, u32[]{:S(2)}) copy-start(s32[1,16]{1,0:T(1,128)} %param.17) | copy-start | bytes 196
  0.7 14.0 %copy-start.9 = (bf16[512,256]{1,0:T(8,128)(2,1)S(1)}, bf16[512,256]{1,0:T(8,128)(2,1)}, u32[]{:S(2)}) copy-start(bf16[512,256]{1,0:T(8,128)(2,1)} %refs_0_.1) | copy-start | bytes 786436
  0.7 14.0 %copy-start.15 = (f32[256]{0:T(256)S(1)}, f32[256]{0:T(256)}, u32[]{:S(2)}) copy-start(f32[256]{0:T(256)} %param.18) | copy-start | bytes 3076
  0.7 15.4 %copy-start.2 = (bf16[256,1024]{1,0:T(8,128)(2,1)S(1)}, bf16[256,1024]{1,0:T(8,128)(2,1)}, u32[]{:S(2)}) copy-start(bf16[256,1024]{1,0:T(8,128)(2,1)} %refs_4_.1) | copy-start | bytes 1572868
  1.8 12.0 %collective-permute-start = (bf16[256,1024]{1,0:T(8,128)(2,1)S(1)}, bf16[256,1024]{1,0:T(8,128)(2,1)S(1)}, u32[]{:S(2)}, u32[]{:S(2)}) collective-permute-start(bf16[256,1024]{1,0:T(8,128)(2,1)S(1)} %constant_dynamic-slice_fusion.own_ref), channel_id=1, source_target_pairs={{30,0},{0,2},{2,4},{4,6},{6,8},{8,10},{10,12},{12,14},{14,16},{16,... | collective-permute-start | bytes 1572872 | tf_op jit(solution)/shard_map/ppermute | solution.py:37
  2.3 13.8 %collective-permute-start.1 = (bf16[256,1024]{1,0:T(8,128)(2,1)S(1)}, bf16[256,1024]{1,0:T(8,128)(2,1)S(1)}, u32[]{:S(2)}, u32[]{:S(2)}) collective-permute-start(bf16[256,1024]{1,0:T(8,128)(2,1)S(1)} %constant_dynamic-slice_fusion.own_ref), channel_id=1, source_target_pairs={{2,0},{4,2},{6,4},{8,6},{10,8},{12,10},{14,12},{16,14},{18,16},{20... | collective-permute-start | bytes 1572872 | tf_op jit(solution)/shard_map/ppermute | solution.py:37
  5.9 31.6 %all-to-all-start = ((bf16[16,128,256]{2,1,0:T(8,128)(2,1)}), bf16[16,128,256]{2,1,0:T(8,128)(2,1)S(1)}, u32[]{:S(2)}, u32[]{:S(2)}) async-start(bf16[16,128,256]{2,1,0:T(8,128)(2,1)} %shard_map.130), calls=%async_computation | async-start | bytes 2097152 | tf_op jit(solution)/shard_map/all_to_all | solution.py:318
  13.6 23.9 %copy-start.13 = (f32[1,16,128]{2,1,0:T(8,128)S(1)}, f32[1,16,128]{2,1,0:T(8,128)}, u32[]{:S(2)}) copy-start(f32[1,16,128]{2,1,0:T(8,128)} %param.16) | copy-start | bytes 24580
  13.7 23.8 %copy-start.12 = (s32[1,16,128]{2,1,0:T(8,128)S(1)}, s32[1,16,128]{2,1,0:T(8,128)}, u32[]{:S(2)}) copy-start(s32[1,16,128]{2,1,0:T(8,128)} %param.15) | copy-start | bytes 24580
  14.6 9.8 %collective-permute-start.2 = (bf16[512,256]{1,0:T(8,128)(2,1)S(1)}, bf16[512,256]{1,0:T(8,128)(2,1)S(1)}, u32[]{:S(2)}, u32[]{:S(2)}) collective-permute-start(bf16[512,256]{1,0:T(8,128)(2,1)S(1)} %copy-done.9), channel_id=1, source_target_pairs={{1,0},{0,1},{3,2},{2,3},{5,4},{4,5},{7,6},{6,7},{9,8},{8,9},{11,10... | collective-permute-start | bytes 786440 | tf_op jit(solution)/shard_map/ppermute | solution.py:37
  14.6 9.8 %collective-permute-start.3 = (f32[256]{0:T(256)S(1)}, f32[256]{0:T(256)S(1)}, u32[]{:S(2)}, u32[]{:S(2)}) collective-permute-start(f32[256]{0:T(256)S(1)} %copy-done.15), channel_id=1, source_target_pairs={{1,0},{0,1},{3,2},{2,3},{5,4},{4,5},{7,6},{6,7},{9,8},{8,9},{11,10... | collective-permute-start | bytes 3080 | tf_op jit(solution)/shard_map/ppermute | solution.py:37
  16.1 13.1 %collective-permute-start.4 = (bf16[256,1024]{1,0:T(8,128)(2,1)S(1)}, bf16[256,1024]{1,0:T(8,128)(2,1)S(1)}, u32[]{:S(2)}, u32[]{:S(2)}) collective-permute-start(bf16[256,1024]{1,0:T(8,128)(2,1)S(1)} %copy-done.2), channel_id=1, source_target_pairs={{1,0},{0,1},{3,2},{2,3},{5,4},{4,5},{7,6},{6,7},{9,8},{8,9},{11,10... | collective-permute-start | bytes 1572872 | tf_op jit(solution)/shard_map/ppermute | solution.py:37
  39.6 7.8 %collective-permute-start.5 = (bf16[512,256]{1,0:T(8,128)(2,1)S(1)}, bf16[512,256]{1,0:T(8,128)(2,1)S(1)}, u32[]{:S(2)}, u32[]{:S(2)}) collective-permute-start(bf16[512,256]{1,0:T(8,128)(2,1)S(1)} %get-tuple-element.67), channel_id=1, source_target_pairs={{1,0},{0,1},{3,2},{2,3},{5,4},{4,5},{7,6},{6,7},{9,8},{8,9},{11,10... | collective-permute-start | bytes 786440 | tf_op jit(solution)/shard_map/ppermute | solution.py:37
  39.7 13.3 %collective-permute-start.6 = (bf16[512,256]{1,0:T(8,128)(2,1)S(1)}, bf16[512,256]{1,0:T(8,128)(2,1)S(1)}, u32[]{:S(2)}, u32[]{:S(2)}) collective-permute-start(bf16[512,256]{1,0:T(8,128)(2,1)S(1)} %get-tuple-element.48), channel_id=1, source_target_pairs={{1,0},{0,1},{3,2},{2,3},{5,4},{4,5},{7,6},{6,7},{9,8},{8,9},{11,10... | collective-permute-start | bytes 786440 | tf_op jit(solution)/shard_map/ppermute | solution.py:37
  56.6 2.1 %collective-permute-start.7 = (bf16[288,256]{1,0:T(8,128)(2,1)S(1)}, bf16[288,256]{1,0:T(8,128)(2,1)S(1)}, u32[]{:S(2)}, u32[]{:S(2)}) collective-permute-start(bf16[288,256]{1,0:T(8,128)(2,1)S(1)} %select_convert_fusion), channel_id=1, source_target_pairs={{0,2},{2,0},{4,6},{6,4},{8,10},{10,8},{12,14},{14,12},{16,18},{18,... | collective-permute-start | bytes 442376 | tf_op jit(solution)/shard_map/ppermute | solution.py:42
  58.8 3.3 %collective-permute-start.8 = (bf16[144,256]{1,0:T(8,128)(2,1)S(1)}, bf16[144,256]{1,0:T(8,128)(2,1)S(1)}, u32[]{:S(2)}, u32[]{:S(2)}) collective-permute-start(bf16[144,256]{1,0:T(8,128)(2,1)S(1)} %select_convert_fusion.1), channel_id=1, source_target_pairs={{0,4},{2,6},{4,0},{6,2},{8,12},{10,14},{12,8},{14,10},{16,20},{18,... | collective-permute-start | bytes 221192 | tf_op jit(solution)/shard_map/ppermute | solution.py:42
  62.1 13.6 %collective-permute-start.11 = (bf16[144,256]{1,0:T(8,128)(2,1)S(1)}, bf16[144,256]{1,0:T(8,128)(2,1)S(1)}, u32[]{:S(2)}, u32[]{:S(2)}) collective-permute-start(bf16[144,256]{1,0:T(8,128)(2,1)S(1)} %convert_add_fusion.2), channel_id=1, source_target_pairs={{0,24},{2,26},{4,28},{6,30},{8,16},{10,18},{12,20},{14,22},{16,8},... | collective-permute-start | bytes 221192 | tf_op jit(solution)/shard_map/ppermute | solution.py:42
  62.1 13.5 %collective-permute-start.10 = (bf16[144,256]{1,0:T(8,128)(2,1)S(1)}, bf16[144,256]{1,0:T(8,128)(2,1)S(1)}, u32[]{:S(2)}, u32[]{:S(2)}) collective-permute-start(bf16[144,256]{1,0:T(8,128)(2,1)S(1)} %convert_add_fusion.2), channel_id=1, source_target_pairs={{0,16},{2,18},{4,20},{6,22},{8,24},{10,26},{12,28},{14,30},{16,0},... | collective-permute-start | bytes 221192 | tf_op jit(solution)/shard_map/ppermute | solution.py:42
  63.8 11.9 %collective-permute-start.9 = (bf16[144,256]{1,0:T(8,128)(2,1)S(1)}, bf16[144,256]{1,0:T(8,128)(2,1)S(1)}, u32[]{:S(2)}, u32[]{:S(2)}) collective-permute-start(bf16[144,256]{1,0:T(8,128)(2,1)S(1)} %convert_add_fusion.2), channel_id=1, source_target_pairs={{0,8},{2,10},{4,12},{6,14},{8,0},{10,2},{12,4},{14,6},{16,24},{18,... | collective-permute-start | bytes 221192 | tf_op jit(solution)/shard_map/ppermute | solution.py:42
  65.7 28.3 %collective-permute-start.13 = (bf16[1024,256]{1,0:T(8,128)(2,1)S(1)}, bf16[1024,256]{1,0:T(8,128)(2,1)}, u32[]{:S(2)}, u32[]{:S(2)}) collective-permute-start(bf16[1024,256]{1,0:T(8,128)(2,1)S(1)} %get-tuple-element.53), channel_id=1, source_target_pairs={{30,0},{0,2},{2,4},{4,6},{6,8},{8,10},{10,12},{12,14},{14,16},{16,... | collective-permute-start | bytes 1572872 | tf_op jit(solution)/shard_map/ppermute | solution.py:37
  67.7 26.3 %collective-permute-start.14 = (bf16[1024,256]{1,0:T(8,128)(2,1)S(1)}, bf16[1024,256]{1,0:T(8,128)(2,1)}, u32[]{:S(2)}, u32[]{:S(2)}) collective-permute-start(bf16[1024,256]{1,0:T(8,128)(2,1)S(1)} %get-tuple-element.52), channel_id=1, source_target_pairs={{2,0},{4,2},{6,4},{8,6},{10,8},{12,10},{14,12},{16,14},{18,16},{20... | collective-permute-start | bytes 1572872 | tf_op jit(solution)/shard_map/ppermute | solution.py:37
  68.0 33.5 %all-to-all-start.1 = ((bf16[16,128,256]{2,1,0:T(8,128)(2,1)}), bf16[16,128,256]{2,1,0:T(8,128)(2,1)S(1)}, u32[]{:S(2)}, u32[]{:S(2)}) async-start(bf16[16,128,256]{2,1,0:T(8,128)(2,1)} %get-tuple-element.59), calls=%async_computation.1 | async-start | bytes 2097152 | tf_op jit(solution)/shard_map/all_to_all | solution.py:393
  75.7 18.2 %collective-permute-start.12 = (f32[144,256]{1,0:T(8,128)S(1)}, f32[144,256]{1,0:T(8,128)S(1)}, u32[]{:S(2)}, u32[]{:S(2)}) collective-permute-start(f32[144,256]{1,0:T(8,128)S(1)} %add_add_fusion), channel_id=1, source_target_pairs={{0,4},{2,6},{4,0},{6,2},{8,12},{10,14},{12,8},{14,10},{16,20},{18,... | collective-permute-start | bytes 442376 | tf_op jit(solution)/shard_map/ppermute | solution.py:42
  94.0 2.3 %collective-permute-start.15 = (f32[288,256]{1,0:T(8,128)S(1)}, f32[288,256]{1,0:T(8,128)S(1)}, u32[]{:S(2)}, u32[]{:S(2)}) collective-permute-start(f32[288,256]{1,0:T(8,128)S(1)} %maximum_select_fusion.mine_ref), channel_id=1, source_target_pairs={{0,2},{2,0},{4,6},{6,4},{8,10},{10,8},{12,14},{14,12},{16,18},{18,... | collective-permute-start | bytes 884744 | tf_op jit(solution)/shard_map/ppermute | solution.py:42
  (14 other events, 51.6 us)

commit v7 on v6

--- a/solution.py
+++ b/solution.py
@@ -212,7 +212,7 @@
     peers, slots, _ = message_ref.shape
     weights_t = masked_weights(weight_ref[...], counts_ref[...]).T
     recv_t = recv_ref[...].T
-    group = 8
+    group = 16
     sent = []
     for p in range(0, peers, group):
         slots_by_nodes(hot, recv_t, first, p, group)

time: 104 us -> 104 us (level)
  no operation moved by 1% of the time
where the time goes in v7:
time: 104 us
  waiting for transfers between devices  39.4 us (38%)
  starting transfers between devices  27.6 us (27%)
  Pallas kernels  20.1 us (19%)
  local copies, waits for them, and re-layouts  13.1 us (13%)
  other arithmetic  2.74 us (3%)
    pallas_call x9, Pallas kernels, call(): pl.pallas_call(kernel, out_shape=tuple(outs), in_specs=[place for place,...  20.1 us
    ppermute x7, waiting for transfers between devices, swapped(): return lax.ppermute(block, axis, [(i, i ^ bit) for i in range(size)])  14.9 us
    ppermute x9, waiting for transfers between devices, shifted(): lax.ppermute(block, axis, [((i + distance) % size, i) for i in range(size)])  12.5 us
    unnamed x42, local copies, waits for them, and re-layouts  11.8 us
    all_to_all x1, starting transfers between devices, on_device(): lax.all_to_all(outgoing, 'dom', split_axis=0, concat_axis=0, tiled=True)  7.72 us
    all_to_all x1, starting transfers between devices, on_device(): lax.all_to_all(message, 'dom', split_axis=0, concat_axis=0, tiled=True)  7.64 us
    all_to_all x1, waiting for transfers between devices, on_device(): lax.all_to_all(outgoing, 'dom', split_axis=0, concat_axis=0, tiled=True)  7.49 us
    ppermute x9, starting transfers between devices, shifted(): lax.ppermute(block, axis, [((i + distance) % size, i) for i in range(size)])  6.18 us
  transfers between devices with their start and end apart: 18, of which 8 were waited for; matrix products, arithmetic and copies ran while one was open for 2% of the time, Pallas kernels for 12%

profile of v7, /device:TPU:31, one launch (start us, length us, event | category | flops | bytes accessed | tf_op | source)
XLA Modules:
  0.0 103.9 jit_solution(12691650809196613122)
XLA Ops:
  2.6 3.2 %shard_map.130 = bf16[16,128,256]{2,1,0:T(8,128)(2,1)} custom-call(s32[1]{0:T(128)} %bitcast.hid_ref, bf16[512,1024]{1,0:T(8,128)(2,1)} %features_ref.1, s32[16,128]{1,0:T(8,128)} %bitcast.21), custom_call_target="tpu_custom_call" | custom-call | flops 1000000000 | bytes 1 | tf_op jit(solution)/shard_map/pallas_call | solution.py:20
  5.9 7.7 %all-to-all-start = ((bf16[16,128,256]{2,1,0:T(8,128)(2,1)}), bf16[16,128,256]{2,1,0:T(8,128)(2,1)S(1)}, u32[]{:S(2)}, u32[]{:S(2)}) async-start(bf16[16,128,256]{2,1,0:T(8,128)(2,1)} %shard_map.130), calls=%async_computation | async-start | bytes 2097152 | tf_op jit(solution)/shard_map/all_to_all | solution.py:318
  14.6 1.5 %collective-permute-start.3 = (f32[256]{0:T(256)S(1)}, f32[256]{0:T(256)S(1)}, u32[]{:S(2)}, u32[]{:S(2)}) collective-permute-start(f32[256]{0:T(256)S(1)} %copy-done.15), channel_id=1, source_target_pairs={{1,0},{0,1},{3,2},{2,3},{5,4},{4,5},{7,6},{6,7},{9,8},{8,9},{11,10... | collective-permute-start | bytes 3080 | tf_op jit(solution)/shard_map/ppermute | solution.py:37
  17.0 2.8 %copy-done = bf16[3072,1024]{1,0:T(8,128)(2,1)S(1)} copy-done((bf16[3072,1024]{1,0:T(8,128)(2,1)S(1)}, bf16[3072,1024]{1,0:T(8,128)(2,1)}, u32[]{:S(2)}) %copy-start) | copy-done | bytes 6291480
  21.8 2.6 %shard_map.129 = f32[1024,256]{1,0:T(8,128)S(1)} custom-call(s32[12,4]{1,0:T(8,128)S(1)} %copy.14.live_ref, bf16[3072,1024]{1,0:T(8,128)(2,1)S(1)} %copy-done, bf16[256,1024]{1,0:T(8,128)(2,1)S(1)} %copy-done.6, bf16[256,1024]{1,0:T(8,128)(2,1)S(1)} %constant_dynamic-slice_fusion.own_ref, bf16[256,1024]{1,0:T(8,128)(2,1)S(1)} %copy-done.8), custom_call_target="tpu_custom_call" | custom-call | flops 60000002048 | bytes 1 | tf_op jit(solution)/shard_map/pallas_call | solution.py:20
  25.2 4.1 %collective-permute-done.4.refs_5_ = bf16[256,1024]{1,0:T(8,128)(2,1)S(1)} collective-permute-done((bf16[256,1024]{1,0:T(8,128)(2,1)S(1)}, bf16[256,1024]{1,0:T(8,128)(2,1)S(1)}, u32[]{:S(2)}, u32[]{:S(2)}) %collective-permute-start.4) | collective-permute-done | bytes 524320 | tf_op jit(solution)/shard_map/ppermute | solution.py:37
  30.0 7.5 %all-to-all-done.arrived_ref = bf16[16,128,256]{2,1,0:T(8,128)(2,1)S(1)} async-done(((bf16[16,128,256]{2,1,0:T(8,128)(2,1)}), bf16[16,128,256]{2,1,0:T(8,128)(2,1)S(1)}, u32[]{:S(2)}, u32[]{:S(2)}) %all-to-all-start) | async-done | bytes 1048608 | tf_op jit(solution)/shard_map/all_to_all | solution.py:318
  37.5 1.9 %shard_map.131 = f32[1024,256]{1,0:T(8,128)S(1)} custom-call(s32[16,128]{1,0:T(8,128)S(1)} %bitcast.15, f32[16,128]{1,0:T(8,128)S(1)} %bitcast.18, s32[16,1]{1,0:T(8,128)S(1)} %copy.15.counts_ref.refs_9_, bf16[16,128,256]{2,1,0:T(8,128)(2,1)S(1)} %all-to-all-done.arrived_ref), custom_call_target="tpu_custom_call" | custom-call | flops 4000000000 | bytes 1 | tf_op jit(solution)/shard_map/pallas_call | solution.py:20
  39.7 1.4 %collective-permute-start.6 = (bf16[512,256]{1,0:T(8,128)(2,1)S(1)}, bf16[512,256]{1,0:T(8,128)(2,1)S(1)}, u32[]{:S(2)}, u32[]{:S(2)}) collective-permute-start(bf16[512,256]{1,0:T(8,128)(2,1)S(1)} %get-tuple-element.48), channel_id=1, source_target_pairs={{1,0},{0,1},{3,2},{2,3},{5,4},{4,5},{7,6},{6,7},{9,8},{8,9},{11,10... | collective-permute-start | bytes 786440 | tf_op jit(solution)/shard_map/ppermute | solution.py:37
  41.2 6.2 %collective-permute-done.5 = bf16[512,256]{1,0:T(8,128)(2,1)S(1)} collective-permute-done((bf16[512,256]{1,0:T(8,128)(2,1)S(1)}, bf16[512,256]{1,0:T(8,128)(2,1)S(1)}, u32[]{:S(2)}, u32[]{:S(2)}) %collective-permute-start.5) | collective-permute-done | bytes 262176 | tf_op jit(solution)/shard_map/ppermute | solution.py:37
  48.4 2.4 %shard_map.132 = (bf16[256,512]{1,0:T(8,128)(2,1)S(1)}, f32[576,256]{1,0:T(8,128)S(1)}, bf16[512,256]{1,0:T(8,128)(2,1)S(1)}, bf16[16,128,256]{2,1,0:T(8,128)(2,1)S(1)}) custom-call(s32[1]{0:T(128)} %bitcast.hid_ref, bf16[512,256]{1,0:T(8,128)(2,1)S(1)} %copy-done.9, bf16[512,256]{1,0:T(8,128)(2,1)S(1)} %copy-done.11, f32[1,256]{1,0:T(1,128)S(1)} %bitcast.23, ...), custom_call_target="tpu_custom_call" | custom-call | flops 2000000000 | bytes 1 | tf_op jit(solution)/shard_map/pallas_call | solution.py:20
  50.8 2.2 %collective-permute-done.6 = bf16[512,256]{1,0:T(8,128)(2,1)S(1)} collective-permute-done((bf16[512,256]{1,0:T(8,128)(2,1)S(1)}, bf16[512,256]{1,0:T(8,128)(2,1)S(1)}, u32[]{:S(2)}, u32[]{:S(2)}) %collective-permute-start.6) | collective-permute-done | bytes 262176 | tf_op jit(solution)/shard_map/ppermute | solution.py:37
  53.1 3.4 %shard_map.133 = (bf16[256,512]{1,0:T(8,128)(2,1)S(1)}, f32[576,256]{1,0:T(8,128)S(1)}, bf16[512,256]{1,0:T(8,128)(2,1)S(1)}, bf16[16,128,256]{2,1,0:T(8,128)(2,1)}) custom-call(s32[1]{0:T(128)} %bitcast.hid_ref, bf16[512,256]{1,0:T(8,128)(2,1)S(1)} %copy-done.9, bf16[512,256]{1,0:T(8,128)(2,1)S(1)} %copy-done.11, f32[1,256]{1,0:T(1,128)S(1)} %bitcast.24, ...), custom_call_target="tpu_custom_call" | custom-call | flops 2000000000 | bytes 1 | tf_op jit(solution)/shard_map/pallas_call | solution.py:20
  58.9 2.0 %shard_map.134 = (bf16[1024,256]{1,0:T(8,128)(2,1)S(1)}, bf16[1024,256]{1,0:T(8,128)(2,1)S(1)}) custom-call(s32[12,4]{1,0:T(8,128)S(1)} %copy.14.live_ref, bf16[3072,1024]{1,0:T(8,128)(2,1)S(1)} %bitcast.14, bf16[1024,256]{1,0:T(8,128)(2,1)S(1)} %constant_dynamic-update-slice_fusion.back_ref), custom_call_target="tpu_custom_call" | custom-call | flops 2000000000 | bytes 1 | tf_op jit(solution)/shard_map/pallas_call | solution.py:20
  62.2 1.6 %collective-permute-start.10 = (bf16[144,256]{1,0:T(8,128)(2,1)S(1)}, bf16[144,256]{1,0:T(8,128)(2,1)S(1)}, u32[]{:S(2)}, u32[]{:S(2)}) collective-permute-start(bf16[144,256]{1,0:T(8,128)(2,1)S(1)} %convert_add_fusion.2), channel_id=1, source_target_pairs={{0,16},{2,18},{4,20},{6,22},{8,24},{10,26},{12,28},{14,30},{16,0},... | collective-permute-start | bytes 221192 | tf_op jit(solution)/shard_map/ppermute | solution.py:42
  63.8 1.9 %collective-permute-start.9 = (bf16[144,256]{1,0:T(8,128)(2,1)S(1)}, bf16[144,256]{1,0:T(8,128)(2,1)S(1)}, u32[]{:S(2)}, u32[]{:S(2)}) collective-permute-start(bf16[144,256]{1,0:T(8,128)(2,1)S(1)} %convert_add_fusion.2), channel_id=1, source_target_pairs={{0,8},{2,10},{4,12},{6,14},{8,0},{10,2},{12,4},{14,6},{16,24},{18,... | collective-permute-start | bytes 221192 | tf_op jit(solution)/shard_map/ppermute | solution.py:42
  65.7 2.0 %collective-permute-start.13 = (bf16[1024,256]{1,0:T(8,128)(2,1)S(1)}, bf16[1024,256]{1,0:T(8,128)(2,1)}, u32[]{:S(2)}, u32[]{:S(2)}) collective-permute-start(bf16[1024,256]{1,0:T(8,128)(2,1)S(1)} %get-tuple-element.53), channel_id=1, source_target_pairs={{30,0},{0,2},{2,4},{4,6},{6,8},{8,10},{10,12},{12,14},{14,16},{16,... | collective-permute-start | bytes 1572872 | tf_op jit(solution)/shard_map/ppermute | solution.py:37
  68.1 7.6 %all-to-all-start.1 = ((bf16[16,128,256]{2,1,0:T(8,128)(2,1)}), bf16[16,128,256]{2,1,0:T(8,128)(2,1)S(1)}, u32[]{:S(2)}, u32[]{:S(2)}) async-start(bf16[16,128,256]{2,1,0:T(8,128)(2,1)} %get-tuple-element.59), calls=%async_computation.1 | async-start | bytes 2097152 | tf_op jit(solution)/shard_map/all_to_all | solution.py:393
  76.1 2.8 %copy-done.1 = bf16[3072,1024]{1,0:T(8,128)(2,1)S(1)} copy-done((bf16[3072,1024]{1,0:T(8,128)(2,1)S(1)}, bf16[3072,1024]{1,0:T(8,128)(2,1)}, u32[]{:S(2)}) %copy-start.1) | copy-done | bytes 6291480
  78.9 1.4 %shard_map.135 = f32[1024,256]{1,0:T(8,128)S(1)} custom-call(s32[12,4]{1,0:T(8,128)S(1)} %copy.14.live_ref, bf16[3072,1024]{1,0:T(8,128)(2,1)S(1)} %copy-done.1, bf16[1024,256]{1,0:T(8,128)(2,1)S(1)} %constant_dynamic-update-slice_fusion.back_ref), custom_call_target="tpu_custom_call" | custom-call | flops 1000000000 | bytes 1 | tf_op jit(solution)/shard_map/pallas_call | solution.py:20
  81.2 12.8 %collective-permute-done.12 = f32[144,256]{1,0:T(8,128)S(1)} collective-permute-done((f32[144,256]{1,0:T(8,128)S(1)}, f32[144,256]{1,0:T(8,128)S(1)}, u32[]{:S(2)}, u32[]{:S(2)}) %collective-permute-start.12) | collective-permute-done | bytes 147488 | tf_op jit(solution)/shard_map/ppermute | solution.py:42
  94.9 1.3 %convert_add_fusion.dense_ref = f32[1024,256]{1,0:T(8,128)S(1)} fusion(bf16[1024,256]{1,0:T(8,128)(2,1)} %collective-permute-done.14, f32[1024,256]{1,0:T(8,128)S(1)} %shard_map.135, bf16[1024,256]{1,0:T(8,128)(2,1)} %collective-permute-done.13), kind=kLoop, calls=%fused_computation | loop fusion | flops 1048576 | bytes 3145728 | tf_op jit(solution)/shard_map/add | solution.py:409
  97.1 4.4 %all-to-all-done.1.returned_ref = bf16[16,128,256]{2,1,0:T(8,128)(2,1)S(1)} async-done(((bf16[16,128,256]{2,1,0:T(8,128)(2,1)}), bf16[16,128,256]{2,1,0:T(8,128)(2,1)S(1)}, u32[]{:S(2)}, u32[]{:S(2)}) %all-to-all-start.1) | async-done | bytes 1048608 | tf_op jit(solution)/shard_map/all_to_all | solution.py:393
  101.6 2.3 %shard_map.136 = bf16[256,1024]{1,0:T(8,128)(2,1)} custom-call(s32[16,128]{1,0:T(8,128)S(1)} %bitcast.22, bf16[16,128,256]{2,1,0:T(8,128)(2,1)S(1)} %all-to-all-done.1.returned_ref, f32[1024,256]{1,0:T(8,128)S(1)} %convert_add_fusion.dense_ref), custom_call_target="tpu_custom_call" | custom-call | flops 1000000000 | bytes 1 | tf_op jit(solution)/shard_map/pallas_call | solution.py:20
  (79 shorter events, 15.7 us)
Async XLA Ops:
  0.6 13.1 %copy-start.17 = (s32[1,16]{1,0:T(1,128)S(1)}, s32[1,16]{1,0:T(1,128)}, u32[]{:S(2)}) copy-start(s32[1,16]{1,0:T(1,128)} %param.17) | copy-start | bytes 196
  0.7 14.0 %copy-start.9 = (bf16[512,256]{1,0:T(8,128)(2,1)S(1)}, bf16[512,256]{1,0:T(8,128)(2,1)}, u32[]{:S(2)}) copy-start(bf16[512,256]{1,0:T(8,128)(2,1)} %refs_0_.1) | copy-start | bytes 786436
  0.7 14.0 %copy-start.15 = (f32[256]{0:T(256)S(1)}, f32[256]{0:T(256)}, u32[]{:S(2)}) copy-start(f32[256]{0:T(256)} %param.18) | copy-start | bytes 3076
  0.7 15.4 %copy-start.2 = (bf16[256,1024]{1,0:T(8,128)(2,1)S(1)}, bf16[256,1024]{1,0:T(8,128)(2,1)}, u32[]{:S(2)}) copy-start(bf16[256,1024]{1,0:T(8,128)(2,1)} %refs_4_.1) | copy-start | bytes 1572868
  1.8 12.0 %collective-permute-start = (bf16[256,1024]{1,0:T(8,128)(2,1)S(1)}, bf16[256,1024]{1,0:T(8,128)(2,1)S(1)}, u32[]{:S(2)}, u32[]{:S(2)}) collective-permute-start(bf16[256,1024]{1,0:T(8,128)(2,1)S(1)} %constant_dynamic-slice_fusion.own_ref), channel_id=1, source_target_pairs={{30,0},{0,2},{2,4},{4,6},{6,8},{8,10},{10,12},{12,14},{14,16},{16,... | collective-permute-start | bytes 1572872 | tf_op jit(solution)/shard_map/ppermute | solution.py:37
  2.3 13.8 %collective-permute-start.1 = (bf16[256,1024]{1,0:T(8,128)(2,1)S(1)}, bf16[256,1024]{1,0:T(8,128)(2,1)S(1)}, u32[]{:S(2)}, u32[]{:S(2)}) collective-permute-start(bf16[256,1024]{1,0:T(8,128)(2,1)S(1)} %constant_dynamic-slice_fusion.own_ref), channel_id=1, source_target_pairs={{2,0},{4,2},{6,4},{8,6},{10,8},{12,10},{14,12},{16,14},{18,16},{20... | collective-permute-start | bytes 1572872 | tf_op jit(solution)/shard_map/ppermute | solution.py:37
  5.9 31.6 %all-to-all-start = ((bf16[16,128,256]{2,1,0:T(8,128)(2,1)}), bf16[16,128,256]{2,1,0:T(8,128)(2,1)S(1)}, u32[]{:S(2)}, u32[]{:S(2)}) async-start(bf16[16,128,256]{2,1,0:T(8,128)(2,1)} %shard_map.130), calls=%async_computation | async-start | bytes 2097152 | tf_op jit(solution)/shard_map/all_to_all | solution.py:318
  13.6 23.9 %copy-start.13 = (f32[1,16,128]{2,1,0:T(8,128)S(1)}, f32[1,16,128]{2,1,0:T(8,128)}, u32[]{:S(2)}) copy-start(f32[1,16,128]{2,1,0:T(8,128)} %param.16) | copy-start | bytes 24580
  13.7 23.8 %copy-start.12 = (s32[1,16,128]{2,1,0:T(8,128)S(1)}, s32[1,16,128]{2,1,0:T(8,128)}, u32[]{:S(2)}) copy-start(s32[1,16,128]{2,1,0:T(8,128)} %param.15) | copy-start | bytes 24580
  14.6 9.8 %collective-permute-start.2 = (bf16[512,256]{1,0:T(8,128)(2,1)S(1)}, bf16[512,256]{1,0:T(8,128)(2,1)S(1)}, u32[]{:S(2)}, u32[]{:S(2)}) collective-permute-start(bf16[512,256]{1,0:T(8,128)(2,1)S(1)} %copy-done.9), channel_id=1, source_target_pairs={{1,0},{0,1},{3,2},{2,3},{5,4},{4,5},{7,6},{6,7},{9,8},{8,9},{11,10... | collective-permute-start | bytes 786440 | tf_op jit(solution)/shard_map/ppermute | solution.py:37
  14.6 9.8 %collective-permute-start.3 = (f32[256]{0:T(256)S(1)}, f32[256]{0:T(256)S(1)}, u32[]{:S(2)}, u32[]{:S(2)}) collective-permute-start(f32[256]{0:T(256)S(1)} %copy-done.15), channel_id=1, source_target_pairs={{1,0},{0,1},{3,2},{2,3},{5,4},{4,5},{7,6},{6,7},{9,8},{8,9},{11,10... | collective-permute-start | bytes 3080 | tf_op jit(solution)/shard_map/ppermute | solution.py:37
  16.1 13.1 %collective-permute-start.4 = (bf16[256,1024]{1,0:T(8,128)(2,1)S(1)}, bf16[256,1024]{1,0:T(8,128)(2,1)S(1)}, u32[]{:S(2)}, u32[]{:S(2)}) collective-permute-start(bf16[256,1024]{1,0:T(8,128)(2,1)S(1)} %copy-done.2), channel_id=1, source_target_pairs={{1,0},{0,1},{3,2},{2,3},{5,4},{4,5},{7,6},{6,7},{9,8},{8,9},{11,10... | collective-permute-start | bytes 1572872 | tf_op jit(solution)/shard_map/ppermute | solution.py:37
  39.6 7.8 %collective-permute-start.5 = (bf16[512,256]{1,0:T(8,128)(2,1)S(1)}, bf16[512,256]{1,0:T(8,128)(2,1)S(1)}, u32[]{:S(2)}, u32[]{:S(2)}) collective-permute-start(bf16[512,256]{1,0:T(8,128)(2,1)S(1)} %get-tuple-element.67), channel_id=1, source_target_pairs={{1,0},{0,1},{3,2},{2,3},{5,4},{4,5},{7,6},{6,7},{9,8},{8,9},{11,10... | collective-permute-start | bytes 786440 | tf_op jit(solution)/shard_map/ppermute | solution.py:37
  39.7 13.3 %collective-permute-start.6 = (bf16[512,256]{1,0:T(8,128)(2,1)S(1)}, bf16[512,256]{1,0:T(8,128)(2,1)S(1)}, u32[]{:S(2)}, u32[]{:S(2)}) collective-permute-start(bf16[512,256]{1,0:T(8,128)(2,1)S(1)} %get-tuple-element.48), channel_id=1, source_target_pairs={{1,0},{0,1},{3,2},{2,3},{5,4},{4,5},{7,6},{6,7},{9,8},{8,9},{11,10... | collective-permute-start | bytes 786440 | tf_op jit(solution)/shard_map/ppermute | solution.py:37
  56.6 2.1 %collective-permute-start.7 = (bf16[288,256]{1,0:T(8,128)(2,1)S(1)}, bf16[288,256]{1,0:T(8,128)(2,1)S(1)}, u32[]{:S(2)}, u32[]{:S(2)}) collective-permute-start(bf16[288,256]{1,0:T(8,128)(2,1)S(1)} %select_convert_fusion), channel_id=1, source_target_pairs={{0,2},{2,0},{4,6},{6,4},{8,10},{10,8},{12,14},{14,12},{16,18},{18,... | collective-permute-start | bytes 442376 | tf_op jit(solution)/shard_map/ppermute | solution.py:42
  58.8 3.3 %collective-permute-start.8 = (bf16[144,256]{1,0:T(8,128)(2,1)S(1)}, bf16[144,256]{1,0:T(8,128)(2,1)S(1)}, u32[]{:S(2)}, u32[]{:S(2)}) collective-permute-start(bf16[144,256]{1,0:T(8,128)(2,1)S(1)} %select_convert_fusion.1), channel_id=1, source_target_pairs={{0,4},{2,6},{4,0},{6,2},{8,12},{10,14},{12,8},{14,10},{16,20},{18,... | collective-permute-start | bytes 221192 | tf_op jit(solution)/shard_map/ppermute | solution.py:42
  62.1 13.6 %collective-permute-start.11 = (bf16[144,256]{1,0:T(8,128)(2,1)S(1)}, bf16[144,256]{1,0:T(8,128)(2,1)S(1)}, u32[]{:S(2)}, u32[]{:S(2)}) collective-permute-start(bf16[144,256]{1,0:T(8,128)(2,1)S(1)} %convert_add_fusion.2), channel_id=1, source_target_pairs={{0,24},{2,26},{4,28},{6,30},{8,16},{10,18},{12,20},{14,22},{16,8},... | collective-permute-start | bytes 221192 | tf_op jit(solution)/shard_map/ppermute | solution.py:42
  62.2 13.5 %collective-permute-start.10 = (bf16[144,256]{1,0:T(8,128)(2,1)S(1)}, bf16[144,256]{1,0:T(8,128)(2,1)S(1)}, u32[]{:S(2)}, u32[]{:S(2)}) collective-permute-start(bf16[144,256]{1,0:T(8,128)(2,1)S(1)} %convert_add_fusion.2), channel_id=1, source_target_pairs={{0,16},{2,18},{4,20},{6,22},{8,24},{10,26},{12,28},{14,30},{16,0},... | collective-permute-start | bytes 221192 | tf_op jit(solution)/shard_map/ppermute | solution.py:42
  63.8 11.9 %collective-permute-start.9 = (bf16[144,256]{1,0:T(8,128)(2,1)S(1)}, bf16[144,256]{1,0:T(8,128)(2,1)S(1)}, u32[]{:S(2)}, u32[]{:S(2)}) collective-permute-start(bf16[144,256]{1,0:T(8,128)(2,1)S(1)} %convert_add_fusion.2), channel_id=1, source_target_pairs={{0,8},{2,10},{4,12},{6,14},{8,0},{10,2},{12,4},{14,6},{16,24},{18,... | collective-permute-start | bytes 221192 | tf_op jit(solution)/shard_map/ppermute | solution.py:42
  65.7 28.3 %collective-permute-start.13 = (bf16[1024,256]{1,0:T(8,128)(2,1)S(1)}, bf16[1024,256]{1,0:T(8,128)(2,1)}, u32[]{:S(2)}, u32[]{:S(2)}) collective-permute-start(bf16[1024,256]{1,0:T(8,128)(2,1)S(1)} %get-tuple-element.53), channel_id=1, source_target_pairs={{30,0},{0,2},{2,4},{4,6},{6,8},{8,10},{10,12},{12,14},{14,16},{16,... | collective-permute-start | bytes 1572872 | tf_op jit(solution)/shard_map/ppermute | solution.py:37
  67.7 26.3 %collective-permute-start.14 = (bf16[1024,256]{1,0:T(8,128)(2,1)S(1)}, bf16[1024,256]{1,0:T(8,128)(2,1)}, u32[]{:S(2)}, u32[]{:S(2)}) collective-permute-start(bf16[1024,256]{1,0:T(8,128)(2,1)S(1)} %get-tuple-element.52), channel_id=1, source_target_pairs={{2,0},{4,2},{6,4},{8,6},{10,8},{12,10},{14,12},{16,14},{18,16},{20... | collective-permute-start | bytes 1572872 | tf_op jit(solution)/shard_map/ppermute | solution.py:37
  68.1 33.5 %all-to-all-start.1 = ((bf16[16,128,256]{2,1,0:T(8,128)(2,1)}), bf16[16,128,256]{2,1,0:T(8,128)(2,1)S(1)}, u32[]{:S(2)}, u32[]{:S(2)}) async-start(bf16[16,128,256]{2,1,0:T(8,128)(2,1)} %get-tuple-element.59), calls=%async_computation.1 | async-start | bytes 2097152 | tf_op jit(solution)/shard_map/all_to_all | solution.py:393
  75.8 18.2 %collective-permute-start.12 = (f32[144,256]{1,0:T(8,128)S(1)}, f32[144,256]{1,0:T(8,128)S(1)}, u32[]{:S(2)}, u32[]{:S(2)}) collective-permute-start(f32[144,256]{1,0:T(8,128)S(1)} %add_add_fusion), channel_id=1, source_target_pairs={{0,4},{2,6},{4,0},{6,2},{8,12},{10,14},{12,8},{14,10},{16,20},{18,... | collective-permute-start | bytes 442376 | tf_op jit(solution)/shard_map/ppermute | solution.py:42
  94.0 2.3 %collective-permute-start.15 = (f32[288,256]{1,0:T(8,128)S(1)}, f32[288,256]{1,0:T(8,128)S(1)}, u32[]{:S(2)}, u32[]{:S(2)}) collective-permute-start(f32[288,256]{1,0:T(8,128)S(1)} %maximum_select_fusion.mine_ref), channel_id=1, source_target_pairs={{0,2},{2,0},{4,6},{6,4},{8,10},{10,8},{12,14},{14,12},{16,18},{18,... | collective-permute-start | bytes 884744 | tf_op jit(solution)/shard_map/ppermute | solution.py:42
  (14 other events, 51.6 us)
